TPU v7x, 32 devices: a whole 2x2x4 slice. The times are simulated.
32 devices in a mesh: seq: 8 (over z, x), dp: 4 (over y, core).
Axes of the slice: x: 2, y: 2, z: 4, core: 2. Of those that a mesh axis runs over, the one named last changes fastest.
Arguments:
- layer_input: bfloat16 [4, 1024, 4096], P('dp', 'seq'), may hold values from -6 to 6
- query_rows: bfloat16 [4, 1024, 4096], P('dp', 'seq')
- key_rows: bfloat16 [4, 1024, 4096], P('dp', 'seq')
- value_rows: bfloat16 [4, 1024, 4096], P('dp', 'seq'), may hold values from -6 to 6
- out_grad: bfloat16 [4, 1024, 4096], P('dp', 'seq'), may hold values from -6 to 6
- neighbours: int32 [4, 8, 8], P('dp'), may hold values from 0 to 7, as said below
- counts: int32 [4, 8], P('dp'), may hold values from 1 to 8, as said below
Outputs:
- query_grad: bfloat16 [4, 1024, 4096], P('dp', 'seq')
- key_grad: bfloat16 [4, 1024, 4096], P('dp', 'seq')
- value_grad: bfloat16 [4, 1024, 4096], P('dp', 'seq')
- weight_grad: float32 [3, 4096, 4096], P(None, 'dp', 'seq')
Inputs may be any that keep to these rules, and one draw needn't show every extreme that they name: `neighbours`: each row lists 8 distinct key blocks of the same snapshot, the query block itself first; entries past counts are not attended. `counts`: every snapshot has a query block with 8.
All inputs are finite; a program needn't handle non-finite values.
Results may differ from a plain program's by a relative error of at most 0.015.
Values may be sent and summed in bfloat16 or wider, within the bound.
No kernel may reach another device: no remote copies, remote signals or barrier semaphores. Data moves between devices by JAX's collectives and lax.ppermute only.
A program may use at most 192 MiB of HBM per device.

v0:
```python
import math

import jax
import jax.numpy as jnp
from jax import lax
from jax.sharding import PartitionSpec as P

HDIM = 128
BLK = 128
MAXNB = 8


def block_backward(query_cols, key_cols, value_cols, grad_cols, links, tallies):
    score_scale = HDIM ** (-0.5)
    rows_total = query_cols.shape[0]
    width_cols = query_cols.shape[1]
    heads_cols = width_cols // HDIM
    block_count = rows_total // BLK
    query_blocks = query_cols.reshape(block_count, BLK, heads_cols, HDIM)
    key_near = key_cols.reshape(block_count, BLK, heads_cols, HDIM)[links].reshape(
        block_count, MAXNB * BLK, heads_cols, HDIM
    )
    value_near = value_cols.reshape(block_count, BLK, heads_cols, HDIM)[links].reshape(
        block_count, MAXNB * BLK, heads_cols, HDIM
    )
    grad_blocks = grad_cols.reshape(block_count, BLK, heads_cols, HDIM)
    live_slot = jnp.arange(MAXNB)[None, :] < tallies[:, None]
    live_keys = jnp.repeat(live_slot, BLK, axis=1)[:, None, None, :]
    scores = (
        jnp.einsum("nthd,nkhd->nhtk", query_blocks, key_near, preferred_element_type=jnp.float32)
        * score_scale
    )
    scores = jnp.where(live_keys, scores, -jnp.inf)
    top_score = jnp.max(scores, axis=-1, keepdims=True)
    weights = jnp.exp(scores - top_score)
    probs = weights / jnp.sum(weights, axis=-1, keepdims=True)
    probs_low = probs.astype(jnp.bfloat16)
    value_part = jnp.einsum(
        "nhtk,nthd->nkhd", probs_low, grad_blocks, preferred_element_type=jnp.float32
    )
    prob_grad = jnp.einsum(
        "nthd,nkhd->nhtk", grad_blocks, value_near, preferred_element_type=jnp.float32
    )
    row_dot = jnp.sum(probs * prob_grad, axis=-1, keepdims=True)
    score_grad = (probs * (prob_grad - row_dot) * score_scale).astype(jnp.bfloat16)
    query_part = jnp.einsum(
        "nhtk,nkhd->nthd", score_grad, key_near, preferred_element_type=jnp.float32
    )
    key_part = jnp.einsum(
        "nhtk,nthd->nkhd", score_grad, query_blocks, preferred_element_type=jnp.float32
    )
    flat_links = links.reshape(-1)
    key_sum = (
        jnp.zeros((block_count, BLK, heads_cols, HDIM), jnp.float32)
        .at[flat_links]
        .add(key_part.reshape(block_count * MAXNB, BLK, heads_cols, HDIM))
    )
    value_sum = (
        jnp.zeros((block_count, BLK, heads_cols, HDIM), jnp.float32)
        .at[flat_links]
        .add(value_part.reshape(block_count * MAXNB, BLK, heads_cols, HDIM))
    )
    return (
        query_part.reshape(rows_total, width_cols).astype(jnp.bfloat16),
        key_sum.reshape(rows_total, width_cols).astype(jnp.bfloat16),
        value_sum.reshape(rows_total, width_cols).astype(jnp.bfloat16),
    )


def local(layer_input, query_rows, key_rows, value_rows, out_grad, neighbours, counts):
    seq_count = lax.axis_size("seq")
    dp_count = lax.axis_size("dp")
    width_here = query_rows.shape[2] // seq_count
    query_here, key_here, value_here, grad_here = (
        lax.all_to_all(query_rows, "seq", split_axis=2, concat_axis=1, tiled=True),
        lax.all_to_all(key_rows, "seq", split_axis=2, concat_axis=1, tiled=True),
        lax.all_to_all(value_rows, "seq", split_axis=2, concat_axis=1, tiled=True),
        lax.all_to_all(out_grad, "seq", split_axis=2, concat_axis=1, tiled=True),
    )
    snap_tokens = query_here.shape[1]
    heads_here = width_here // HDIM
    query_flat = query_here[0]
    key_flat = key_here[0]
    value_flat = value_here[0]
    grad_flat = grad_here[0]
    links = neighbours[0]
    tallies = counts[0]
    empty = jnp.zeros((snap_tokens, width_here), jnp.bfloat16)

    def head_step(head_index, carried):
        first_col = head_index * HDIM
        pieces = [
            lax.dynamic_slice_in_dim(array, first_col, HDIM, 1)
            for array in (query_flat, key_flat, value_flat, grad_flat)
        ]
        outputs = block_backward(pieces[0], pieces[1], pieces[2], pieces[3], links, tallies)
        return tuple(
            (
                lax.dynamic_update_slice_in_dim(carried[i], outputs[i], first_col, 1)
                for i in range(3)
            )
        )

    query_back, key_back, value_back = lax.fori_loop(
        0, heads_here, head_step, (empty, empty, empty)
    )
    query_grad, key_grad, value_grad = (
        lax.all_to_all(query_back[None], "seq", split_axis=1, concat_axis=2, tiled=True),
        lax.all_to_all(key_back[None], "seq", split_axis=1, concat_axis=2, tiled=True),
        lax.all_to_all(value_back[None], "seq", split_axis=1, concat_axis=2, tiled=True),
    )
    norm_factor = 1.0 / math.sqrt(snap_tokens * dp_count)
    shard_piece = lax.all_gather(layer_input, "seq", axis=1, tiled=True)
    terms = [
        jnp.dot(shard_piece[0].T, grad_part, preferred_element_type=jnp.float32)
        for grad_part in (query_back, key_back, value_back)
    ]
    summed = jnp.stack(terms, axis=0)
    owned = lax.psum_scatter(
        summed.astype(jnp.bfloat16), "dp", scatter_dimension=1, tiled=True
    ).astype(jnp.float32)
    return (query_grad, key_grad, value_grad, owned * norm_factor)


def solution(mesh):
    placed = (
        P("dp", "seq", None),
        P("dp", "seq", None),
        P("dp", "seq", None),
        P("dp", "seq", None),
        P("dp", "seq", None),
        P("dp", None, None),
        P("dp", None),
    )
    return jax.shard_map(
        local,
        mesh=mesh,
        in_specs=placed,
        out_specs=(
            P("dp", "seq", None),
            P("dp", "seq", None),
            P("dp", "seq", None),
            P(None, "dp", "seq"),
        ),
        check_vma=False,
    )
```

profile of v0, /device:TPU:0, one launch (start us, length us, event | category | flops | bytes accessed | tf_op | source)
XLA Modules:
  0.0 651.7 jit_solution(11835048650799633075)
XLA Ops:
  7.2 5.0 copy.65
  12.7 22.4 %reduce.12 = bf16[4096,128]{1,0:T(8,128)(2,1)S(1)} reduce(bf16[4096,1,128]{2,1,0:T(2,128)(2,1)S(1)} %bitcast.217, bf16[]{:T(256)} %broadcast.126), dimensions={1}, to_apply=%bitcast.95.reduce_sub_computation | reduce | bytes 2097154
  36.2 7.3 %all-to-all-start = ((bf16[8,2,32768]{2,1,0:T(2,128)(2,1)}), bf16[8,2,32768]{2,1,0:T(2,128)(2,1)S(1)}, u32[]{:S(2)}, u32[]{:S(2)}) async-start(bf16[8,2,32768]{2,1,0:T(2,128)(2,1)} %reshape.260), calls=%async_computation | async-start | bytes 2097152 | tf_op jit(solution)/shard_map/all_to_all | solution.py:76
  43.5 5.0 copy.67
  48.5 23.3 %reduce.13 = bf16[4096,128]{1,0:T(8,128)(2,1)} reduce(bf16[4096,1,128]{2,1,0:T(2,128)(2,1)S(1)} %bitcast.221, bf16[]{:T(256)} %broadcast.126), dimensions={1}, to_apply=%bitcast.97.reduce_sub_computation | reduce | bytes 2097154
  74.0 6.2 all-to-all-start.1
  80.2 5.0 copy.69
  85.2 23.3 %reduce.14 = bf16[4096,128]{1,0:T(8,128)(2,1)} reduce(bf16[4096,1,128]{2,1,0:T(2,128)(2,1)S(1)} %bitcast.222, bf16[]{:T(256)} %broadcast.126), dimensions={1}, to_apply=%bitcast.99.reduce_sub_computation | reduce | bytes 2097154
  110.7 6.0 all-to-all-start.2
  121.8 23.4 %reduce.15 = bf16[4096,128]{1,0:T(8,128)(2,1)} reduce(bf16[4096,1,128]{2,1,0:T(2,128)(2,1)S(1)} %bitcast.223, bf16[]{:T(256)} %broadcast.126), dimensions={1}, to_apply=%bitcast.101.reduce_sub_computation | reduce | bytes 2097154
  147.2 6.0 all-to-all-start.3
  173.2 23.0 %all-to-all-done.3 = bf16[8,2,32768]{2,1,0:T(2,128)(2,1)} async-done(((bf16[8,2,32768]{2,1,0:T(2,128)(2,1)}), bf16[8,2,32768]{2,1,0:T(2,128)(2,1)}, u32[]{:S(2)}, u32[]{:S(2)}) %all-to-all-start.3) | async-done | bytes 1048608 | tf_op jit(solution)/shard_map/all_to_all | solution.py:77
  207.0 299.5 %while.18 = (s32[]{:T(128)}, bf16[1024,512]{1,0:T(8,128)(2,1)}, bf16[1024,512]{1,0:T(8,128)(2,1)}, bf16[1024,512]{1,0:T(8,128)(2,1)}, bf16[1024,512]{1,0:T(8,128...) while((s32[]{:T(128)}, bf16[1024,512]{1,0:T(8,128)(2,1)}, ...), condition=%wide.wide.region_6.7_spmd, body=%wide.wide.region_0.6_spmd.sunk | while | flops 1365645824 | bytes 118791400 | solution.py:104
  216.5 5.3 fusion.112
  221.8 11.7 %fusion.113 = bf16[8,128,128]{1,2,0:T(8,128)(2,1)S(1)} fusion(bf16[8,1024,128]{2,1,0:T(8,128)(2,1)S(1)} %bitcast.205, f32[8,128,1024]{2,1,0:T(8,128)} %fusion.111, f32[8,128,1024]{2,1,0:T(8,128)} %get-tuple-element.364, f32[8,128]{1,0:T(8,128)S(1)} %get-tuple-element.365), kind=kOutput, calls=%fused_computation.23.clone.clone.1 | convolution fusion | flops 275908608 | bytes 10752000 | tf_op jit(solution)/shard_map/while/body/eval_jaxpr/nhtk,nkhd->nthd/dot_general | solution.py:46
  239.2 5.4 copy.102
  244.6 8.8 %scatter_fusion = f32[8,128,128]{2,1,0:T(8,128)S(1)} fusion(f32[8,128,128]{2,1,0:T(8,128)S(1)} %broadcast.162.clone, s32[64]{0:T(128)S(1)} %fusion.114, f32[64,128,128]{2,1,0:T(8,128)} %bitcast.202), kind=kCustom, calls=%fused_computation.3.clone.clone.1 | custom fusion | flops 1048576 | bytes 12583168 | tf_op jit(solution)/shard_map/while/body/eval_jaxpr/scatter-add | solution.py:61
  253.5 13.9 %fusion.115 = f32[8,1024,1,128]{1,3,0,2:T(8,128)} fusion(bf16[8,128,128]{2,1,0:T(8,128)(2,1)S(1)} %bitcast.225, f32[8,128,1024]{2,1,0:T(8,128)} %fusion.111, f32[8,128,1024]{2,1,0:T(8,128)} %get-tuple-element.364, f32[8,128]{1,0:T(8,128)S(1)} %get-tuple-element.365), kind=kOutput, calls=%fused_computation.15.clone.clone.1 | convolution fusion | flops 275777536 | bytes 12849152 | tf_op jit(solution)/shard_map/while/body/eval_jaxpr/nhtk,nthd->nkhd/dot_general | solution.py:49
  267.3 5.3 copy.103
  272.7 8.8 %scatter_fusion.1 = f32[8,128,128]{2,1,0:T(8,128)S(1)} fusion(f32[8,128,128]{2,1,0:T(8,128)S(1)} %broadcast.162.clone.1, s32[64]{0:T(128)S(1)} %fusion.114, f32[64,128,128]{2,1,0:T(8,128)} %bitcast.201), kind=kCustom, calls=%fused_computation.2.clone.clone.1 | custom fusion | flops 1048576 | bytes 12583168 | tf_op jit(solution)/shard_map/while/body/eval_jaxpr/scatter-add | solution.py:56
  296.5 11.7 %fusion.113 = bf16[8,128,128]{1,2,0:T(8,128)(2,1)S(1)} fusion(bf16[8,1024,128]{2,1,0:T(8,128)(2,1)S(1)} %bitcast.205, f32[8,128,1024]{2,1,0:T(8,128)} %fusion.111, f32[8,128,1024]{2,1,0:T(8,128)} %get-tuple-element.364, f32[8,128]{1,0:T(8,128)S(1)} %get-tuple-element.365), kind=kOutput, calls=%fused_computation.23.clone.clone.1 | convolution fusion | flops 275908608 | bytes 10752000 | tf_op jit(solution)/shard_map/while/body/eval_jaxpr/nhtk,nkhd->nthd/dot_general | solution.py:46
  313.9 5.3 copy.102
  319.2 8.8 %scatter_fusion = f32[8,128,128]{2,1,0:T(8,128)S(1)} fusion(f32[8,128,128]{2,1,0:T(8,128)S(1)} %broadcast.162.clone, s32[64]{0:T(128)S(1)} %fusion.114, f32[64,128,128]{2,1,0:T(8,128)} %bitcast.202), kind=kCustom, calls=%fused_computation.3.clone.clone.1 | custom fusion | flops 1048576 | bytes 12583168 | tf_op jit(solution)/shard_map/while/body/eval_jaxpr/scatter-add | solution.py:61
  328.1 13.9 %fusion.115 = f32[8,1024,1,128]{1,3,0,2:T(8,128)} fusion(bf16[8,128,128]{2,1,0:T(8,128)(2,1)S(1)} %bitcast.225, f32[8,128,1024]{2,1,0:T(8,128)} %fusion.111, f32[8,128,1024]{2,1,0:T(8,128)} %get-tuple-element.364, f32[8,128]{1,0:T(8,128)S(1)} %get-tuple-element.365), kind=kOutput, calls=%fused_computation.15.clone.clone.1 | convolution fusion | flops 275777536 | bytes 12849152 | tf_op jit(solution)/shard_map/while/body/eval_jaxpr/nhtk,nthd->nkhd/dot_general | solution.py:49
  341.9 5.3 copy.103
  347.3 8.8 %scatter_fusion.1 = f32[8,128,128]{2,1,0:T(8,128)S(1)} fusion(f32[8,128,128]{2,1,0:T(8,128)S(1)} %broadcast.162.clone.1, s32[64]{0:T(128)S(1)} %fusion.114, f32[64,128,128]{2,1,0:T(8,128)} %bitcast.201), kind=kCustom, calls=%fused_computation.2.clone.clone.1 | custom fusion | flops 1048576 | bytes 12583168 | tf_op jit(solution)/shard_map/while/body/eval_jaxpr/scatter-add | solution.py:56
  371.1 11.7 %fusion.113 = bf16[8,128,128]{1,2,0:T(8,128)(2,1)S(1)} fusion(bf16[8,1024,128]{2,1,0:T(8,128)(2,1)S(1)} %bitcast.205, f32[8,128,1024]{2,1,0:T(8,128)} %fusion.111, f32[8,128,1024]{2,1,0:T(8,128)} %get-tuple-element.364, f32[8,128]{1,0:T(8,128)S(1)} %get-tuple-element.365), kind=kOutput, calls=%fused_computation.23.clone.clone.1 | convolution fusion | flops 275908608 | bytes 10752000 | tf_op jit(solution)/shard_map/while/body/eval_jaxpr/nhtk,nkhd->nthd/dot_general | solution.py:46
  388.5 5.3 copy.102
  393.8 8.8 %scatter_fusion = f32[8,128,128]{2,1,0:T(8,128)S(1)} fusion(f32[8,128,128]{2,1,0:T(8,128)S(1)} %broadcast.162.clone, s32[64]{0:T(128)S(1)} %fusion.114, f32[64,128,128]{2,1,0:T(8,128)} %bitcast.202), kind=kCustom, calls=%fused_computation.3.clone.clone.1 | custom fusion | flops 1048576 | bytes 12583168 | tf_op jit(solution)/shard_map/while/body/eval_jaxpr/scatter-add | solution.py:61
  402.7 13.9 %fusion.115 = f32[8,1024,1,128]{1,3,0,2:T(8,128)} fusion(bf16[8,128,128]{2,1,0:T(8,128)(2,1)S(1)} %bitcast.225, f32[8,128,1024]{2,1,0:T(8,128)} %fusion.111, f32[8,128,1024]{2,1,0:T(8,128)} %get-tuple-element.364, f32[8,128]{1,0:T(8,128)S(1)} %get-tuple-element.365), kind=kOutput, calls=%fused_computation.15.clone.clone.1 | convolution fusion | flops 275777536 | bytes 12849152 | tf_op jit(solution)/shard_map/while/body/eval_jaxpr/nhtk,nthd->nkhd/dot_general | solution.py:49
  416.5 5.3 copy.103
  421.9 8.8 %scatter_fusion.1 = f32[8,128,128]{2,1,0:T(8,128)S(1)} fusion(f32[8,128,128]{2,1,0:T(8,128)S(1)} %broadcast.162.clone.1, s32[64]{0:T(128)S(1)} %fusion.114, f32[64,128,128]{2,1,0:T(8,128)} %bitcast.201), kind=kCustom, calls=%fused_computation.2.clone.clone.1 | custom fusion | flops 1048576 | bytes 12583168 | tf_op jit(solution)/shard_map/while/body/eval_jaxpr/scatter-add | solution.py:56
  445.7 11.7 %fusion.113 = bf16[8,128,128]{1,2,0:T(8,128)(2,1)S(1)} fusion(bf16[8,1024,128]{2,1,0:T(8,128)(2,1)S(1)} %bitcast.205, f32[8,128,1024]{2,1,0:T(8,128)} %fusion.111, f32[8,128,1024]{2,1,0:T(8,128)} %get-tuple-element.364, f32[8,128]{1,0:T(8,128)S(1)} %get-tuple-element.365), kind=kOutput, calls=%fused_computation.23.clone.clone.1 | convolution fusion | flops 275908608 | bytes 10752000 | tf_op jit(solution)/shard_map/while/body/eval_jaxpr/nhtk,nkhd->nthd/dot_general | solution.py:46
  463.0 5.3 copy.102
  468.4 8.8 %scatter_fusion = f32[8,128,128]{2,1,0:T(8,128)S(1)} fusion(f32[8,128,128]{2,1,0:T(8,128)S(1)} %broadcast.162.clone, s32[64]{0:T(128)S(1)} %fusion.114, f32[64,128,128]{2,1,0:T(8,128)} %bitcast.202), kind=kCustom, calls=%fused_computation.3.clone.clone.1 | custom fusion | flops 1048576 | bytes 12583168 | tf_op jit(solution)/shard_map/while/body/eval_jaxpr/scatter-add | solution.py:61
  477.2 13.9 %fusion.115 = f32[8,1024,1,128]{1,3,0,2:T(8,128)} fusion(bf16[8,128,128]{2,1,0:T(8,128)(2,1)S(1)} %bitcast.225, f32[8,128,1024]{2,1,0:T(8,128)} %fusion.111, f32[8,128,1024]{2,1,0:T(8,128)} %get-tuple-element.364, f32[8,128]{1,0:T(8,128)S(1)} %get-tuple-element.365), kind=kOutput, calls=%fused_computation.15.clone.clone.1 | convolution fusion | flops 275777536 | bytes 12849152 | tf_op jit(solution)/shard_map/while/body/eval_jaxpr/nhtk,nthd->nkhd/dot_general | solution.py:49
  491.1 5.3 copy.103
  496.5 8.8 %scatter_fusion.1 = f32[8,128,128]{2,1,0:T(8,128)S(1)} fusion(f32[8,128,128]{2,1,0:T(8,128)S(1)} %broadcast.162.clone.1, s32[64]{0:T(128)S(1)} %fusion.114, f32[64,128,128]{2,1,0:T(8,128)} %bitcast.201), kind=kCustom, calls=%fused_computation.2.clone.clone.1 | custom fusion | flops 1048576 | bytes 12583168 | tf_op jit(solution)/shard_map/while/body/eval_jaxpr/scatter-add | solution.py:56
  506.6 8.4 %fusion.48 = bf16[1,4096,512]{1,2,0:T(8,128)(2,1)S(1)} fusion(bf16[1024,512]{1,0:T(8,128)(2,1)} %get-tuple-element.192, bf16[1,1024,4096]{2,1,0:T(8,128)(2,1)} %all-gather.2.cloned.1.call-done), kind=kOutput, calls=%fused_computation.55 | convolution fusion | flops 4297064448 | bytes 13631488 | tf_op jit(solution)/shard_map/dot_general | solution.py:115
  525.0 5.7 pad_maximum_fusion
  532.4 7.0 %reduce.16 = bf16[1024,512]{1,0:T(8,128)(2,1)S(1)} reduce(bf16[1024,1,512]{2,1,0:T(2,128)(2,1)S(1)} %bitcast.219, bf16[]{:T(256)} %broadcast.126), dimensions={1}, to_apply=%bitcast.126.reduce_sub_computation | reduce | bytes 2097154
  547.9 8.0 %reduce.17 = bf16[1024,512]{1,0:T(8,128)(2,1)} reduce(bf16[1024,1,512]{2,1,0:T(2,128)(2,1)S(1)} %bitcast.220, bf16[]{:T(256)} %broadcast.126), dimensions={1}, to_apply=%bitcast.125.reduce_sub_computation | reduce | bytes 2097154
  558.6 9.2 %all-to-all-done.4 = bf16[8,2,32768]{2,1,0:T(2,128)(2,1)S(1)} async-done(((bf16[8,2,32768]{2,1,0:T(2,128)(2,1)}), bf16[8,2,32768]{2,1,0:T(2,128)(2,1)S(1)}, u32[]{:S(2)}, u32[]{:S(2)}) %all-to-all-start.4) | async-done | bytes 1048608 | tf_op jit(solution)/shard_map/all_to_all | solution.py:108
  575.2 8.0 %reduce.18 = bf16[1024,512]{1,0:T(8,128)(2,1)} reduce(bf16[1024,1,512]{2,1,0:T(2,128)(2,1)S(1)} %bitcast.218, bf16[]{:T(256)} %broadcast.126), dimensions={1}, to_apply=%bitcast.124.reduce_sub_computation | reduce | bytes 2097154
  585.8 10.5 %all-to-all-done.5 = bf16[8,2,32768]{2,1,0:T(2,128)(2,1)} async-done(((bf16[8,2,32768]{2,1,0:T(2,128)(2,1)}), bf16[8,2,32768]{2,1,0:T(2,128)(2,1)}, u32[]{:S(2)}, u32[]{:S(2)}) %all-to-all-start.5) | async-done | bytes 1048608 | tf_op jit(solution)/shard_map/all_to_all | solution.py:109
  610.8 15.0 %all-to-all-done.6 = bf16[8,2,32768]{2,1,0:T(2,128)(2,1)} async-done(((bf16[8,2,32768]{2,1,0:T(2,128)(2,1)}), bf16[8,2,32768]{2,1,0:T(2,128)(2,1)}, u32[]{:S(2)}, u32[]{:S(2)}) %all-to-all-start.6) | async-done | bytes 1048608 | tf_op jit(solution)/shard_map/all_to_all | solution.py:110
  632.4 5.5 convert_multiply_fusion
  637.8 6.6 %copy.82 = f32[3,1024,512]{2,1,0:T(8,128)} copy(f32[3,1024,512]{1,2,0:T(8,128)} %convert_multiply_fusion) | data formatting | bytes 12582912
  (171 shorter events, 175.5 us)
Async XLA Ops:
  36.2 37.8 %all-to-all-start = ((bf16[8,2,32768]{2,1,0:T(2,128)(2,1)}), bf16[8,2,32768]{2,1,0:T(2,128)(2,1)S(1)}, u32[]{:S(2)}, u32[]{:S(2)}) async-start(bf16[8,2,32768]{2,1,0:T(2,128)(2,1)} %reshape.260), calls=%async_computation | async-start | bytes 2097152 | tf_op jit(solution)/shard_map/all_to_all | solution.py:76
  74.0 36.7 %all-to-all-start.1 = ((bf16[8,2,32768]{2,1,0:T(2,128)(2,1)}), bf16[8,2,32768]{2,1,0:T(2,128)(2,1)}, u32[]{:S(2)}, u32[]{:S(2)}) async-start(bf16[8,2,32768]{2,1,0:T(2,128)(2,1)} %reshape.262), calls=%async_computation.1 | async-start | bytes 2097152 | tf_op jit(solution)/shard_map/all_to_all | solution.py:75
  110.7 36.5 %all-to-all-start.2 = ((bf16[8,2,32768]{2,1,0:T(2,128)(2,1)}), bf16[8,2,32768]{2,1,0:T(2,128)(2,1)}, u32[]{:S(2)}, u32[]{:S(2)}) async-start(bf16[8,2,32768]{2,1,0:T(2,128)(2,1)} %reshape.264), calls=%async_computation.2 | async-start | bytes 2097152 | tf_op jit(solution)/shard_map/all_to_all | solution.py:78
  121.8 32.3 %copy-start.5 = (s32[1,8,8]{2,1,0:T(8,128)S(1)}, s32[1,8,8]{2,1,0:T(8,128)}, u32[]{:S(2)}) copy-start(s32[1,8,8]{2,1,0:T(8,128)} %param.14) | copy-start | bytes 772
  147.2 48.9 %all-to-all-start.3 = ((bf16[8,2,32768]{2,1,0:T(2,128)(2,1)}), bf16[8,2,32768]{2,1,0:T(2,128)(2,1)}, u32[]{:S(2)}, u32[]{:S(2)}) async-start(bf16[8,2,32768]{2,1,0:T(2,128)(2,1)} %reshape.266), calls=%async_computation.3 | async-start | bytes 2097152 | tf_op jit(solution)/shard_map/all_to_all | solution.py:77
  153.2 353.3 %all-gather.2.cloned.1.call-start = ((), (), s32[]{:S(2)}) async-start(), calls=%async_computation.8 | async-start | bytes 9437184 | tf_op jit(solution)/shard_map/all_gather | solution.py:113
  154.0 478.4 %reduce-scatter.2.cloned.1.call-start = ((), (), s32[]{:S(2)}) async-start(), calls=%async_computation.9 | async-start | bytes 15728640 | tf_op jit(solution)/shard_map/reduce_scatter | solution.py:119
  200.5 6.5 %copy-start.7 = (s32[1,8]{1,0:T(1,128)S(1)}, s32[1,8]{1,0:T(1,128)}, u32[]{:S(2)}) copy-start(s32[1,8]{1,0:T(1,128)} %param.15) | copy-start | bytes 100
  207.2 2.3 copy-start.1
  215.3 6.5 %copy-start = (bf16[64,128,128]{2,1,0:T(8,128)(2,1)S(1)}, bf16[64,128,128]{2,1,0:T(8,128)(2,1)}, u32[]{:S(2)}) copy-start(bf16[64,128,128]{2,1,0:T(8,128)(2,1)} %gather_fusion) | copy-start | bytes 6291460 | tf_op jit(solution)/shard_map/while
  272.7 9.7 %copy-start.2 = (bf16[1024,512]{1,0:T(8,128)(2,1)S(1)}, bf16[1024,512]{1,0:T(8,128)(2,1)}, u32[]{:S(2)}) copy-start(bf16[1024,512]{1,0:T(8,128)(2,1)} %copy-done.1) | copy-start | bytes 3145732 | tf_op jit(solution)/shard_map/while
  282.4 2.3 copy-start.1
  290.4 6.0 copy-start
  347.3 9.7 %copy-start.2 = (bf16[1024,512]{1,0:T(8,128)(2,1)S(1)}, bf16[1024,512]{1,0:T(8,128)(2,1)}, u32[]{:S(2)}) copy-start(bf16[1024,512]{1,0:T(8,128)(2,1)} %copy-done.1) | copy-start | bytes 3145732 | tf_op jit(solution)/shard_map/while
  357.0 2.3 copy-start.1
  365.0 6.0 copy-start
  421.9 9.7 %copy-start.2 = (bf16[1024,512]{1,0:T(8,128)(2,1)S(1)}, bf16[1024,512]{1,0:T(8,128)(2,1)}, u32[]{:S(2)}) copy-start(bf16[1024,512]{1,0:T(8,128)(2,1)} %copy-done.1) | copy-start | bytes 3145732 | tf_op jit(solution)/shard_map/while
  431.6 2.3 copy-start.1
  439.6 6.0 copy-start
  496.5 9.7 %copy-start.2 = (bf16[1024,512]{1,0:T(8,128)(2,1)S(1)}, bf16[1024,512]{1,0:T(8,128)(2,1)}, u32[]{:S(2)}) copy-start(bf16[1024,512]{1,0:T(8,128)(2,1)} %copy-done.1) | copy-start | bytes 3145732 | tf_op jit(solution)/shard_map/while
  506.6 8.4 %copy-start.4 = (bf16[1024,512]{1,0:T(8,128)(2,1)S(1)}, bf16[1024,512]{1,0:T(8,128)(2,1)}, u32[]{:S(2)}) copy-start(bf16[1024,512]{1,0:T(8,128)(2,1)} %get-tuple-element.191) | copy-start | bytes 3145732
  506.6 8.4 %copy-start.6 = (bf16[1,1024,4096]{2,1,0:T(8,128)(2,1)S(1)}, bf16[1,1024,4096]{2,1,0:T(8,128)(2,1)}, u32[]{:S(2)}) copy-start(bf16[1,1024,4096]{2,1,0:T(8,128)(2,1)} %all-gather.2.cloned.1.call-done) | copy-start | bytes 25165828
  515.0 5.0 copy-start.3
  541.0 26.8 %all-to-all-start.4 = ((bf16[8,2,32768]{2,1,0:T(2,128)(2,1)}), bf16[8,2,32768]{2,1,0:T(2,128)(2,1)S(1)}, u32[]{:S(2)}, u32[]{:S(2)}) async-start(bf16[8,2,32768]{2,1,0:T(2,128)(2,1)} %reshape.268), calls=%async_computation.4 | async-start | bytes 2097152 | tf_op jit(solution)/shard_map/all_to_all | solution.py:108
  567.8 28.5 %all-to-all-start.5 = ((bf16[8,2,32768]{2,1,0:T(2,128)(2,1)}), bf16[8,2,32768]{2,1,0:T(2,128)(2,1)}, u32[]{:S(2)}, u32[]{:S(2)}) async-start(bf16[8,2,32768]{2,1,0:T(2,128)(2,1)} %reshape.270), calls=%async_computation.5 | async-start | bytes 2097152 | tf_op jit(solution)/shard_map/all_to_all | solution.py:109
  596.3 29.5 %all-to-all-start.6 = ((bf16[8,2,32768]{2,1,0:T(2,128)(2,1)}), bf16[8,2,32768]{2,1,0:T(2,128)(2,1)}, u32[]{:S(2)}, u32[]{:S(2)}) async-start(bf16[8,2,32768]{2,1,0:T(2,128)(2,1)} %reshape.272), calls=%async_computation.6 | async-start | bytes 2097152 | tf_op jit(solution)/shard_map/all_to_all | solution.py:110
Sparse Core Ops, SparseCore 0:
  156.2 133.5 all-gather.1
  530.9 96.5 reduce-scatter.1
where the time goes:
time: 663 us; the launch traced here: 652 us
  other arithmetic  197 us (30%)
  matrix products  171 us (26%)
  local copies, waits for them, and re-layouts  170 us (26%)
  waiting for transfers between devices  58.4 us (9%)
  starting transfers between devices  38.4 us (6%)
  between operations  14.9 us (2%)
    unnamed x7, other arithmetic  115 us
    unnamed x40, local copies, waits for them, and re-layouts  74.6 us
    dot_general x4, matrix products, block_backward(): jnp.einsum('nhtk,nthd->nkhd', score_grad, query_blocks, preferred_element...  55.5 us
    dot_general x4, matrix products, block_backward(): jnp.einsum('nhtk,nkhd->nthd', score_grad, key_near, preferred_element_typ...  46.9 us
    scatter-add x4, other arithmetic, block_backward(): key_sum = jnp.zeros((block_count, BLK, heads_cols, HDIM), jnp.float32).at...  35.1 us
    scatter-add x4, other arithmetic, block_backward(): value_sum = jnp.zeros((block_count, BLK, heads_cols, HDIM), jnp.float32)....  35.1 us
    all_to_all x1, waiting for transfers between devices, local(): lax.all_to_all(value_rows, 'seq', split_axis=2, concat_axis=1, tiled=True)  23 us
    transpose x4, local copies, waits for them, and re-layouts, block_backward(): jnp.einsum('nhtk,nthd->nkhd', probs_low, grad_blocks, preferred_element_t...  21.3 us
  transfers between devices with their start and end apart: 9, of which 4 were waited for; matrix products, arithmetic and copies ran while one was open for 73% of the time, Pallas kernels for 0%

commit v1 on v0

v1 whole, which is shorter than its diff:
```python
import math

import jax
import jax.numpy as jnp
from jax import lax
from jax.experimental import pallas as pl
from jax.experimental.pallas import tpu as pltpu
from jax.sharding import PartitionSpec as P

HDIM = 128
BLK = 128
MIB = 1 << 20
BF = jnp.bfloat16
F32 = jnp.float32


def pack_rows(arrays, parts, chunks):
    tokens, width = arrays[0].shape
    each = width // parts
    cut = each // chunks

    def kernel(*refs):
        ins, outs = refs[: len(arrays)], refs[len(arrays) :]
        for i, ref in enumerate(ins):
            for c, out in enumerate(outs):
                out[0, i] = ref[:, c * cut : (c + 1) * cut]

    return pl.pallas_call(
        kernel,
        grid=(parts,),
        in_specs=[pl.BlockSpec((tokens, each), lambda s: (0, s))] * len(arrays),
        out_specs=[pl.BlockSpec((1, len(arrays), tokens, cut), lambda s: (s, 0, 0, 0))] * chunks,
        out_shape=[jax.ShapeDtypeStruct((parts, len(arrays), tokens, cut), BF)] * chunks,
        name="pack_rows",
    )(*arrays)


def unpack_rows(chunked):
    parts, kinds, tokens, cut = chunked[0].shape
    chunks = len(chunked)

    def kernel(*refs):
        ins, outs = refs[:chunks], refs[chunks:]
        for i, out in enumerate(outs):
            for c, ref in enumerate(ins):
                out[:, c * cut : (c + 1) * cut] = ref[0, i]

    return pl.pallas_call(
        kernel,
        grid=(parts,),
        in_specs=[pl.BlockSpec((1, kinds, tokens, cut), lambda s: (s, 0, 0, 0))] * chunks,
        out_specs=[pl.BlockSpec((tokens, chunks * cut), lambda s: (0, s))] * kinds,
        out_shape=[jax.ShapeDtypeStruct((tokens, parts * chunks * cut), BF)] * kinds,
        name="unpack_rows",
    )(*chunked)


def turn(array):
    tokens, width = array.shape
    step = 512

    def kernel(ref, out):
        out[...] = ref[...].T

    return pl.pallas_call(
        kernel,
        grid=(width // step,),
        in_specs=[pl.BlockSpec((tokens, step), lambda i: (0, i))],
        out_specs=pl.BlockSpec((step, tokens), lambda i: (i, 0)),
        out_shape=jax.ShapeDtypeStruct((width, tokens), BF),
        name="turn_layer_input",
    )(array)


def attention(items, bias):
    blocks, _, _, width = items.shape
    heads = width // HDIM
    tokens = blocks * BLK
    pair = 2 * BLK
    factor = HDIM ** (-0.5)
    nt = (((1,), (1,)), ((), ()))

    def kernel(items_ref, bias_ref, out_ref, key_sum, value_sum):
        for h in range(heads):
            cols = slice(h * HDIM, (h + 1) * HDIM)
            keys = items_ref[:, 1, :, cols].reshape(tokens, HDIM)
            values = items_ref[:, 2, :, cols].reshape(tokens, HDIM)
            keys_t = keys.T
            key_sum[...] = jnp.zeros_like(key_sum)
            value_sum[...] = jnp.zeros_like(value_sum)

            def step(n, _):
                query = items_ref[pl.ds(2 * n, 2), 0, :, cols].reshape(pair, HDIM)
                grad = items_ref[pl.ds(2 * n, 2), 3, :, cols].reshape(pair, HDIM)
                scores = lax.dot_general(keys, query, nt, preferred_element_type=F32)
                near = bias_ref[n]
                scores = (
                    scores.reshape(blocks, BLK, pair) * (factor * math.log2(math.e)) + near[:, None, :]
                ).reshape(tokens, pair)
                top = jnp.max(scores, axis=0, keepdims=True)
                weights = jnp.exp2(scores - top)
                prob_grad = lax.dot_general(values, grad, nt, preferred_element_type=F32)
                inverse = 1.0 / jnp.sum(weights, axis=0, keepdims=True)
                row_dot = jnp.sum(weights * prob_grad, axis=0, keepdims=True) * inverse
                probs = weights * inverse
                probs_low = probs.astype(BF)
                score_grad = (probs * (prob_grad - row_dot)).astype(BF)
                value_sum[...] += jnp.dot(probs_low, grad, preferred_element_type=F32)
                key_sum[...] += jnp.dot(score_grad, query, preferred_element_type=F32)
                query_grad_t = jnp.dot(keys_t, score_grad, preferred_element_type=F32) * factor
                out_ref[pl.ds(2 * n, 2), 0, :, cols] = query_grad_t.T.astype(BF).reshape(2, BLK, HDIM)
                return 0

            lax.fori_loop(0, blocks // 2, step, 0)
            out_ref[:, 1, :, cols] = (key_sum[...] * factor).astype(BF).reshape(blocks, BLK, HDIM)
            out_ref[:, 2, :, cols] = value_sum[...].astype(BF).reshape(blocks, BLK, HDIM)

    return pl.pallas_call(
        kernel,
        in_specs=[pl.BlockSpec(memory_space=pltpu.VMEM)] * 2,
        out_specs=pl.BlockSpec(memory_space=pltpu.VMEM),
        out_shape=jax.ShapeDtypeStruct((blocks, 3, BLK, width), BF),
        scratch_shapes=[pltpu.VMEM((tokens, HDIM), F32), pltpu.VMEM((tokens, HDIM), F32)],
        compiler_params=pltpu.CompilerParams(vmem_limit_bytes=40 * MIB),
        cost_estimate=pl.CostEstimate(
            flops=20 * heads * tokens * tokens * HDIM,
            bytes_accessed=14 * tokens * width,
            transcendentals=heads * tokens * tokens,
        ),
        name="attention_backward",
    )(items, bias)


def weight_products(turned, grads, norm):
    blocks, snaps, rows, _ = turned.shape
    chunks = len(grads[0])
    cut = grads[0][0].shape[-1]
    flat = [grads[k][c] for k in range(snaps) for c in range(chunks)]
    group = 4
    row_step = rows // 2

    def kernel(*refs):
        turned_ref, grad_refs, out_ref = refs[0], refs[1:-1], refs[-1]
        at = pl.program_id(1)

        @pl.when(at == 0)
        def _():
            out_ref[...] = jnp.zeros_like(out_ref)

        for k in range(snaps):
            left = jnp.concatenate([turned_ref[b, k] for b in range(group)], axis=1)
            for c in range(chunks):
                ref = grad_refs[k * chunks + c]
                for kind in range(3):
                    right = ref[:, kind].reshape(group * BLK, cut)
                    out_ref[kind, :, c * cut : (c + 1) * cut] += jnp.dot(
                        left, right, preferred_element_type=F32
                    )

        @pl.when(at == pl.num_programs(1) - 1)
        def _():
            out_ref[...] = out_ref[...] * norm

    return pl.pallas_call(
        kernel,
        grid=(2, blocks // group),
        in_specs=[pl.BlockSpec((group, snaps, row_step, BLK), lambda r, b: (b, 0, r, 0))]
        + [pl.BlockSpec((group, 3, BLK, cut), lambda r, b: (b, 0, 0, 0))] * len(flat),
        out_specs=pl.BlockSpec((3, row_step, chunks * cut), lambda r, b: (0, r, 0)),
        out_shape=jax.ShapeDtypeStruct((3, rows, chunks * cut), F32),
        compiler_params=pltpu.CompilerParams(vmem_limit_bytes=56 * MIB),
        cost_estimate=pl.CostEstimate(
            flops=6 * blocks * BLK * snaps * rows * chunks * cut,
            bytes_accessed=2 * blocks * snaps * BLK * (rows + 3 * chunks * cut) + 12 * rows * chunks * cut,
            transcendentals=0,
        ),
        name="weight_products",
    )(turned, *flat)


def local(layer_input, query_rows, key_rows, value_rows, out_grad, neighbours, counts):
    seq_count = lax.axis_size("seq")
    dp_count = lax.axis_size("dp")
    here = lax.axis_index("dp")
    width = query_rows.shape[2]
    heads_here = width // seq_count // HDIM
    blocks = neighbours.shape[1]
    chunks = 2 if heads_here % 2 == 0 else 1
    rows_here = layer_input.shape[2] // dp_count
    y_count = dp_count // 2

    def peer(p, j, e):
        return ((p // 2 + j) % y_count) * 2 + ((p % 2) ^ e)

    peers = [(j, e) for j in range(y_count) for e in range(2)]

    def dp_move(array, j, e):
        return lax.ppermute(array, "dp", [(peer(p, j, e), p) for p in range(dp_count)])

    packed = pack_rows([query_rows[0], key_rows[0], value_rows[0], out_grad[0]], seq_count, chunks)

    turned = turn(layer_input[0])
    slabs = []
    for j, e in peers:
        to = peer(here, (y_count - j) % y_count, e)
        slab = lax.dynamic_slice_in_dim(turned, to * rows_here, rows_here, 0)
        slabs.append(slab if (j, e) == (0, 0) else dp_move(slab, j, e))
    turned_all = lax.all_gather(jnp.stack(slabs), "seq", axis=0, tiled=False)

    live = jnp.arange(neighbours.shape[2])[None, :] < counts[0][:, None]
    hit = (neighbours[0][:, :, None] == jnp.arange(blocks)[None, None, :]) & live[:, :, None]
    near = jnp.where(jnp.any(hit, axis=1), 0.0, -jnp.inf).astype(F32)
    bias = jnp.repeat(near.reshape(blocks // 2, 2, blocks).transpose(0, 2, 1), BLK, axis=2)

    grads = [[None] * chunks for _ in peers]
    back = []
    for c in range(chunks):
        items = lax.all_to_all(packed[c], "seq", 0, 0, tiled=True)
        out = attention(items, bias)
        back.append(lax.all_to_all(out, "seq", 0, 0, tiled=True))
        for n, (j, e) in enumerate(peers):
            if e == 0:
                grads[n][c] = out if j == 0 else dp_move(out, j, 0)
        for n, (j, e) in enumerate(peers):
            if e == 1:
                grads[n][c] = dp_move(grads[n - 1][c], 0, 1)
    norm = 1.0 / math.sqrt(neighbours.shape[1] * BLK * dp_count)
    weight_grad = weight_products(turned_all, grads, norm)
    query_grad, key_grad, value_grad = unpack_rows(back)
    return query_grad[None], key_grad[None], value_grad[None], weight_grad


def solution(mesh):
    placed = (P("dp", "seq", None),) * 5 + (P("dp", None, None), P("dp", None))
    return jax.shard_map(
        local,
        mesh=mesh,
        in_specs=placed,
        out_specs=(P("dp", "seq", None),) * 3 + (P(None, "dp", "seq"),),
        check_vma=False,
    )
```

time: 663 us -> 347 us (0.52); the launches traced: 652 us -> 347 us
  other arithmetic: 197 us -> 1.36 us
  matrix products: 171 us -> 0 us
  local copies, waits for them, and re-layouts: 170 us -> 5.24 us
  waiting for transfers between devices: 58.4 us -> 160 us
  blocking collectives: 0 us -> 86.4 us
  Pallas kernels: 0 us -> 61.7 us
  starting transfers between devices: 38.4 us -> 17.6 us
    dot_general x19 -> x0, matrix products: 151 us -> none  [the longest x4 55.5 us: block_backward(): jnp.einsum('nhtk,nthd->nkhd', score_grad, query_blocks, preferred_element...]
    unnamed x7 -> x0, other arithmetic: 115 us -> none
    all_to_all x0 -> x1, blocking collectives: none -> 86.4 us  [local(): items = lax.all_to_all(packed[c], 'seq', 0, 0, tiled=True)]
    unnamed x40 -> x12, local copies, waits for them, and re-layouts: 74.6 us -> 3.91 us
    scatter-add x8 -> x0, other arithmetic: 70.3 us -> none  [the longest x4 35.1 us: block_backward(): key_sum = jnp.zeros((block_count, BLK, heads_cols, HDIM), jnp.float32).at...]
    pallas_call x0 -> x6, Pallas kernels: none -> 61.7 us  [the longest x2 22.8 us: attention(): pl.pallas_call(kernel, in_specs=[pl.BlockSpec(memory_space=pltpu.VMEM)] *...]
    all_to_all x7 -> x3, waiting for transfers between devices: 57.7 us -> 119 us  [the longest x1 88 us: local(): items = lax.all_to_all(packed[c], 'seq', 0, 0, tiled=True)]
    transpose x8 -> x0, local copies, waits for them, and re-layouts: 42.6 us -> none  [the longest x4 21.3 us: block_backward(): jnp.einsum('nhtk,nthd->nkhd', probs_low, grad_blocks, preferred_element_t...]
  transfers between devices with their start and end apart: 9 -> 13, of which waited for: 4 -> 6; matrix products, arithmetic and copies ran while one was open for 73% -> 0% of each run, Pallas kernels for 0% -> 10%
where the time goes in v1:
time: 347 us
  waiting for transfers between devices  160 us (46%)
  blocking collectives  86.4 us (25%)
  Pallas kernels  61.7 us (18%)
  starting transfers between devices  17.6 us (5%)
  between operations  14.2 us (4%)
  local copies, waits for them, and re-layouts  5.24 us (2%)
    all_to_all x1, waiting for transfers between devices, local(): items = lax.all_to_all(packed[c], 'seq', 0, 0, tiled=True)  88 us
    all_to_all x1, blocking collectives, local(): items = lax.all_to_all(packed[c], 'seq', 0, 0, tiled=True)  86.4 us
    ppermute x9, waiting for transfers between devices, dp_move(): lax.ppermute(array, 'dp', [(peer(p, j, e), p) for p in range(dp_count)])  40.9 us
    all_to_all x2, waiting for transfers between devices, local(): back.append(lax.all_to_all(out, 'seq', 0, 0, tiled=True))  31.2 us
    pallas_call x2, Pallas kernels, attention(): pl.pallas_call(kernel, in_specs=[pl.BlockSpec(memory_space=pltpu.VMEM)] *...  22.8 us
    pallas_call x1, Pallas kernels, weight_products(): pl.pallas_call(kernel, grid=(2, blocks // group), in_specs=[pl.BlockSpec(...  20.6 us
    all_to_all x2, starting transfers between devices, local(): back.append(lax.all_to_all(out, 'seq', 0, 0, tiled=True))  7.92 us
  transfers between devices with their start and end apart: 13, of which 6 were waited for; matrix products, arithmetic and copies ran while one was open for 0% of the time, Pallas kernels for 10%

profile of v1, /device:TPU:0, one launch (start us, length us, event | category | flops | bytes accessed | tf_op | source)
XLA Modules:
  0.0 346.6 jit_solution(13025292620668732770)
XLA Ops:
  7.2 0.0 all-gather.3.cloned.1.call-start
  7.3 5.5 %turn_layer_input.1 = bf16[4096,128]{1,0:T(8,128)(2,1)} custom-call(bf16[128,4096]{1,0:T(8,128)(2,1)} %bitcast.21), custom_call_target="tpu_custom_call" | custom-call | tf_op jit(solution)/shard_map/turn_layer_input/pallas_call | solution.py:65
  12.7 1.3 dynamic-slice_bitcast_fusion
  14.0 0.5 collective-permute-start
  14.5 2.6 collective-permute-start.1
  17.1 0.1 collective-permute-start.2
  17.2 0.0 collective-permute-done
  17.2 7.1 %collective-permute-done.1 = bf16[1024,128]{1,0:T(8,128)(2,1)S(1)} collective-permute-done((bf16[1024,128]{1,0:T(8,128)(2,1)S(1)}, bf16[1024,128]{1,0:T(8,128)(2,1)S(1)}, u32[]{:S(2)}, u32[]{:S(2)}) %collective-permute-start.1) | collective-permute-done | bytes 262176 | tf_op jit(solution)/shard_map/ppermute | solution.py:198
  24.3 5.1 %collective-permute-done.2 = bf16[1024,128]{1,0:T(8,128)(2,1)S(1)} collective-permute-done((bf16[1024,128]{1,0:T(8,128)(2,1)S(1)}, bf16[1024,128]{1,0:T(8,128)(2,1)S(1)}, u32[]{:S(2)}, u32[]{:S(2)}) %collective-permute-start.2) | collective-permute-done | bytes 262176 | tf_op jit(solution)/shard_map/ppermute | solution.py:198
  29.4 1.2 pad_maximum_fusion
  30.6 0.0 all-gather.3.cloned.1.call-update
  30.6 6.6 %pack_rows.1 = (bf16[8,4,128,256]{3,2,1,0:T(8,128)(2,1)}, bf16[8,4,128,256]{3,2,1,0:T(8,128)(2,1)}) custom-call(bf16[128,4096]{1,0:T(8,128)(2,1)} %bitcast.22, bf16[128,4096]{1,0:T(8,128)(2,1)} %bitcast.23, bf16[128,4096]{1,0:T(8,128)(2,1)} %bitcast.24, bf16[128,4096]{1,0:T(8,128)(2,1)} %bitcast.25), custom_call_target="tpu_custom_call" | custom-call | tf_op jit(solution)/shard_map/pack_rows/pallas_call | solution.py:28
  37.2 86.4 %all_to_all.20.items_ref = bf16[8,4,128,256]{3,2,1,0:T(8,128)(2,1)} all-to-all(bf16[8,4,128,256]{3,2,1,0:T(8,128)(2,1)} %get-tuple-element.9), channel_id=1, replica_groups=mesh['seq'=8,'dp'=4] {'seq'}, dimensions={0} | all-to-all | bytes 4194304 | tf_op jit(solution)/shard_map/all_to_all | solution.py:218
  123.6 0.0 copy-start.5
  123.6 0.0 copy-start.4
  123.6 3.7 %all-to-all-start.2 = ((bf16[8,4,128,256]{3,2,1,0:T(8,128)(2,1)}), bf16[8,4,128,256]{3,2,1,0:T(8,128)(2,1)S(1)}, u32[]{:S(2)}, u32[]{:S(2)}) async-start(bf16[8,4,128,256]{3,2,1,0:T(8,128)(2,1)} %get-tuple-element.10), calls=%async_computation.2 | async-start | bytes 4194304 | tf_op jit(solution)/shard_map/all_to_all | solution.py:218
  127.4 0.0 copy-done.5
  127.4 0.1 iota_compare_fusion.1
  127.5 0.0 copy-done.4
  127.5 0.1 fusion.1
  127.6 0.1 broadcast_bitcast_fusion.bias_ref
  127.7 1.6 copy-done
  129.3 10.8 %attention_backward.2.refs_1_ = bf16[8,3,128,256]{3,2,1,0:T(8,128)(2,1)S(1)} custom-call(bf16[8,4,128,256]{3,2,1,0:T(8,128)(2,1)S(1)} %copy-done, f32[4,8,256]{2,1,0:T(8,128)S(1)} %broadcast_bitcast_fusion.bias_ref), custom_call_target="tpu_custom_call" | custom-call | flops 5368709120 | bytes 3670016 | tf_op jit(solution)/shard_map/attention_backward/pallas_call | solution.py:118
  140.1 0.0 copy-start.1
  140.1 1.1 copy-done.1
  141.2 88.0 %all-to-all-done.2.items_ref = bf16[8,4,128,256]{3,2,1,0:T(8,128)(2,1)S(1)} async-done(((bf16[8,4,128,256]{3,2,1,0:T(8,128)(2,1)}), bf16[8,4,128,256]{3,2,1,0:T(8,128)(2,1)S(1)}, u32[]{:S(2)}, u32[]{:S(2)}) %all-to-all-start.2) | async-done | bytes 2097184 | tf_op jit(solution)/shard_map/all_to_all | solution.py:218
  229.2 4.3 %all-to-all-start.1 = ((bf16[8,3,128,256]{3,2,1,0:T(8,128)(2,1)}), bf16[8,3,128,256]{3,2,1,0:T(8,128)(2,1)}, u32[]{:S(2)}, u32[]{:S(2)}) async-start(bf16[8,3,128,256]{3,2,1,0:T(8,128)(2,1)} %copy-done.1), calls=%async_computation.1 | async-start | bytes 3145728 | tf_op jit(solution)/shard_map/all_to_all | solution.py:220
  233.5 1.5 collective-permute-start.5
  235.1 12.0 %attention_backward.3.refs_2_ = bf16[8,3,128,256]{3,2,1,0:T(8,128)(2,1)} custom-call(bf16[8,4,128,256]{3,2,1,0:T(8,128)(2,1)S(1)} %all-to-all-done.2.items_ref, f32[4,8,256]{2,1,0:T(8,128)S(1)} %broadcast_bitcast_fusion.bias_ref), custom_call_target="tpu_custom_call" | custom-call | flops 5368709120 | bytes 3670016 | tf_op jit(solution)/shard_map/attention_backward/pallas_call | solution.py:118
  247.1 0.6 collective-permute-start.6
  247.7 23.3 %all-to-all-done.1.refs_0_ = bf16[8,3,128,256]{3,2,1,0:T(8,128)(2,1)} async-done(((bf16[8,3,128,256]{3,2,1,0:T(8,128)(2,1)}), bf16[8,3,128,256]{3,2,1,0:T(8,128)(2,1)}, u32[]{:S(2)}, u32[]{:S(2)}) %all-to-all-start.1) | async-done | bytes 1572896 | tf_op jit(solution)/shard_map/all_to_all | solution.py:220
  271.0 3.6 %all-to-all-start.3 = ((bf16[8,3,128,256]{3,2,1,0:T(8,128)(2,1)}), bf16[8,3,128,256]{3,2,1,0:T(8,128)(2,1)S(1)}, u32[]{:S(2)}, u32[]{:S(2)}) async-start(bf16[8,3,128,256]{3,2,1,0:T(8,128)(2,1)} %attention_backward.3.refs_2_), calls=%async_computation.3 | async-start | bytes 3145728 | tf_op jit(solution)/shard_map/all_to_all | solution.py:220
  274.6 0.0 copy-done.2
  274.6 0.1 collective-permute-start.3
  274.7 0.5 collective-permute-start.4
  275.2 0.0 collective-permute-done.5.refs_5_
  275.2 0.1 collective-permute-start.7
  275.2 28.7 %collective-permute-done.6.refs_6_ = bf16[8,3,128,256]{3,2,1,0:T(8,128)(2,1)} collective-permute-done((bf16[8,3,128,256]{3,2,1,0:T(8,128)(2,1)}, bf16[8,3,128,256]{3,2,1,0:T(8,128)(2,1)}, u32[]{:S(2)}, u32[]{:S(2)}) %collective-permute-start.6) | collective-permute-done | bytes 1572896 | tf_op jit(solution)/shard_map/ppermute | solution.py:198
  303.9 0.0 collective-permute-start.8
  303.9 7.9 %all-to-all-done.3.refs_1_ = bf16[8,3,128,256]{3,2,1,0:T(8,128)(2,1)S(1)} async-done(((bf16[8,3,128,256]{3,2,1,0:T(8,128)(2,1)}), bf16[8,3,128,256]{3,2,1,0:T(8,128)(2,1)S(1)}, u32[]{:S(2)}, u32[]{:S(2)}) %all-to-all-start.3) | async-done | bytes 1572896 | tf_op jit(solution)/shard_map/all_to_all | solution.py:220
  311.8 1.1 copy-done.3
  312.9 6.2 %unpack_rows.1 = (bf16[128,4096]{1,0:T(8,128)(2,1)}, bf16[128,4096]{1,0:T(8,128)(2,1)}, bf16[128,4096]{1,0:T(8,128)(2,1)}) custom-call(bf16[8,3,128,256]{3,2,1,0:T(8,128)(2,1)} %all-to-all-done.1.refs_0_, bf16[8,3,128,256]{3,2,1,0:T(8,128)(2,1)} %copy-done.3), custom_call_target="tpu_custom_call" | custom-call | tf_op jit(solution)/shard_map/unpack_rows/pallas_call | solution.py:48
  319.1 0.0 collective-permute-done.3.refs_3_
  319.1 0.0 collective-permute-done.4.refs_4_
  319.1 0.0 collective-permute-done.7.refs_7_
  319.1 0.0 collective-permute-done.8.refs_8_
  319.1 0.0 all-gather.3.cloned.1.call-done
  319.2 20.6 %weight_products.1 = f32[3,1024,512]{2,1,0:T(8,128)} custom-call(bf16[8,4,1024,128]{3,2,1,0:T(8,128)(2,1)} %bitcast.31, bf16[8,3,128,256]{3,2,1,0:T(8,128)(2,1)} %copy-done.1, bf16[8,3,128,256]{3,2,1,0:T(8,128)(2,1)} %attention_backward.3.refs_2_, bf16[8,3,128,256]{3,2,1,0:T(8,128)(2,1)} %collective-permute-done.3.refs_3_, ...), custom_call_target="tpu_custom_call" | custom-call | flops 12884901888 | bytes 27262976 | tf_op jit(solution)/shard_map/weight_products/pallas_call | solution.py:164
  (4 shorter events, 0.0 us)
Async XLA Ops:
  7.2 312.0 %all-gather.3.cloned.1.call-start = ((), (), s32[]{:S(2)}) async-start(), calls=%async_computation.4 | async-start | bytes 9437184 | tf_op jit(solution)/shard_map/all_gather | solution.py:208
  14.0 3.2 collective-permute-start
  14.5 9.8 %collective-permute-start.1 = (bf16[1024,128]{1,0:T(8,128)(2,1)S(1)}, bf16[1024,128]{1,0:T(8,128)(2,1)S(1)}, u32[]{:S(2)}, u32[]{:S(2)}) collective-permute-start(bf16[1024,128]{1,0:T(8,128)(2,1)S(1)} %get-tuple-element.16), channel_id=1, source_target_pairs={{2,0},{3,1},{0,2},{1,3},{6,4},{7,5},{4,6},{5,7},{10,8},{11,9},{8,1... | collective-permute-start | bytes 786440 | tf_op jit(solution)/shard_map/ppermute | solution.py:198
  17.1 12.3 %collective-permute-start.2 = (bf16[1024,128]{1,0:T(8,128)(2,1)S(1)}, bf16[1024,128]{1,0:T(8,128)(2,1)S(1)}, u32[]{:S(2)}, u32[]{:S(2)}) collective-permute-start(bf16[1024,128]{1,0:T(8,128)(2,1)S(1)} %get-tuple-element.15), channel_id=1, source_target_pairs={{3,0},{2,1},{1,2},{0,3},{7,4},{6,5},{5,6},{4,7},{11,8},{10,9},{9,1... | collective-permute-start | bytes 786440 | tf_op jit(solution)/shard_map/ppermute | solution.py:198
  123.6 3.7 %copy-start.5 = (s32[1,8]{1,0:T(1,128)S(1)}, s32[1,8]{1,0:T(1,128)}, u32[]{:S(2)}) copy-start(s32[1,8]{1,0:T(1,128)} %param.13) | copy-start | bytes 100
  123.6 3.8 %copy-start.4 = (s32[1,8,8]{2,1,0:T(8,128)S(1)}, s32[1,8,8]{2,1,0:T(8,128)}, u32[]{:S(2)}) copy-start(s32[1,8,8]{2,1,0:T(8,128)} %param.12) | copy-start | bytes 772
  123.6 105.6 %all-to-all-start.2 = ((bf16[8,4,128,256]{3,2,1,0:T(8,128)(2,1)}), bf16[8,4,128,256]{3,2,1,0:T(8,128)(2,1)S(1)}, u32[]{:S(2)}, u32[]{:S(2)}) async-start(bf16[8,4,128,256]{3,2,1,0:T(8,128)(2,1)} %get-tuple-element.10), calls=%async_computation.2 | async-start | bytes 4194304 | tf_op jit(solution)/shard_map/all_to_all | solution.py:218
  127.7 1.6 copy-start
  140.1 1.1 copy-start.1
  229.2 41.7 %all-to-all-start.1 = ((bf16[8,3,128,256]{3,2,1,0:T(8,128)(2,1)}), bf16[8,3,128,256]{3,2,1,0:T(8,128)(2,1)}, u32[]{:S(2)}, u32[]{:S(2)}) async-start(bf16[8,3,128,256]{3,2,1,0:T(8,128)(2,1)} %copy-done.1), calls=%async_computation.1 | async-start | bytes 3145728 | tf_op jit(solution)/shard_map/all_to_all | solution.py:220
  233.5 41.6 %collective-permute-start.5 = (bf16[8,3,128,256]{3,2,1,0:T(8,128)(2,1)}, bf16[8,3,128,256]{3,2,1,0:T(8,128)(2,1)}, u32[]{:S(2)}, u32[]{:S(2)}) collective-permute-start(bf16[8,3,128,256]{3,2,1,0:T(8,128)(2,1)} %copy-done.1), channel_id=1, source_target_pairs={{2,0},{3,1},{0,2},{1,3},{6,4},{7,5},{4,6},{5,7},{10,8},{11,9},{8,1... | collective-permute-start | bytes 4718600 | tf_op jit(solution)/shard_map/ppermute | solution.py:198
  247.1 27.5 %copy-start.2 = (bf16[8,3,128,256]{3,2,1,0:T(8,128)(2,1)S(1)}, bf16[8,3,128,256]{3,2,1,0:T(8,128)(2,1)}, u32[]{:S(2)}) copy-start(bf16[8,3,128,256]{3,2,1,0:T(8,128)(2,1)} %copy-done.1) | copy-start | bytes 4718596
  247.1 56.8 %collective-permute-start.6 = (bf16[8,3,128,256]{3,2,1,0:T(8,128)(2,1)}, bf16[8,3,128,256]{3,2,1,0:T(8,128)(2,1)}, u32[]{:S(2)}, u32[]{:S(2)}) collective-permute-start(bf16[8,3,128,256]{3,2,1,0:T(8,128)(2,1)} %attention_backward.3.refs_2_), channel_id=1, source_target_pairs={{2,0},{3,1},{0,2},{1,3},{6,4},{7,5},{4,6},{5,7},{10,8},{11,9},{8,1... | collective-permute-start | bytes 4718600 | tf_op jit(solution)/shard_map/ppermute | solution.py:198
  271.0 40.8 %all-to-all-start.3 = ((bf16[8,3,128,256]{3,2,1,0:T(8,128)(2,1)}), bf16[8,3,128,256]{3,2,1,0:T(8,128)(2,1)S(1)}, u32[]{:S(2)}, u32[]{:S(2)}) async-start(bf16[8,3,128,256]{3,2,1,0:T(8,128)(2,1)} %attention_backward.3.refs_2_), calls=%async_computation.3 | async-start | bytes 3145728 | tf_op jit(solution)/shard_map/all_to_all | solution.py:220
  274.6 44.5 %collective-permute-start.3 = (bf16[8,3,128,256]{3,2,1,0:T(8,128)(2,1)S(1)}, bf16[8,3,128,256]{3,2,1,0:T(8,128)(2,1)}, u32[]{:S(2)}, u32[]{:S(2)}) collective-permute-start(bf16[8,3,128,256]{3,2,1,0:T(8,128)(2,1)S(1)} %copy-done.2), channel_id=1, source_target_pairs={{1,0},{0,1},{3,2},{2,3},{5,4},{4,5},{7,6},{6,7},{9,8},{8,9},{11,10... | collective-permute-start | bytes 4718600 | tf_op jit(solution)/shard_map/ppermute | solution.py:198
  274.7 44.5 %collective-permute-start.4 = (bf16[8,3,128,256]{3,2,1,0:T(8,128)(2,1)}, bf16[8,3,128,256]{3,2,1,0:T(8,128)(2,1)}, u32[]{:S(2)}, u32[]{:S(2)}) collective-permute-start(bf16[8,3,128,256]{3,2,1,0:T(8,128)(2,1)} %attention_backward.3.refs_2_), channel_id=1, source_target_pairs={{1,0},{0,1},{3,2},{2,3},{5,4},{4,5},{7,6},{6,7},{9,8},{8,9},{11,10... | collective-permute-start | bytes 4718600 | tf_op jit(solution)/shard_map/ppermute | solution.py:198
  275.2 44.0 %collective-permute-start.7 = (bf16[8,3,128,256]{3,2,1,0:T(8,128)(2,1)}, bf16[8,3,128,256]{3,2,1,0:T(8,128)(2,1)}, u32[]{:S(2)}, u32[]{:S(2)}) collective-permute-start(bf16[8,3,128,256]{3,2,1,0:T(8,128)(2,1)} %collective-permute-done.5.refs_5_), channel_id=1, source_target_pairs={{1,0},{0,1},{3,2},{2,3},{5,4},{4,5},{7,6},{6,7},{9,8},{8,9},{11,10... | collective-permute-start | bytes 4718600 | tf_op jit(solution)/shard_map/ppermute | solution.py:198
  303.9 15.2 %collective-permute-start.8 = (bf16[8,3,128,256]{3,2,1,0:T(8,128)(2,1)}, bf16[8,3,128,256]{3,2,1,0:T(8,128)(2,1)}, u32[]{:S(2)}, u32[]{:S(2)}) collective-permute-start(bf16[8,3,128,256]{3,2,1,0:T(8,128)(2,1)} %collective-permute-done.6.refs_6_), channel_id=1, source_target_pairs={{1,0},{0,1},{3,2},{2,3},{5,4},{4,5},{7,6},{6,7},{9,8},{8,9},{11,10... | collective-permute-start | bytes 4718600 | tf_op jit(solution)/shard_map/ppermute | solution.py:198
  311.8 1.1 copy-start.3
Sparse Core Ops, SparseCore 0:
  30.7 206.5 all-gather.2

commit v2 on v1

v2 whole, which is shorter than its diff:
```python
import math

import jax
import jax.numpy as jnp
from jax import lax
from jax.experimental import pallas as pl
from jax.experimental.pallas import tpu as pltpu
from jax.sharding import PartitionSpec as P

HDIM = 128
BLK = 128
MIB = 1 << 20
BF = jnp.bfloat16
F32 = jnp.float32


def move_pieces(pairs, buffer, sems):
    ins = [pltpu.make_async_copy(a, buffer.at[n], sems.at[0, n]) for n, (a, _) in enumerate(pairs)]
    outs = [pltpu.make_async_copy(buffer.at[n], b, sems.at[1, n]) for n, (_, b) in enumerate(pairs)]
    for copy in ins:
        copy.start()
    for copy, then in zip(ins, outs):
        copy.wait()
        then.start()
    for copy in outs:
        copy.wait()


def pack_rows(arrays, parts, chunk, chunks, after=()):
    tokens, width = arrays[0].shape
    cut = width // parts // chunks
    kinds = len(arrays)

    def kernel(*refs):
        ins, (out, buffer, sems) = refs[:kinds], refs[-3:]
        pairs = [
            (ins[i].at[:, pl.ds((s * chunks + chunk) * cut, cut)], out.at[s, i])
            for s in range(parts)
            for i in range(kinds)
        ]
        move_pieces(pairs, buffer, sems)

    return pl.pallas_call(
        kernel,
        in_specs=[pl.BlockSpec(memory_space=pl.ANY)] * (kinds + len(after)),
        out_specs=pl.BlockSpec(memory_space=pl.ANY),
        out_shape=jax.ShapeDtypeStruct((parts, kinds, tokens, cut), BF),
        scratch_shapes=[
            pltpu.VMEM((parts * kinds, tokens, cut), BF),
            pltpu.SemaphoreType.DMA((2, parts * kinds)),
        ],
        cost_estimate=pl.CostEstimate(
            flops=0, bytes_accessed=4 * kinds * tokens * parts * cut, transcendentals=0
        ),
        name="pack_rows",
    )(*arrays, *after)


def unpack_rows(packed, chunk, chunks, before, after=()):
    parts, kinds, tokens, cut = packed.shape
    before = before or []

    def kernel(*refs):
        ref, outs, (buffer, sems) = refs[0], refs[-2 - kinds : -2], refs[-2:]
        pairs = [
            (ref.at[s, i], outs[i].at[:, pl.ds((s * chunks + chunk) * cut, cut)])
            for s in range(parts)
            for i in range(kinds)
        ]
        move_pieces(pairs, buffer, sems)

    return pl.pallas_call(
        kernel,
        in_specs=[pl.BlockSpec(memory_space=pl.ANY)] * (1 + len(before) + len(after)),
        out_specs=[pl.BlockSpec(memory_space=pl.ANY)] * kinds,
        out_shape=[jax.ShapeDtypeStruct((tokens, parts * chunks * cut), BF)] * kinds,
        scratch_shapes=[
            pltpu.VMEM((parts * kinds, tokens, cut), BF),
            pltpu.SemaphoreType.DMA((2, parts * kinds)),
        ],
        input_output_aliases={1 + i: i for i in range(len(before))},
        cost_estimate=pl.CostEstimate(
            flops=0, bytes_accessed=4 * kinds * tokens * parts * cut, transcendentals=0
        ),
        name="unpack_rows",
    )(packed, *before, *after)


def hold(array, after):
    def kernel(*refs):
        pass

    return pl.pallas_call(
        kernel,
        in_specs=[pl.BlockSpec(memory_space=pl.ANY)] * (1 + len(after)),
        out_specs=pl.BlockSpec(memory_space=pl.ANY),
        out_shape=jax.ShapeDtypeStruct(array.shape, array.dtype),
        input_output_aliases={0: 0},
        name="hold",
    )(array, *after)


def turn(array, after=()):
    tokens, width = array.shape
    step = width // 2

    def kernel(*refs):
        refs[-1][...] = refs[0][...].T

    return pl.pallas_call(
        kernel,
        grid=(width // step,),
        in_specs=[pl.BlockSpec((tokens, step), lambda i: (0, i))]
        + [pl.BlockSpec(memory_space=pl.ANY)] * len(after),
        out_specs=pl.BlockSpec((step, tokens), lambda i: (i, 0)),
        out_shape=jax.ShapeDtypeStruct((width, tokens), BF),
        name="turn_layer_input",
    )(array, *after)


def attention(items, bias, after=()):
    blocks, _, _, width = items.shape
    heads = width // HDIM
    tokens = blocks * BLK
    pair = 2 * BLK
    factor = HDIM ** (-0.5)
    nt = (((1,), (1,)), ((), ()))

    def kernel(*refs):
        items_ref, bias_ref = refs[:2]
        out_ref, key_sum, value_sum = refs[-3:]
        for h in range(heads):
            cols = slice(h * HDIM, (h + 1) * HDIM)
            keys = items_ref[:, 1, :, cols].reshape(tokens, HDIM)
            values = items_ref[:, 2, :, cols].reshape(tokens, HDIM)
            keys_t = keys.T
            key_sum[...] = jnp.zeros_like(key_sum)
            value_sum[...] = jnp.zeros_like(value_sum)

            def step(n, _):
                query = items_ref[pl.ds(2 * n, 2), 0, :, cols].reshape(pair, HDIM)
                grad = items_ref[pl.ds(2 * n, 2), 3, :, cols].reshape(pair, HDIM)
                scores = lax.dot_general(keys, query, nt, preferred_element_type=F32)
                near = bias_ref[n]
                scores = (
                    scores.reshape(blocks, BLK, pair) * (factor * math.log2(math.e)) + near[:, None, :]
                ).reshape(tokens, pair)
                top = jnp.max(scores, axis=0, keepdims=True)
                weights = jnp.exp2(scores - top)
                prob_grad = lax.dot_general(values, grad, nt, preferred_element_type=F32)
                inverse = 1.0 / jnp.sum(weights, axis=0, keepdims=True)
                row_dot = jnp.sum(weights * prob_grad, axis=0, keepdims=True) * inverse
                probs = weights * inverse
                probs_low = probs.astype(BF)
                score_grad = (probs * (prob_grad - row_dot)).astype(BF)
                value_sum[...] += jnp.dot(probs_low, grad, preferred_element_type=F32)
                key_sum[...] += jnp.dot(score_grad, query, preferred_element_type=F32)
                query_grad_t = jnp.dot(keys_t, score_grad, preferred_element_type=F32) * factor
                out_ref[pl.ds(2 * n, 2), 0, :, cols] = query_grad_t.T.astype(BF).reshape(2, BLK, HDIM)
                return 0

            lax.fori_loop(0, blocks // 2, step, 0)
            out_ref[:, 1, :, cols] = (key_sum[...] * factor).astype(BF).reshape(blocks, BLK, HDIM)
            out_ref[:, 2, :, cols] = value_sum[...].astype(BF).reshape(blocks, BLK, HDIM)

    return pl.pallas_call(
        kernel,
        in_specs=[pl.BlockSpec(memory_space=pltpu.VMEM)] * 2 + [pl.BlockSpec(memory_space=pl.ANY)] * len(after),
        out_specs=pl.BlockSpec(memory_space=pltpu.VMEM),
        out_shape=jax.ShapeDtypeStruct((blocks, 3, BLK, width), BF),
        scratch_shapes=[pltpu.VMEM((tokens, HDIM), F32), pltpu.VMEM((tokens, HDIM), F32)],
        compiler_params=pltpu.CompilerParams(vmem_limit_bytes=40 * MIB),
        cost_estimate=pl.CostEstimate(
            flops=20 * heads * tokens * tokens * HDIM,
            bytes_accessed=14 * tokens * width,
            transcendentals=heads * tokens * tokens,
        ),
        name="attention_backward",
    )(items, bias, *after)


def weight_products(units, places, grads, chunk, chunks, norm, before):
    blocks = len(units)
    snaps, rows, _ = units[0].shape
    cut = grads[0].shape[-1]
    group = 4
    steps = 4
    row_step = rows // steps
    before = [] if before is None else [before]

    def kernel(*refs):
        places_ref, unit_refs, grad_refs = refs[0], refs[1 : 1 + blocks], refs[1 + blocks : 1 + blocks + snaps]
        out_ref = refs[-1]
        for start in range(0, blocks, group):
            for k in range(snaps):
                left = jnp.concatenate([unit_refs[start + u][k] for u in range(group)], axis=1)
                for kind in range(3):
                    right = jnp.concatenate(
                        [grad_refs[k][places_ref[start + u], kind] for u in range(group)], axis=0
                    )
                    part = jnp.dot(left, right, preferred_element_type=F32)
                    if start == 0 and k == 0:
                        out_ref[kind] = part
                    elif start + group == blocks and k == snaps - 1:
                        out_ref[kind] = (out_ref[kind] + part) * norm
                    else:
                        out_ref[kind] += part

    return pl.pallas_call(
        kernel,
        grid_spec=pltpu.PrefetchScalarGridSpec(
            num_scalar_prefetch=1,
            grid=(steps,),
            in_specs=[pl.BlockSpec((snaps, row_step, BLK), lambda r, _: (0, r, 0))] * blocks
            + [pl.BlockSpec((blocks, 3, BLK, cut), lambda r, _: (0, 0, 0, 0))] * snaps
            + [pl.BlockSpec(memory_space=pl.ANY)] * len(before),
            out_specs=pl.BlockSpec((3, row_step, cut), lambda r, _: (0, r, chunk)),
        ),
        out_shape=jax.ShapeDtypeStruct((3, rows, chunks * cut), F32),
        input_output_aliases={1 + blocks + snaps: 0} if before else {},
        compiler_params=pltpu.CompilerParams(vmem_limit_bytes=56 * MIB),
        cost_estimate=pl.CostEstimate(
            flops=6 * blocks * BLK * snaps * rows * cut,
            bytes_accessed=2 * blocks * snaps * BLK * (rows + 3 * cut) + 12 * rows * cut,
            transcendentals=0,
        ),
        name="weight_products",
    )(places, *units, *grads, *before)


def seq_swap(array, bit):
    return lax.ppermute(array, "seq", [(i, i ^ bit) for i in range(lax.axis_size("seq"))])


def local(layer_input, query_rows, key_rows, value_rows, out_grad, neighbours, counts):
    seq_count = lax.axis_size("seq")
    dp_count = lax.axis_size("dp")
    here = lax.axis_index("dp")
    width = query_rows.shape[2]
    heads_here = width // seq_count // HDIM
    blocks = neighbours.shape[1]
    chunks = 2 if heads_here % 2 == 0 else 1
    rows_here = layer_input.shape[2] // dp_count
    y_count = dp_count // 2

    def peer(p, j, e):
        return ((p // 2 + j) % y_count) * 2 + ((p % 2) ^ e)

    peers = [(j, e) for j in range(y_count) for e in range(2)]

    def dp_move(array, j, e):
        return lax.ppermute(array, "dp", [(peer(p, j, e), p) for p in range(dp_count)])

    rows_in = [query_rows[0], key_rows[0], value_rows[0], out_grad[0]]
    live = jnp.arange(neighbours.shape[2])[None, :] < counts[0][:, None]
    hit = (neighbours[0][:, :, None] == jnp.arange(blocks)[None, None, :]) & live[:, :, None]
    near = jnp.where(jnp.any(hit, axis=1), 0.0, -jnp.inf).astype(F32)
    bias = jnp.repeat(near.reshape(blocks // 2, 2, blocks).transpose(0, 2, 1), BLK, axis=2)

    packed = [pack_rows(rows_in, seq_count, 0, chunks)]
    items = [lax.all_to_all(packed[0], "seq", 0, 0, tiled=True)]

    turned = turn(layer_input[0], packed)
    slabs = []
    for j, e in peers:
        to = peer(here, (y_count - j) % y_count, e)
        slab = lax.dynamic_slice_in_dim(turned, to * rows_here, rows_here, 0)
        slabs.append(slab if (j, e) == (0, 0) else dp_move(slab, j, e))
    packed += [pack_rows(rows_in, seq_count, c, chunks, [turned]) for c in range(1, chunks)]
    own = jnp.stack(slabs)
    at = lax.axis_index("seq")
    ready, behind = [[] for _ in range(chunks)], [[], []]
    if seq_count == 8:
        beside, far, own_x = seq_swap(own, 2), seq_swap(own, 4), seq_swap(own, 1)
        beside_x = seq_swap(beside, 1)
        for c in range(1, chunks):
            packed[c] = hold(packed[c], [beside, far, own_x, beside_x])
        ready[0] = packed[1:2]
        far_beside, far_x = seq_swap(far, 2), seq_swap(far, 1)
        far_beside_x = seq_swap(far_beside, 1)
        behind = [[far_beside, far_x], [far_beside_x]]
        units = [own, beside, far, far_beside, own_x, beside_x, far_x, far_beside_x]
        places = jnp.stack([at ^ bits for bits in (0, 2, 4, 6, 1, 3, 5, 7)]).astype(jnp.int32)
    else:
        every = lax.all_gather(own, "seq", axis=0, tiled=False)
        units, places = [every[i] for i in range(seq_count)], jnp.arange(seq_count, dtype=jnp.int32)
    items += [lax.all_to_all(a, "seq", 0, 0, tiled=True) for a in packed[1:]]

    norm = 1.0 / math.sqrt(neighbours.shape[1] * BLK * dp_count)
    weight_grad, done = None, None
    for c in range(chunks):
        out = attention(items[c], bias, ready[c])
        over_y = [out] + [dp_move(out, j, 0) for j in range(1, y_count)]
        grads = [a for there in over_y for a in (there, dp_move(there, 0, 1))]
        late = behind[c] + (over_y[1:] if c == 0 else [])
        back = hold(out, late) if late and chunks == 2 else out
        back = lax.all_to_all(back, "seq", 0, 0, tiled=True)
        weight_grad = weight_products(units, places, grads, c, chunks, norm, weight_grad)
        done = unpack_rows(back, c, chunks, done, [weight_grad] if c == chunks - 1 else [])
    query_grad, key_grad, value_grad = done
    return query_grad[None], key_grad[None], value_grad[None], weight_grad


def solution(mesh):
    placed = (P("dp", "seq", None),) * 5 + (P("dp", None, None), P("dp", None))
    return jax.shard_map(
        local,
        mesh=mesh,
        in_specs=placed,
        out_specs=(P("dp", "seq", None),) * 3 + (P(None, "dp", "seq"),),
        check_vma=False,
    )
```

time: 347 us -> 261 us (0.75)
  blocking collectives: 86.4 us -> 0 us
  starting transfers between devices: 17.6 us -> 39 us
  between operations: 14.2 us -> 0.99 us
  waiting for transfers between devices: 160 us -> 152 us
    ppermute x0 -> x7, waiting for transfers between devices: none -> 131 us  [seq_swap(): lax.ppermute(array, 'seq', [(i, i ^ bit) for i in range(lax.axis_size('se...]
    all_to_all x3 -> x4, waiting for transfers between devices: 119 us -> 5.32 us  [the longest x2 5.31 us: local(): back = lax.all_to_all(back, 'seq', 0, 0, tiled=True)]
    all_to_all x1 -> x0, blocking collectives: 86.4 us -> none  [local(): items = lax.all_to_all(packed[c], 'seq', 0, 0, tiled=True)]
    ppermute x9, waiting for transfers between devices: 40.9 us -> 15.6 us  [dp_move(): lax.ppermute(array, 'dp', [(peer(p, j, e), p) for p in range(dp_count)])]
    ppermute x0 -> x7, starting transfers between devices: none -> 12.3 us  [seq_swap(): lax.ppermute(array, 'seq', [(i, i ^ bit) for i in range(lax.axis_size('se...]
    all_to_all x3 -> x4, starting transfers between devices: 11.7 us -> 21 us  [the longest x2 9.26 us: local(): back = lax.all_to_all(back, 'seq', 0, 0, tiled=True)]
    pallas_call x3 -> x9, Pallas kernels: 33.5 us -> 35.5 us  [the longest x2 25 us: weight_products(): pl.pallas_call(kernel, grid_spec=pltpu.PrefetchScalarGridSpec(num_scalar_...]
  transfers between devices with their start and end apart: 13 -> 20, of which waited for: 6 -> 9; matrix products, arithmetic and copies ran while one was open for 0% -> 2% of each run, Pallas kernels for 10% -> 22%
where the time goes in v2:
time: 261 us
  waiting for transfers between devices  152 us (58%)
  Pallas kernels  62.7 us (24%)
  starting transfers between devices  39 us (15%)
  local copies, waits for them, and re-layouts  5.26 us (2%)
    ppermute x7, waiting for transfers between devices, seq_swap(): lax.ppermute(array, 'seq', [(i, i ^ bit) for i in range(lax.axis_size('se...  131 us
    pallas_call x2, Pallas kernels, attention(): pl.pallas_call(kernel, in_specs=[pl.BlockSpec(memory_space=pltpu.VMEM)] *...  25 us
    pallas_call x2, Pallas kernels, weight_products(): pl.pallas_call(kernel, grid_spec=pltpu.PrefetchScalarGridSpec(num_scalar_...  25 us
    ppermute x9, waiting for transfers between devices, dp_move(): lax.ppermute(array, 'dp', [(peer(p, j, e), p) for p in range(dp_count)])  15.6 us
    ppermute x7, starting transfers between devices, seq_swap(): lax.ppermute(array, 'seq', [(i, i ^ bit) for i in range(lax.axis_size('se...  12.3 us
    all_to_all x2, starting transfers between devices, local(): back = lax.all_to_all(back, 'seq', 0, 0, tiled=True)  9.26 us
    all_to_all x1, starting transfers between devices, local(): items = [lax.all_to_all(packed[0], 'seq', 0, 0, tiled=True)]  7.26 us
    ppermute x9, starting transfers between devices, dp_move(): lax.ppermute(array, 'dp', [(peer(p, j, e), p) for p in range(dp_count)])  5.69 us
  transfers between devices with their start and end apart: 20, of which 9 were waited for; matrix products, arithmetic and copies ran while one was open for 2% of the time, Pallas kernels for 22%

profile of v2, /device:TPU:0, one launch (start us, length us, event | category | flops | bytes accessed | tf_op | source)
XLA Modules:
  0.0 260.6 jit_solution(4667612075562889269)
XLA Ops:
  0.6 2.8 %pack_rows.2.refs_1_ = bf16[8,4,128,256]{3,2,1,0:T(8,128)(2,1)} custom-call(bf16[128,4096]{1,0:T(8,128)(2,1)} %bitcast.28, bf16[128,4096]{1,0:T(8,128)(2,1)} %bitcast.30, bf16[128,4096]{1,0:T(8,128)(2,1)} %bitcast.32, bf16[128,4096]{1,0:T(8,128)(2,1)} %bitcast.34), custom_call_target="tpu_custom_call" | custom-call | bytes 4194304 | tf_op jit(solution)/shard_map/pack_rows/pallas_call | solution.py:43
  3.4 7.3 %all-to-all-start.2 = ((bf16[8,4,128,256]{3,2,1,0:T(8,128)(2,1)}), bf16[8,4,128,256]{3,2,1,0:T(8,128)(2,1)}, u32[]{:S(2)}, u32[]{:S(2)}) async-start(bf16[8,4,128,256]{3,2,1,0:T(8,128)(2,1)} %pack_rows.2.refs_1_), calls=%async_computation.2 | async-start | bytes 4194304 | tf_op jit(solution)/shard_map/all_to_all | solution.py:261
  10.7 2.2 turn_layer_input.1.refs_4_
  12.9 1.3 dynamic-slice_bitcast_fusion
  14.2 0.1 collective-permute-start
  14.3 1.6 collective-permute-start.1
  15.9 0.3 collective-permute-start.2
  16.1 7.3 %collective-permute-done.1 = bf16[1024,128]{1,0:T(8,128)(2,1)S(1)} collective-permute-done((bf16[1024,128]{1,0:T(8,128)(2,1)S(1)}, bf16[1024,128]{1,0:T(8,128)(2,1)S(1)}, u32[]{:S(2)}, u32[]{:S(2)}) %collective-permute-start.1) | collective-permute-done | bytes 262176 | tf_op jit(solution)/shard_map/ppermute | solution.py:252
  23.4 4.7 %collective-permute-done.2 = bf16[1024,128]{1,0:T(8,128)(2,1)S(1)} collective-permute-done((bf16[1024,128]{1,0:T(8,128)(2,1)S(1)}, bf16[1024,128]{1,0:T(8,128)(2,1)S(1)}, u32[]{:S(2)}, u32[]{:S(2)}) %collective-permute-start.2) | collective-permute-done | bytes 262176 | tf_op jit(solution)/shard_map/ppermute | solution.py:252
  28.2 0.1 pad_maximum_fusion.refs_1_
  28.3 2.1 collective-permute-start.3
  30.4 2.4 collective-permute-start.4
  32.8 1.5 collective-permute-start.5
  34.2 47.7 %collective-permute-done.3.refs_1_.refs_2_ = bf16[4,1024,128]{2,1,0:T(8,128)(2,1)S(1)} collective-permute-done((bf16[4,1024,128]{2,1,0:T(8,128)(2,1)S(1)}, bf16[4,1024,128]{2,1,0:T(8,128)(2,1)S(1)}, u32[]{:S(2)}, u32[]{:S(2)}) %collective-permute-start.3) | collective-permute-done | bytes 1048608 | tf_op jit(solution)/shard_map/ppermute | solution.py:232
  82.0 1.0 collective-permute-start.6
  82.9 2.9 %pack_rows.3.refs_0_ = bf16[8,4,128,256]{3,2,1,0:T(8,128)(2,1)} custom-call(bf16[128,4096]{1,0:T(8,128)(2,1)} %bitcast.29, bf16[128,4096]{1,0:T(8,128)(2,1)} %bitcast.31, bf16[128,4096]{1,0:T(8,128)(2,1)} %bitcast.33, bf16[128,4096]{1,0:T(8,128)(2,1)} %bitcast.35, bf16[4096,128]{1,0:T(8,128)(2,1)} %turn_layer_input.1.refs_4_), custom_call_target="tpu_custom_call" | custom-call | bytes 4194304 | tf_op jit(solution)/shard_map/pack_rows/pallas_call | solution.py:43
  85.8 18.1 %collective-permute-done.4.refs_2_.refs_3_ = bf16[4,1024,128]{2,1,0:T(8,128)(2,1)S(1)} collective-permute-done((bf16[4,1024,128]{2,1,0:T(8,128)(2,1)S(1)}, bf16[4,1024,128]{2,1,0:T(8,128)(2,1)S(1)}, u32[]{:S(2)}, u32[]{:S(2)}) %collective-permute-start.4) | collective-permute-done | bytes 1048608 | tf_op jit(solution)/shard_map/ppermute | solution.py:232
  103.9 0.0 collective-permute-done.5.refs_3_.refs_5_
  103.9 3.3 %collective-permute-done.6.refs_4_.refs_6_ = bf16[4,1024,128]{2,1,0:T(8,128)(2,1)} collective-permute-done((bf16[4,1024,128]{2,1,0:T(8,128)(2,1)S(1)}, bf16[4,1024,128]{2,1,0:T(8,128)(2,1)}, u32[]{:S(2)}, u32[]{:S(2)}) %collective-permute-start.6) | collective-permute-done | bytes 1048608 | tf_op jit(solution)/shard_map/ppermute | solution.py:232
  107.3 0.0 all-to-all-done.2.refs_0_
  107.3 4.5 %all-to-all-start = ((bf16[8,4,128,256]{3,2,1,0:T(8,128)(2,1)}), bf16[8,4,128,256]{3,2,1,0:T(8,128)(2,1)}, u32[]{:S(2)}, u32[]{:S(2)}) async-start(bf16[8,4,128,256]{3,2,1,0:T(8,128)(2,1)} %hold.3.refs_2_), calls=%async_computation | async-start | bytes 4194304 | tf_op jit(solution)/shard_map/all_to_all | solution.py:287
  111.8 0.1 iota_compare_fusion.1
  111.8 0.1 fusion.1
  112.0 0.1 broadcast_bitcast_fusion.refs_1_
  112.0 12.5 %attention_backward.3.refs_9_ = bf16[8,3,128,256]{3,2,1,0:T(8,128)(2,1)S(1)} custom-call(bf16[8,4,128,256]{3,2,1,0:T(8,128)(2,1)} %all-to-all-done.2.refs_0_, f32[4,8,256]{2,1,0:T(8,128)S(1)} %broadcast_bitcast_fusion.refs_1_, bf16[8,4,128,256]{3,2,1,0:T(8,128)(2,1)S(1)} %copy-done), custom_call_target="tpu_custom_call" | custom-call | flops 5368709120 | bytes 3670016 | tf_op jit(solution)/shard_map/attention_backward/pallas_call | solution.py:166
  124.6 1.6 collective-permute-start.10
  126.2 1.9 collective-permute-start.7
  128.1 1.5 collective-permute-start.9
  129.5 1.1 copy.20.refs_0_
  130.7 39.4 %collective-permute-done.7.refs_1_.refs_4_ = bf16[4,1024,128]{2,1,0:T(8,128)(2,1)} collective-permute-done((bf16[4,1024,128]{2,1,0:T(8,128)(2,1)S(1)}, bf16[4,1024,128]{2,1,0:T(8,128)(2,1)}, u32[]{:S(2)}, u32[]{:S(2)}) %collective-permute-start.7) | collective-permute-done | bytes 1048608 | tf_op jit(solution)/shard_map/ppermute | solution.py:232
  170.0 0.0 collective-permute-done.9.refs_2_.refs_7_
  170.0 1.0 copy-done.5
  171.0 4.7 %all-to-all-start.3 = ((bf16[8,3,128,256]{3,2,1,0:T(8,128)(2,1)}), bf16[8,3,128,256]{3,2,1,0:T(8,128)(2,1)}, u32[]{:S(2)}, u32[]{:S(2)}) async-start(bf16[8,3,128,256]{3,2,1,0:T(8,128)(2,1)} %hold.5), calls=%async_computation.3 | async-start | bytes 3145728 | tf_op jit(solution)/shard_map/all_to_all | solution.py:297
  175.8 2.0 collective-permute-start.8
  177.8 12.4 %attention_backward.2.refs_9_ = bf16[8,3,128,256]{3,2,1,0:T(8,128)(2,1)S(1)} custom-call(bf16[8,4,128,256]{3,2,1,0:T(8,128)(2,1)} %all-to-all-done.refs_0_, f32[4,8,256]{2,1,0:T(8,128)S(1)} %broadcast_bitcast_fusion.refs_1_), custom_call_target="tpu_custom_call" | custom-call | flops 5368709120 | bytes 3670016 | tf_op jit(solution)/shard_map/attention_backward/pallas_call | solution.py:166
  190.2 1.6 collective-permute-start.12
  191.8 0.5 collective-permute-start.15
  192.3 1.1 copy.19.refs_0_
  193.5 22.9 %collective-permute-done.8.refs_1_.refs_8_ = bf16[4,1024,128]{2,1,0:T(8,128)(2,1)} collective-permute-done((bf16[4,1024,128]{2,1,0:T(8,128)(2,1)}, bf16[4,1024,128]{2,1,0:T(8,128)(2,1)}, u32[]{:S(2)}, u32[]{:S(2)}) %collective-permute-start.8) | collective-permute-done | bytes 1048608 | tf_op jit(solution)/shard_map/ppermute | solution.py:232
  216.4 4.5 %all-to-all-start.1 = ((bf16[8,3,128,256]{3,2,1,0:T(8,128)(2,1)}), bf16[8,3,128,256]{3,2,1,0:T(8,128)(2,1)}, u32[]{:S(2)}, u32[]{:S(2)}) async-start(bf16[8,3,128,256]{3,2,1,0:T(8,128)(2,1)} %hold.4), calls=%async_computation.1 | async-start | bytes 3145728 | tf_op jit(solution)/shard_map/all_to_all | solution.py:297
  221.0 0.1 collective-permute-start.11
  221.0 3.5 %collective-permute-done.12.refs_11_ = bf16[8,3,128,256]{3,2,1,0:T(8,128)(2,1)} collective-permute-done((bf16[8,3,128,256]{3,2,1,0:T(8,128)(2,1)S(1)}, bf16[8,3,128,256]{3,2,1,0:T(8,128)(2,1)}, u32[]{:S(2)}, u32[]{:S(2)}) %collective-permute-start.12) | collective-permute-done | bytes 1572896 | tf_op jit(solution)/shard_map/ppermute | solution.py:252
  224.6 0.6 stack.55.refs_0_
  225.2 12.5 %weight_products.2.refs_13_ = f32[3,1024,512]{2,1,0:T(8,128)} custom-call(s32[8]{0:T(128)} %stack.55.refs_0_, bf16[4,1024,128]{2,1,0:T(8,128)(2,1)} %copy-done.4, bf16[4,1024,128]{2,1,0:T(8,128)(2,1)} %copy-done.6, bf16[4,1024,128]{2,1,0:T(8,128)(2,1)} %copy-done.7, bf16[4,1024,128]{2,1,0:T(8,128)(2,1)} %collective-permute-done.7.refs_1_.refs_4_, ...), custom_call_target="tpu_custom_call" | custom-call | flops 6442450944 | bytes 17825792 | tf_op jit(solution)/shard_map/weight_products/pallas_call | solution.py:209
  237.7 2.5 unpack_rows.2
  240.2 12.5 %weight_products.3.refs_4_ = f32[3,1024,512]{2,1,0:T(8,128)} custom-call(s32[8]{0:T(128)} %stack.55.refs_0_, bf16[4,1024,128]{2,1,0:T(8,128)(2,1)} %copy-done.4, bf16[4,1024,128]{2,1,0:T(8,128)(2,1)} %copy-done.6, bf16[4,1024,128]{2,1,0:T(8,128)(2,1)} %copy-done.7, ...), custom_call_target="tpu_custom_call", output_to_operand_aliasing={{}: (13, {})} | custom-call | flops 6442450944 | bytes 17825792 | tf_op jit(solution)/shard_map/weight_products/pallas_call | solution.py:209
  252.7 5.3 %all-to-all-done.1.refs_0_ = bf16[8,3,128,256]{3,2,1,0:T(8,128)(2,1)} async-done(((bf16[8,3,128,256]{3,2,1,0:T(8,128)(2,1)}), bf16[8,3,128,256]{3,2,1,0:T(8,128)(2,1)}, u32[]{:S(2)}, u32[]{:S(2)}) %all-to-all-start.1) | async-done | bytes 1572896 | tf_op jit(solution)/shard_map/all_to_all | solution.py:297
  258.0 2.5 unpack_rows.3
  (35 shorter events, 0.1 us)
Async XLA Ops:
  3.4 103.8 %all-to-all-start.2 = ((bf16[8,4,128,256]{3,2,1,0:T(8,128)(2,1)}), bf16[8,4,128,256]{3,2,1,0:T(8,128)(2,1)}, u32[]{:S(2)}, u32[]{:S(2)}) async-start(bf16[8,4,128,256]{3,2,1,0:T(8,128)(2,1)} %pack_rows.2.refs_1_), calls=%async_computation.2 | async-start | bytes 4194304 | tf_op jit(solution)/shard_map/all_to_all | solution.py:261
  14.2 1.9 collective-permute-start
  14.3 9.2 %collective-permute-start.1 = (bf16[1024,128]{1,0:T(8,128)(2,1)S(1)}, bf16[1024,128]{1,0:T(8,128)(2,1)S(1)}, u32[]{:S(2)}, u32[]{:S(2)}) collective-permute-start(bf16[1024,128]{1,0:T(8,128)(2,1)S(1)} %get-tuple-element.18), channel_id=1, source_target_pairs={{2,0},{3,1},{0,2},{1,3},{6,4},{7,5},{4,6},{5,7},{10,8},{11,9},{8,1... | collective-permute-start | bytes 786440 | tf_op jit(solution)/shard_map/ppermute | solution.py:252
  15.9 12.3 %collective-permute-start.2 = (bf16[1024,128]{1,0:T(8,128)(2,1)S(1)}, bf16[1024,128]{1,0:T(8,128)(2,1)S(1)}, u32[]{:S(2)}, u32[]{:S(2)}) collective-permute-start(bf16[1024,128]{1,0:T(8,128)(2,1)S(1)} %get-tuple-element.17), channel_id=1, source_target_pairs={{3,0},{2,1},{1,2},{0,3},{7,4},{6,5},{5,6},{4,7},{11,8},{10,9},{9,1... | collective-permute-start | bytes 786440 | tf_op jit(solution)/shard_map/ppermute | solution.py:252
  28.3 57.5 %copy-start.4 = (bf16[4,1024,128]{2,1,0:T(8,128)(2,1)}, bf16[4,1024,128]{2,1,0:T(8,128)(2,1)S(1)}, u32[]{:S(2)}) copy-start(bf16[4,1024,128]{2,1,0:T(8,128)(2,1)S(1)} %pad_maximum_fusion.refs_1_) | copy-start | bytes 3145732
  28.3 53.6 %collective-permute-start.3 = (bf16[4,1024,128]{2,1,0:T(8,128)(2,1)S(1)}, bf16[4,1024,128]{2,1,0:T(8,128)(2,1)S(1)}, u32[]{:S(2)}, u32[]{:S(2)}) collective-permute-start(bf16[4,1024,128]{2,1,0:T(8,128)(2,1)S(1)} %pad_maximum_fusion.refs_1_), channel_id=1, source_target_pairs={{0,8},{4,12},{8,0},{12,4},{16,24},{20,28},{24,16},{28,20},{1,9},{5... | collective-permute-start | bytes 3145736 | tf_op jit(solution)/shard_map/ppermute | solution.py:232
  30.4 73.5 %collective-permute-start.4 = (bf16[4,1024,128]{2,1,0:T(8,128)(2,1)S(1)}, bf16[4,1024,128]{2,1,0:T(8,128)(2,1)S(1)}, u32[]{:S(2)}, u32[]{:S(2)}) collective-permute-start(bf16[4,1024,128]{2,1,0:T(8,128)(2,1)S(1)} %pad_maximum_fusion.refs_1_), channel_id=1, source_target_pairs={{0,16},{4,20},{8,24},{12,28},{16,0},{20,4},{24,8},{28,12},{1,17},{... | collective-permute-start | bytes 3145736 | tf_op jit(solution)/shard_map/ppermute | solution.py:232
  32.8 71.2 %collective-permute-start.5 = (bf16[4,1024,128]{2,1,0:T(8,128)(2,1)S(1)}, bf16[4,1024,128]{2,1,0:T(8,128)(2,1)}, u32[]{:S(2)}, u32[]{:S(2)}) collective-permute-start(bf16[4,1024,128]{2,1,0:T(8,128)(2,1)S(1)} %pad_maximum_fusion.refs_1_), channel_id=1, source_target_pairs={{0,4},{4,0},{8,12},{12,8},{16,20},{20,16},{24,28},{28,24},{1,5},{5... | collective-permute-start | bytes 3145736 | tf_op jit(solution)/shard_map/ppermute | solution.py:232
  81.9 3.9 %copy-start.6 = (bf16[4,1024,128]{2,1,0:T(8,128)(2,1)}, bf16[4,1024,128]{2,1,0:T(8,128)(2,1)S(1)}, u32[]{:S(2)}) copy-start(bf16[4,1024,128]{2,1,0:T(8,128)(2,1)S(1)} %collective-permute-done.3.refs_1_.refs_2_) | copy-start | bytes 3145732
  82.0 25.3 %collective-permute-start.6 = (bf16[4,1024,128]{2,1,0:T(8,128)(2,1)S(1)}, bf16[4,1024,128]{2,1,0:T(8,128)(2,1)}, u32[]{:S(2)}, u32[]{:S(2)}) collective-permute-start(bf16[4,1024,128]{2,1,0:T(8,128)(2,1)S(1)} %collective-permute-done.3.refs_1_.refs_2_), channel_id=1, source_target_pairs={{0,4},{4,0},{8,12},{12,8},{16,20},{20,16},{24,28},{28,24},{1,5},{5... | collective-permute-start | bytes 3145736 | tf_op jit(solution)/shard_map/ppermute | solution.py:232
  103.9 3.3 %copy-start.7 = (bf16[4,1024,128]{2,1,0:T(8,128)(2,1)}, bf16[4,1024,128]{2,1,0:T(8,128)(2,1)S(1)}, u32[]{:S(2)}) copy-start(bf16[4,1024,128]{2,1,0:T(8,128)(2,1)S(1)} %collective-permute-done.4.refs_2_.refs_3_) | copy-start | bytes 3145732
  107.2 4.5 %copy-start.10 = (s32[1,8]{1,0:T(1,128)S(1)}, s32[1,8]{1,0:T(1,128)}, u32[]{:S(2)}) copy-start(s32[1,8]{1,0:T(1,128)} %param.13) | copy-start | bytes 100
  107.2 4.6 %copy-start.9 = (s32[1,8,8]{2,1,0:T(8,128)S(1)}, s32[1,8,8]{2,1,0:T(8,128)}, u32[]{:S(2)}) copy-start(s32[1,8,8]{2,1,0:T(8,128)} %param.12) | copy-start | bytes 772
  107.2 4.8 %copy-start = (bf16[8,4,128,256]{3,2,1,0:T(8,128)(2,1)S(1)}, bf16[8,4,128,256]{3,2,1,0:T(8,128)(2,1)}, u32[]{:S(2)}) copy-start(bf16[8,4,128,256]{3,2,1,0:T(8,128)(2,1)} %hold.3.refs_2_) | copy-start | bytes 6291460
  107.3 63.8 %all-to-all-start = ((bf16[8,4,128,256]{3,2,1,0:T(8,128)(2,1)}), bf16[8,4,128,256]{3,2,1,0:T(8,128)(2,1)}, u32[]{:S(2)}, u32[]{:S(2)}) async-start(bf16[8,4,128,256]{3,2,1,0:T(8,128)(2,1)} %hold.3.refs_2_), calls=%async_computation | async-start | bytes 4194304 | tf_op jit(solution)/shard_map/all_to_all | solution.py:287
  112.0 14.1 %copy-start.8 = (bf16[4,1024,128]{2,1,0:T(8,128)(2,1)S(1)}, bf16[4,1024,128]{2,1,0:T(8,128)(2,1)}, u32[]{:S(2)}) copy-start(bf16[4,1024,128]{2,1,0:T(8,128)(2,1)} %copy-done.7) | copy-start | bytes 3145732
  124.6 6.1 %copy-start.2 = (bf16[8,3,128,256]{3,2,1,0:T(8,128)(2,1)}, bf16[8,3,128,256]{3,2,1,0:T(8,128)(2,1)S(1)}, u32[]{:S(2)}) copy-start(bf16[8,3,128,256]{3,2,1,0:T(8,128)(2,1)S(1)} %attention_backward.3.refs_9_) | copy-start | bytes 4718596
  124.6 45.5 %collective-permute-start.10 = (bf16[8,3,128,256]{3,2,1,0:T(8,128)(2,1)S(1)}, bf16[8,3,128,256]{3,2,1,0:T(8,128)(2,1)}, u32[]{:S(2)}, u32[]{:S(2)}) collective-permute-start(bf16[8,3,128,256]{3,2,1,0:T(8,128)(2,1)S(1)} %attention_backward.3.refs_9_), channel_id=1, source_target_pairs={{2,0},{3,1},{0,2},{1,3},{6,4},{7,5},{4,6},{5,7},{10,8},{11,9},{8,1... | collective-permute-start | bytes 4718600 | tf_op jit(solution)/shard_map/ppermute | solution.py:252
  126.2 43.9 %collective-permute-start.7 = (bf16[4,1024,128]{2,1,0:T(8,128)(2,1)S(1)}, bf16[4,1024,128]{2,1,0:T(8,128)(2,1)}, u32[]{:S(2)}, u32[]{:S(2)}) collective-permute-start(bf16[4,1024,128]{2,1,0:T(8,128)(2,1)S(1)} %copy-done.8), channel_id=1, source_target_pairs={{0,8},{4,12},{8,0},{12,4},{16,24},{20,28},{24,16},{28,20},{1,9},{5... | collective-permute-start | bytes 3145736 | tf_op jit(solution)/shard_map/ppermute | solution.py:232
  128.1 42.0 %collective-permute-start.9 = (bf16[4,1024,128]{2,1,0:T(8,128)(2,1)S(1)}, bf16[4,1024,128]{2,1,0:T(8,128)(2,1)S(1)}, u32[]{:S(2)}, u32[]{:S(2)}) collective-permute-start(bf16[4,1024,128]{2,1,0:T(8,128)(2,1)S(1)} %copy-done.8), channel_id=1, source_target_pairs={{0,4},{4,0},{8,12},{12,8},{16,20},{20,16},{24,28},{28,24},{1,5},{5... | collective-permute-start | bytes 3145736 | tf_op jit(solution)/shard_map/ppermute | solution.py:232
  170.0 1.0 copy-start.5
  171.0 45.4 %all-to-all-start.3 = ((bf16[8,3,128,256]{3,2,1,0:T(8,128)(2,1)}), bf16[8,3,128,256]{3,2,1,0:T(8,128)(2,1)}, u32[]{:S(2)}, u32[]{:S(2)}) async-start(bf16[8,3,128,256]{3,2,1,0:T(8,128)(2,1)} %hold.5), calls=%async_computation.3 | async-start | bytes 3145728 | tf_op jit(solution)/shard_map/all_to_all | solution.py:297
  175.8 16.1 %copy-start.3 = (bf16[8,3,128,256]{3,2,1,0:T(8,128)(2,1)S(1)}, bf16[8,3,128,256]{3,2,1,0:T(8,128)(2,1)}, u32[]{:S(2)}) copy-start(bf16[8,3,128,256]{3,2,1,0:T(8,128)(2,1)} %copy-done.2) | copy-start | bytes 4718596
  175.8 40.6 %collective-permute-start.8 = (bf16[4,1024,128]{2,1,0:T(8,128)(2,1)}, bf16[4,1024,128]{2,1,0:T(8,128)(2,1)}, u32[]{:S(2)}, u32[]{:S(2)}) collective-permute-start(bf16[4,1024,128]{2,1,0:T(8,128)(2,1)} %collective-permute-done.7.refs_1_.refs_4_), channel_id=1, source_target_pairs={{0,4},{4,0},{8,12},{12,8},{16,20},{20,16},{24,28},{28,24},{1,5},{5... | collective-permute-start | bytes 3145736 | tf_op jit(solution)/shard_map/ppermute | solution.py:232
  190.2 30.7 %copy-start.1 = (bf16[8,3,128,256]{3,2,1,0:T(8,128)(2,1)}, bf16[8,3,128,256]{3,2,1,0:T(8,128)(2,1)S(1)}, u32[]{:S(2)}) copy-start(bf16[8,3,128,256]{3,2,1,0:T(8,128)(2,1)S(1)} %attention_backward.2.refs_9_) | copy-start | bytes 4718596
  190.2 34.3 %collective-permute-start.12 = (bf16[8,3,128,256]{3,2,1,0:T(8,128)(2,1)S(1)}, bf16[8,3,128,256]{3,2,1,0:T(8,128)(2,1)}, u32[]{:S(2)}, u32[]{:S(2)}) collective-permute-start(bf16[8,3,128,256]{3,2,1,0:T(8,128)(2,1)S(1)} %attention_backward.2.refs_9_), channel_id=1, source_target_pairs={{2,0},{3,1},{0,2},{1,3},{6,4},{7,5},{4,6},{5,7},{10,8},{11,9},{8,1... | collective-permute-start | bytes 4718600 | tf_op jit(solution)/shard_map/ppermute | solution.py:252
  191.8 33.4 %collective-permute-start.14 = (bf16[8,3,128,256]{3,2,1,0:T(8,128)(2,1)S(1)}, bf16[8,3,128,256]{3,2,1,0:T(8,128)(2,1)}, u32[]{:S(2)}, u32[]{:S(2)}) collective-permute-start(bf16[8,3,128,256]{3,2,1,0:T(8,128)(2,1)S(1)} %copy-done.3), channel_id=1, source_target_pairs={{1,0},{0,1},{3,2},{2,3},{5,4},{4,5},{7,6},{6,7},{9,8},{8,9},{11,10... | collective-permute-start | bytes 4718600 | tf_op jit(solution)/shard_map/ppermute | solution.py:252
  191.8 33.4 %collective-permute-start.15 = (bf16[8,3,128,256]{3,2,1,0:T(8,128)(2,1)}, bf16[8,3,128,256]{3,2,1,0:T(8,128)(2,1)}, u32[]{:S(2)}, u32[]{:S(2)}) collective-permute-start(bf16[8,3,128,256]{3,2,1,0:T(8,128)(2,1)} %collective-permute-done.10.refs_3_.refs_11_), channel_id=1, source_target_pairs={{1,0},{0,1},{3,2},{2,3},{5,4},{4,5},{7,6},{6,7},{9,8},{8,9},{11,10... | collective-permute-start | bytes 4718600 | tf_op jit(solution)/shard_map/ppermute | solution.py:252
  216.4 41.5 %all-to-all-start.1 = ((bf16[8,3,128,256]{3,2,1,0:T(8,128)(2,1)}), bf16[8,3,128,256]{3,2,1,0:T(8,128)(2,1)}, u32[]{:S(2)}, u32[]{:S(2)}) async-start(bf16[8,3,128,256]{3,2,1,0:T(8,128)(2,1)} %hold.4), calls=%async_computation.1 | async-start | bytes 3145728 | tf_op jit(solution)/shard_map/all_to_all | solution.py:297
  221.0 19.2 %collective-permute-start.11 = (bf16[8,3,128,256]{3,2,1,0:T(8,128)(2,1)S(1)}, bf16[8,3,128,256]{3,2,1,0:T(8,128)(2,1)}, u32[]{:S(2)}, u32[]{:S(2)}) collective-permute-start(bf16[8,3,128,256]{3,2,1,0:T(8,128)(2,1)S(1)} %attention_backward.2.refs_9_), channel_id=1, source_target_pairs={{1,0},{0,1},{3,2},{2,3},{5,4},{4,5},{7,6},{6,7},{9,8},{8,9},{11,10... | collective-permute-start | bytes 4718600 | tf_op jit(solution)/shard_map/ppermute | solution.py:252
  224.6 15.6 %collective-permute-start.13 = (bf16[8,3,128,256]{3,2,1,0:T(8,128)(2,1)}, bf16[8,3,128,256]{3,2,1,0:T(8,128)(2,1)}, u32[]{:S(2)}, u32[]{:S(2)}) collective-permute-start(bf16[8,3,128,256]{3,2,1,0:T(8,128)(2,1)} %collective-permute-done.12.refs_11_), channel_id=1, source_target_pairs={{1,0},{0,1},{3,2},{2,3},{5,4},{4,5},{7,6},{6,7},{9,8},{8,9},{11,10... | collective-permute-start | bytes 4718600 | tf_op jit(solution)/shard_map/ppermute | solution.py:252

commit v3 on v2

--- a/solution.py
+++ b/solution.py
@@ -12,6 +12,10 @@
 MIB = 1 << 20
 BF = jnp.bfloat16
 F32 = jnp.float32
+HOLD_1 = [(2, 0), (2, 1), (4, 0), (4, 1), (1, 0), (1, 1), (3, 0), (3, 1)]
+HOLD_2 = [(6, 0), (5, 0), (5, 1)]
+LATE = [(7, 1)]
+HOLD_3 = [(6, 1), (7, 0)]
 
 
 def move_pieces(pairs, buffer, sems):
@@ -180,44 +184,49 @@
 
 
 def weight_products(units, places, grads, chunk, chunks, norm, before):
-    blocks = len(units)
-    snaps, rows, _ = units[0].shape
+    blocks, snaps = len(units), len(grads)
+    rows = units[0][0][0].shape[1]
     cut = grads[0].shape[-1]
     group = 4
     steps = 4
     row_step = rows // steps
     before = [] if before is None else [before]
-
-    def kernel(*refs):
-        places_ref, unit_refs, grad_refs = refs[0], refs[1 : 1 + blocks], refs[1 + blocks : 1 + blocks + snaps]
-        out_ref = refs[-1]
+    flat = [piece for unit in units for piece, _ in unit]
+    spots, at = [], 0
+    for unit in units:
+        spot = {}
+        for piece, snap in unit:
+            spot.update({snap + i: (at, i) for i in range(piece.shape[0])})
+            at += 1
+        spots.append(spot)
+
+    def kernel(*refs):
+        places_ref, unit_refs = refs[0], refs[1 : 1 + len(flat)]
+        grad_refs, out_ref = refs[1 + len(flat) : 1 + len(flat) + snaps], refs[-1]
         for start in range(0, blocks, group):
             for k in range(snaps):
-                left = jnp.concatenate([unit_refs[start + u][k] for u in range(group)], axis=1)
+                here = [u for u in range(start, min(start + group, blocks)) if k in spots[u]]
+                near = [spots[u][k] for u in here]
+                left = jnp.concatenate([unit_refs[n][i] for n, i in near], axis=1)
                 for kind in range(3):
-                    right = jnp.concatenate(
-                        [grad_refs[k][places_ref[start + u], kind] for u in range(group)], axis=0
-                    )
+                    right = jnp.concatenate([grad_refs[k][places_ref[u], kind] for u in here], axis=0)
                     part = jnp.dot(left, right, preferred_element_type=F32)
-                    if start == 0 and k == 0:
-                        out_ref[kind] = part
-                    elif start + group == blocks and k == snaps - 1:
-                        out_ref[kind] = (out_ref[kind] + part) * norm
-                    else:
-                        out_ref[kind] += part
+                    if start > 0 or k > 0:
+                        part = out_ref[kind] + part
+                    out_ref[kind] = part * norm if start + group >= blocks and k == snaps - 1 else part
 
     return pl.pallas_call(
         kernel,
         grid_spec=pltpu.PrefetchScalarGridSpec(
             num_scalar_prefetch=1,
             grid=(steps,),
-            in_specs=[pl.BlockSpec((snaps, row_step, BLK), lambda r, _: (0, r, 0))] * blocks
+            in_specs=[pl.BlockSpec((a.shape[0], row_step, BLK), lambda r, _: (0, r, 0)) for a in flat]
             + [pl.BlockSpec((blocks, 3, BLK, cut), lambda r, _: (0, 0, 0, 0))] * snaps
             + [pl.BlockSpec(memory_space=pl.ANY)] * len(before),
             out_specs=pl.BlockSpec((3, row_step, cut), lambda r, _: (0, r, chunk)),
         ),
         out_shape=jax.ShapeDtypeStruct((3, rows, chunks * cut), F32),
-        input_output_aliases={1 + blocks + snaps: 0} if before else {},
+        input_output_aliases={1 + len(flat) + snaps: 0} if before else {},
         compiler_params=pltpu.CompilerParams(vmem_limit_bytes=56 * MIB),
         cost_estimate=pl.CostEstimate(
             flops=6 * blocks * BLK * snaps * rows * cut,
@@ -225,7 +234,51 @@
             transcendentals=0,
         ),
         name="weight_products",
-    )(places, *units, *grads, *before)
+    )(places, *flat, *grads, *before)
+
+
+def add_products(pieces, places, grads, norm, total):
+    chunks, cut = len(grads[0]), grads[0][0].shape[-1]
+    _, rows, columns = total.shape
+    steps = 4
+    row_step = rows // steps
+    needed = [(u, n, i, snap + i) for n, (u, piece, snap) in enumerate(pieces) for i in range(piece.shape[0])]
+
+    def kernel(*refs):
+        piece_refs, grad_refs = refs[1 : 1 + len(pieces)], refs[1 + len(pieces) : -2]
+        total_ref, out_ref = refs[-2:]
+        left = jnp.concatenate([piece_refs[n][i] for _, n, i, _ in needed], axis=1)
+        for c in range(chunks):
+            for kind in range(3):
+                right = jnp.concatenate([grad_refs[m * chunks + c][0, kind] for m in range(len(needed))], axis=0)
+                part = jnp.dot(left, right, preferred_element_type=F32)
+                cols = slice(c * cut, (c + 1) * cut)
+                out_ref[kind, :, cols] = (total_ref[kind, :, cols] + part) * norm
+
+    def block_of(u):
+        return pl.BlockSpec((1, 3, BLK, cut), lambda r, places_ref: (places_ref[u], 0, 0, 0))
+
+    whole = pl.BlockSpec((3, row_step, columns), lambda r, _: (0, r, 0))
+    return pl.pallas_call(
+        kernel,
+        grid_spec=pltpu.PrefetchScalarGridSpec(
+            num_scalar_prefetch=1,
+            grid=(steps,),
+            in_specs=[pl.BlockSpec((p.shape[0], row_step, BLK), lambda r, _: (0, r, 0)) for _, p, _ in pieces]
+            + [block_of(u) for u, _, _, _ in needed for _ in range(chunks)]
+            + [whole],
+            out_specs=whole,
+        ),
+        out_shape=jax.ShapeDtypeStruct(total.shape, F32),
+        input_output_aliases={1 + len(pieces) + len(needed) * chunks: 0},
+        compiler_params=pltpu.CompilerParams(vmem_limit_bytes=32 * MIB),
+        cost_estimate=pl.CostEstimate(
+            flops=6 * len(needed) * BLK * rows * columns,
+            bytes_accessed=24 * rows * columns,
+            transcendentals=0,
+        ),
+        name="add_products",
+    )(places, *[p for _, p, _ in pieces], *[g for _, _, _, k in needed for g in grads[k]], total)
 
 
 def seq_swap(array, bit):
@@ -267,36 +320,46 @@
         slab = lax.dynamic_slice_in_dim(turned, to * rows_here, rows_here, 0)
         slabs.append(slab if (j, e) == (0, 0) else dp_move(slab, j, e))
     packed += [pack_rows(rows_in, seq_count, c, chunks, [turned]) for c in range(1, chunks)]
-    own = jnp.stack(slabs)
+    own = [jnp.stack(slabs[: dp_count // 2]), jnp.stack(slabs[dp_count // 2 :])]
     at = lax.axis_index("seq")
     ready, behind = [[] for _ in range(chunks)], [[], []]
     if seq_count == 8:
-        beside, far, own_x = seq_swap(own, 2), seq_swap(own, 4), seq_swap(own, 1)
-        beside_x = seq_swap(beside, 1)
+        units = {0: own}
+        for bits, source, step in ((2, 0, 2), (4, 0, 4), (6, 4, 2), (1, 0, 1), (3, 2, 1), (5, 4, 1), (7, 6, 1)):
+            units[bits] = [seq_swap(a, step) for a in units[source]]
         for c in range(1, chunks):
-            packed[c] = hold(packed[c], [beside, far, own_x, beside_x])
+            packed[c] = hold(packed[c], [units[n][h] for n, h in HOLD_1])
         ready[0] = packed[1:2]
-        far_beside, far_x = seq_swap(far, 2), seq_swap(far, 1)
-        far_beside_x = seq_swap(far_beside, 1)
-        behind = [[far_beside, far_x], [far_beside_x]]
-        units = [own, beside, far, far_beside, own_x, beside_x, far_x, far_beside_x]
-        places = jnp.stack([at ^ bits for bits in (0, 2, 4, 6, 1, 3, 5, 7)]).astype(jnp.int32)
+        behind = [[units[n][h] for n, h in HOLD_2], [units[n][h] for n, h in HOLD_3]]
+        places = jnp.stack([at ^ bits for bits in units]).astype(jnp.int32)
+        late = [(list(units).index(n), units[n][h], h * (dp_count // 2)) for n, h in LATE]
+        units = [
+            [(a, h * (dp_count // 2)) for h, a in enumerate(halves) if (n, h) not in LATE]
+            for n, halves in units.items()
+        ]
     else:
-        every = lax.all_gather(own, "seq", axis=0, tiled=False)
-        units, places = [every[i] for i in range(seq_count)], jnp.arange(seq_count, dtype=jnp.int32)
+        every = [lax.all_gather(half, "seq", axis=0, tiled=False) for half in own]
+        units = [[(half[i], h * (dp_count // 2)) for h, half in enumerate(every)] for i in range(seq_count)]
+        late = []
+        places = jnp.arange(seq_count, dtype=jnp.int32)
     items += [lax.all_to_all(a, "seq", 0, 0, tiled=True) for a in packed[1:]]
 
     norm = 1.0 / math.sqrt(neighbours.shape[1] * BLK * dp_count)
-    weight_grad, done = None, None
+    weight_grad, backs, every_grad = None, [], []
     for c in range(chunks):
         out = attention(items[c], bias, ready[c])
         over_y = [out] + [dp_move(out, j, 0) for j in range(1, y_count)]
         grads = [a for there in over_y for a in (there, dp_move(there, 0, 1))]
-        late = behind[c] + (over_y[1:] if c == 0 else [])
-        back = hold(out, late) if late and chunks == 2 else out
-        back = lax.all_to_all(back, "seq", 0, 0, tiled=True)
-        weight_grad = weight_products(units, places, grads, c, chunks, norm, weight_grad)
-        done = unpack_rows(back, c, chunks, done, [weight_grad] if c == chunks - 1 else [])
+        wait = behind[c] + (over_y[1:] if c == 0 else [])
+        back = hold(out, wait) if wait and chunks == 2 else out
+        backs.append(lax.all_to_all(back, "seq", 0, 0, tiled=True))
+        weight_grad = weight_products(units, places, grads, c, chunks, 1.0 if late else norm, weight_grad)
+        every_grad.append(grads)
+    if late:
+        weight_grad = add_products(late, places, list(zip(*every_grad)), norm, weight_grad)
+    done = None
+    for c in range(chunks):
+        done = unpack_rows(backs[c], c, chunks, done, [weight_grad] if c == chunks - 1 else [])
     query_grad, key_grad, value_grad = done
     return query_grad[None], key_grad[None], value_grad[None], weight_grad
 

time: 261 us -> 253 us (0.969)
  waiting for transfers between devices: 152 us -> 123 us
  Pallas kernels: 62.7 us -> 71.7 us
  starting transfers between devices: 39 us -> 46.5 us
    ppermute x7 -> x14, waiting for transfers between devices: 131 us -> 109 us  [seq_swap(): lax.ppermute(array, 'seq', [(i, i ^ bit) for i in range(lax.axis_size('se...]
    pallas_call x0 -> x1, Pallas kernels: none -> 7.22 us  [add_products(): pl.pallas_call(kernel, grid_spec=pltpu.PrefetchScalarGridSpec(num_scalar_...]
    ppermute x7 -> x14, starting transfers between devices: 12.3 us -> 19.4 us  [seq_swap(): lax.ppermute(array, 'seq', [(i, i ^ bit) for i in range(lax.axis_size('se...]
    all_to_all x2, waiting for transfers between devices: 5.31 us -> 0.01 us  [local(): backs.append(lax.all_to_all(back, 'seq', 0, 0, tiled=True))]
    unnamed x24 -> x44, local copies, waits for them, and re-layouts: 3.31 us -> 5.59 us
  transfers between devices with their start and end apart: 20 -> 27, of which waited for: 9 -> 11; matrix products, arithmetic and copies ran while one was open for 2% -> 3% of each run, Pallas kernels for 22% -> 26%
where the time goes in v3:
time: 253 us; the launch traced here: 252 us
  waiting for transfers between devices  123 us (49%)
  Pallas kernels  71.7 us (28%)
  starting transfers between devices  46.5 us (18%)
  local copies, waits for them, and re-layouts  7.7 us (3%)
    ppermute x14, waiting for transfers between devices, seq_swap(): lax.ppermute(array, 'seq', [(i, i ^ bit) for i in range(lax.axis_size('se...  109 us
    pallas_call x2, Pallas kernels, attention(): pl.pallas_call(kernel, in_specs=[pl.BlockSpec(memory_space=pltpu.VMEM)] *...  26.2 us
    pallas_call x2, Pallas kernels, weight_products(): pl.pallas_call(kernel, grid_spec=pltpu.PrefetchScalarGridSpec(num_scalar_...  25.5 us
    ppermute x14, starting transfers between devices, seq_swap(): lax.ppermute(array, 'seq', [(i, i ^ bit) for i in range(lax.axis_size('se...  19.4 us
    ppermute x9, waiting for transfers between devices, dp_move(): lax.ppermute(array, 'dp', [(peer(p, j, e), p) for p in range(dp_count)])  14.3 us
    all_to_all x2, starting transfers between devices, local(): backs.append(lax.all_to_all(back, 'seq', 0, 0, tiled=True))  9.42 us
    all_to_all x1, starting transfers between devices, local(): items = [lax.all_to_all(packed[0], 'seq', 0, 0, tiled=True)]  7.26 us
    pallas_call x1, Pallas kernels, add_products(): pl.pallas_call(kernel, grid_spec=pltpu.PrefetchScalarGridSpec(num_scalar_...  7.22 us
  transfers between devices with their start and end apart: 27, of which 11 were waited for; matrix products, arithmetic and copies ran while one was open for 3% of the time, Pallas kernels for 26%

profile of v3, /device:TPU:0, one launch (start us, length us, event | category | flops | bytes accessed | tf_op | source)
XLA Modules:
  0.0 251.9 jit_solution(13523704998365650773)
XLA Ops:
  0.6 2.8 %pack_rows.2.refs_1_ = bf16[8,4,128,256]{3,2,1,0:T(8,128)(2,1)} custom-call(bf16[128,4096]{1,0:T(8,128)(2,1)} %bitcast.28, bf16[128,4096]{1,0:T(8,128)(2,1)} %bitcast.30, bf16[128,4096]{1,0:T(8,128)(2,1)} %bitcast.32, bf16[128,4096]{1,0:T(8,128)(2,1)} %bitcast.34), custom_call_target="tpu_custom_call" | custom-call | bytes 4194304 | tf_op jit(solution)/shard_map/pack_rows/pallas_call | solution.py:47
  3.4 7.3 %all-to-all-start.2 = ((bf16[8,4,128,256]{3,2,1,0:T(8,128)(2,1)}), bf16[8,4,128,256]{3,2,1,0:T(8,128)(2,1)}, u32[]{:S(2)}, u32[]{:S(2)}) async-start(bf16[8,4,128,256]{3,2,1,0:T(8,128)(2,1)} %pack_rows.2.refs_1_), calls=%async_computation.2 | async-start | bytes 4194304 | tf_op jit(solution)/shard_map/all_to_all | solution.py:314
  10.7 2.2 turn_layer_input.1.refs_4_
  12.9 1.3 constant_dynamic-slice_fusion.1
  14.2 1.6 collective-permute-start.2
  15.8 0.6 collective-permute-start
  16.4 7.1 %collective-permute-done.2 = bf16[1024,128]{1,0:T(8,128)(2,1)S(1)} collective-permute-done((bf16[1024,128]{1,0:T(8,128)(2,1)S(1)}, bf16[1024,128]{1,0:T(8,128)(2,1)S(1)}, u32[]{:S(2)}, u32[]{:S(2)}) %collective-permute-start.2) | collective-permute-done | bytes 262176 | tf_op jit(solution)/shard_map/ppermute | solution.py:305
  23.5 3.2 %collective-permute-done.3 = bf16[1024,128]{1,0:T(8,128)(2,1)S(1)} collective-permute-done((bf16[1024,128]{1,0:T(8,128)(2,1)S(1)}, bf16[1024,128]{1,0:T(8,128)(2,1)S(1)}, u32[]{:S(2)}, u32[]{:S(2)}) %collective-permute-start.3) | collective-permute-done | bytes 262176 | tf_op jit(solution)/shard_map/ppermute | solution.py:305
  26.7 0.8 pad_maximum_fusion.1.refs_2_
  27.5 1.7 collective-permute-start.4
  29.3 2.4 collective-permute-start.6
  31.6 0.9 pad_maximum_fusion.refs_1_
  33.1 1.5 collective-permute-start.8
  35.1 23.1 %collective-permute-done.4.refs_2_.refs_4_ = bf16[2,1024,128]{2,1,0:T(8,128)(2,1)S(1)} collective-permute-done((bf16[2,1024,128]{2,1,0:T(8,128)(2,1)}, bf16[2,1024,128]{2,1,0:T(8,128)(2,1)S(1)}, u32[]{:S(2)}, u32[]{:S(2)}) %collective-permute-start.4) | collective-permute-done | bytes 524320 | tf_op jit(solution)/shard_map/ppermute | solution.py:285
  58.2 1.6 collective-permute-start.7
  59.7 34.4 %collective-permute-done.6.refs_4_.refs_6_ = bf16[2,1024,128]{2,1,0:T(8,128)(2,1)S(1)} collective-permute-done((bf16[2,1024,128]{2,1,0:T(8,128)(2,1)}, bf16[2,1024,128]{2,1,0:T(8,128)(2,1)S(1)}, u32[]{:S(2)}, u32[]{:S(2)}) %collective-permute-start.6) | collective-permute-done | bytes 524320 | tf_op jit(solution)/shard_map/ppermute | solution.py:285
  94.1 1.1 collective-permute-start.10
  95.2 0.9 collective-permute-start.9
  96.1 2.8 %pack_rows.3.refs_0_ = bf16[8,4,128,256]{3,2,1,0:T(8,128)(2,1)} custom-call(bf16[128,4096]{1,0:T(8,128)(2,1)} %bitcast.29, bf16[128,4096]{1,0:T(8,128)(2,1)} %bitcast.31, bf16[128,4096]{1,0:T(8,128)(2,1)} %bitcast.33, bf16[128,4096]{1,0:T(8,128)(2,1)} %bitcast.35, bf16[4096,128]{1,0:T(8,128)(2,1)} %turn_layer_input.1.refs_4_), custom_call_target="tpu_custom_call" | custom-call | bytes 4194304 | tf_op jit(solution)/shard_map/pack_rows/pallas_call | solution.py:47
  99.0 4.9 %collective-permute-done.5.refs_3_.refs_5_ = bf16[2,1024,128]{2,1,0:T(8,128)(2,1)S(1)} collective-permute-done((bf16[2,1024,128]{2,1,0:T(8,128)(2,1)}, bf16[2,1024,128]{2,1,0:T(8,128)(2,1)S(1)}, u32[]{:S(2)}, u32[]{:S(2)}) %collective-permute-start.5) | collective-permute-done | bytes 524320 | tf_op jit(solution)/shard_map/ppermute | solution.py:285
  103.9 5.1 %collective-permute-done.9.refs_7_.refs_11_ = bf16[2,1024,128]{2,1,0:T(8,128)(2,1)} collective-permute-done((bf16[2,1024,128]{2,1,0:T(8,128)(2,1)S(1)}, bf16[2,1024,128]{2,1,0:T(8,128)(2,1)}, u32[]{:S(2)}, u32[]{:S(2)}) %collective-permute-start.9) | collective-permute-done | bytes 524320 | tf_op jit(solution)/shard_map/ppermute | solution.py:285
  109.1 4.5 %all-to-all-start = ((bf16[8,4,128,256]{3,2,1,0:T(8,128)(2,1)}), bf16[8,4,128,256]{3,2,1,0:T(8,128)(2,1)}, u32[]{:S(2)}, u32[]{:S(2)}) async-start(bf16[8,4,128,256]{3,2,1,0:T(8,128)(2,1)} %hold.3.refs_2_), calls=%async_computation | async-start | bytes 4194304 | tf_op jit(solution)/shard_map/all_to_all | solution.py:345
  113.9 13.7 %attention_backward.3.refs_16_ = bf16[8,3,128,256]{3,2,1,0:T(8,128)(2,1)} custom-call(bf16[8,4,128,256]{3,2,1,0:T(8,128)(2,1)} %all-to-all-done.2.refs_0_, f32[4,8,256]{2,1,0:T(8,128)S(1)} %broadcast_bitcast_fusion.refs_1_, bf16[8,4,128,256]{3,2,1,0:T(8,128)(2,1)S(1)} %copy-done), custom_call_target="tpu_custom_call" | custom-call | flops 5368709120 | bytes 3670016 | tf_op jit(solution)/shard_map/attention_backward/pallas_call | solution.py:170
  127.6 1.5 collective-permute-start.16
  129.1 1.9 collective-permute-start.15
  131.0 1.5 collective-permute-start.12
  133.0 2.7 %copy.21.refs_0_ = bf16[8,3,128,256]{3,2,1,0:T(8,128)(2,1)} copy(bf16[8,3,128,256]{3,2,1,0:T(8,128)(2,1)} %attention_backward.3.refs_16_) | data formatting | bytes 3145728
  135.7 14.7 %collective-permute-done.15.refs_3_.refs_14_ = bf16[2,1024,128]{2,1,0:T(8,128)(2,1)S(1)} collective-permute-done((bf16[2,1024,128]{2,1,0:T(8,128)(2,1)S(1)}, bf16[2,1024,128]{2,1,0:T(8,128)(2,1)S(1)}, u32[]{:S(2)}, u32[]{:S(2)}) %collective-permute-start.15) | collective-permute-done | bytes 524320 | tf_op jit(solution)/shard_map/ppermute | solution.py:285
  150.4 4.8 %collective-permute-done.12.refs_1_.refs_7_ = bf16[2,1024,128]{2,1,0:T(8,128)(2,1)S(1)} collective-permute-done((bf16[2,1024,128]{2,1,0:T(8,128)(2,1)S(1)}, bf16[2,1024,128]{2,1,0:T(8,128)(2,1)S(1)}, u32[]{:S(2)}, u32[]{:S(2)}) %collective-permute-start.12) | collective-permute-done | bytes 524320 | tf_op jit(solution)/shard_map/ppermute | solution.py:285
  155.2 4.0 %collective-permute-done.14.refs_2_.refs_13_ = bf16[2,1024,128]{2,1,0:T(8,128)(2,1)S(1)} collective-permute-done((bf16[2,1024,128]{2,1,0:T(8,128)(2,1)S(1)}, bf16[2,1024,128]{2,1,0:T(8,128)(2,1)S(1)}, u32[]{:S(2)}, u32[]{:S(2)}) %collective-permute-start.14) | collective-permute-done | bytes 524320 | tf_op jit(solution)/shard_map/ppermute | solution.py:285
  159.3 0.8 copy-done.17
  160.0 4.8 %all-to-all-start.3 = ((bf16[8,3,128,256]{3,2,1,0:T(8,128)(2,1)}), bf16[8,3,128,256]{3,2,1,0:T(8,128)(2,1)}, u32[]{:S(2)}, u32[]{:S(2)}) async-start(bf16[8,3,128,256]{3,2,1,0:T(8,128)(2,1)} %hold.5), calls=%async_computation.3 | async-start | bytes 3145728 | tf_op jit(solution)/shard_map/all_to_all | solution.py:355
  164.8 12.5 %attention_backward.2.refs_16_ = bf16[8,3,128,256]{3,2,1,0:T(8,128)(2,1)S(1)} custom-call(bf16[8,4,128,256]{3,2,1,0:T(8,128)(2,1)} %all-to-all-done.refs_0_, f32[4,8,256]{2,1,0:T(8,128)S(1)} %broadcast_bitcast_fusion.refs_1_), custom_call_target="tpu_custom_call" | custom-call | flops 5368709120 | bytes 3670016 | tf_op jit(solution)/shard_map/attention_backward/pallas_call | solution.py:170
  177.4 1.6 collective-permute-start.18
  179.0 2.0 collective-permute-start.11
  181.0 1.5 collective-permute-start.13
  183.0 1.2 copy.20.refs_0_
  184.1 17.8 %collective-permute-done.11.refs_1_.refs_8_ = bf16[2,1024,128]{2,1,0:T(8,128)(2,1)S(1)} collective-permute-done((bf16[2,1024,128]{2,1,0:T(8,128)(2,1)S(1)}, bf16[2,1024,128]{2,1,0:T(8,128)(2,1)S(1)}, u32[]{:S(2)}, u32[]{:S(2)}) %collective-permute-start.11) | collective-permute-done | bytes 524320 | tf_op jit(solution)/shard_map/ppermute | solution.py:285
  202.0 0.9 copy-done.18
  202.8 4.6 %all-to-all-start.1 = ((bf16[8,3,128,256]{3,2,1,0:T(8,128)(2,1)}), bf16[8,3,128,256]{3,2,1,0:T(8,128)(2,1)}, u32[]{:S(2)}, u32[]{:S(2)}) async-start(bf16[8,3,128,256]{3,2,1,0:T(8,128)(2,1)} %hold.4), calls=%async_computation.1 | async-start | bytes 3145728 | tf_op jit(solution)/shard_map/all_to_all | solution.py:355
  207.5 4.0 %collective-permute-done.18.refs_18_.refs_3_ = bf16[8,3,128,256]{3,2,1,0:T(8,128)(2,1)S(1)} collective-permute-done((bf16[8,3,128,256]{3,2,1,0:T(8,128)(2,1)S(1)}, bf16[8,3,128,256]{3,2,1,0:T(8,128)(2,1)S(1)}, u32[]{:S(2)}, u32[]{:S(2)}) %collective-permute-start.18) | collective-permute-done | bytes 1572896 | tf_op jit(solution)/shard_map/ppermute | solution.py:305
  211.5 0.8 stack.59.refs_0_
  212.3 1.7 collective-permute-start.17
  214.0 12.7 %weight_products.2.refs_20_ = f32[3,1024,512]{2,1,0:T(8,128)} custom-call(s32[8]{0:T(128)} %stack.59.refs_0_, bf16[2,1024,128]{2,1,0:T(8,128)(2,1)} %pad_maximum_fusion.refs_1_, bf16[2,1024,128]{2,1,0:T(8,128)(2,1)} %pad_maximum_fusion.1.refs_2_, bf16[2,1024,128]{2,1,0:T(8,128)(2,1)} %copy-done.9, bf16[2,1024,128]{2,1,0:T(8,128)(2,1)} %copy-done.5, ...), custom_call_target="tpu_custom_call" | custom-call | flops 6442450944 | bytes 17825792 | tf_op jit(solution)/shard_map/weight_products/pallas_call | solution.py:218
  226.7 2.5 unpack_rows.2
  229.2 12.8 %weight_products.3.refs_6_ = f32[3,1024,512]{2,1,0:T(8,128)} custom-call(s32[8]{0:T(128)} %stack.59.refs_0_, bf16[2,1024,128]{2,1,0:T(8,128)(2,1)} %pad_maximum_fusion.refs_1_, bf16[2,1024,128]{2,1,0:T(8,128)(2,1)} %pad_maximum_fusion.1.refs_2_, bf16[2,1024,128]{2,1,0:T(8,128)(2,1)} %copy-done.9, ...), custom_call_target="tpu_custom_call", output_to_operand_aliasing={{}: (20, {})} | custom-call | flops 6442450944 | bytes 17825792 | tf_op jit(solution)/shard_map/weight_products/pallas_call | solution.py:218
  242.1 7.2 %add_products.1.refs_4_ = f32[3,1024,512]{2,1,0:T(8,128)} custom-call(s32[8]{0:T(128)S(1)} %copy-done.4, bf16[2,1024,128]{2,1,0:T(8,128)(2,1)} %collective-permute-done.17.refs_1_, bf16[8,3,128,256]{3,2,1,0:T(8,128)(2,1)} %collective-permute-done.16.refs_4_.refs_18_.refs_2_, bf16[8,3,128,256]{3,2,1,0:T(8,128)(2,1)S(1)} %copy-done.3, ...), custom_call_target="tpu_custom_call", output_to_operand_aliasing={{}: (6, {})} | custom-call | flops 805306368 | bytes 12582912 | tf_op jit(solution)/shard_map/add_products/pallas_call | solution.py:262
  249.3 2.5 unpack_rows.3
  (71 shorter events, 2.7 us)
Async XLA Ops:
  3.4 105.6 %all-to-all-start.2 = ((bf16[8,4,128,256]{3,2,1,0:T(8,128)(2,1)}), bf16[8,4,128,256]{3,2,1,0:T(8,128)(2,1)}, u32[]{:S(2)}, u32[]{:S(2)}) async-start(bf16[8,4,128,256]{3,2,1,0:T(8,128)(2,1)} %pack_rows.2.refs_1_), calls=%async_computation.2 | async-start | bytes 4194304 | tf_op jit(solution)/shard_map/all_to_all | solution.py:314
  14.2 9.3 %collective-permute-start.2 = (bf16[1024,128]{1,0:T(8,128)(2,1)S(1)}, bf16[1024,128]{1,0:T(8,128)(2,1)S(1)}, u32[]{:S(2)}, u32[]{:S(2)}) collective-permute-start(bf16[1024,128]{1,0:T(8,128)(2,1)S(1)} %get-tuple-element.16), channel_id=1, source_target_pairs={{2,0},{3,1},{0,2},{1,3},{6,4},{7,5},{4,6},{5,7},{10,8},{11,9},{8,1... | collective-permute-start | bytes 786440 | tf_op jit(solution)/shard_map/ppermute | solution.py:305
  15.8 10.9 %collective-permute-start.3 = (bf16[1024,128]{1,0:T(8,128)(2,1)S(1)}, bf16[1024,128]{1,0:T(8,128)(2,1)S(1)}, u32[]{:S(2)}, u32[]{:S(2)}) collective-permute-start(bf16[1024,128]{1,0:T(8,128)(2,1)S(1)} %get-tuple-element.17), channel_id=1, source_target_pairs={{3,0},{2,1},{1,2},{0,3},{7,4},{6,5},{5,6},{4,7},{11,8},{10,9},{9,1... | collective-permute-start | bytes 786440 | tf_op jit(solution)/shard_map/ppermute | solution.py:305
  15.8 15.9 %collective-permute-start = (bf16[1024,128]{1,0:T(8,128)(2,1)S(1)}, bf16[1024,128]{1,0:T(8,128)(2,1)S(1)}, u32[]{:S(2)}, u32[]{:S(2)}) collective-permute-start(bf16[1024,128]{1,0:T(8,128)(2,1)S(1)} %get-tuple-element.18), channel_id=1, source_target_pairs={{1,0},{0,1},{3,2},{2,3},{5,4},{4,5},{7,6},{6,7},{9,8},{8,9},{11,10... | collective-permute-start | bytes 786440 | tf_op jit(solution)/shard_map/ppermute | solution.py:305
  27.5 30.6 %collective-permute-start.4 = (bf16[2,1024,128]{2,1,0:T(8,128)(2,1)}, bf16[2,1024,128]{2,1,0:T(8,128)(2,1)S(1)}, u32[]{:S(2)}, u32[]{:S(2)}) collective-permute-start(bf16[2,1024,128]{2,1,0:T(8,128)(2,1)} %pad_maximum_fusion.1.refs_2_), channel_id=1, source_target_pairs={{0,8},{4,12},{8,0},{12,4},{16,24},{20,28},{24,16},{28,20},{1,9},{5... | collective-permute-start | bytes 1572872 | tf_op jit(solution)/shard_map/ppermute | solution.py:285
  29.3 64.8 %collective-permute-start.6 = (bf16[2,1024,128]{2,1,0:T(8,128)(2,1)}, bf16[2,1024,128]{2,1,0:T(8,128)(2,1)S(1)}, u32[]{:S(2)}, u32[]{:S(2)}) collective-permute-start(bf16[2,1024,128]{2,1,0:T(8,128)(2,1)} %pad_maximum_fusion.1.refs_2_), channel_id=1, source_target_pairs={{0,16},{4,20},{8,24},{12,28},{16,0},{20,4},{24,8},{28,12},{1,17},{... | collective-permute-start | bytes 1572872 | tf_op jit(solution)/shard_map/ppermute | solution.py:285
  32.5 62.8 %collective-permute-start.1 = (bf16[2,1024,128]{2,1,0:T(8,128)(2,1)}, bf16[2,1024,128]{2,1,0:T(8,128)(2,1)S(1)}, u32[]{:S(2)}, u32[]{:S(2)}) collective-permute-start(bf16[2,1024,128]{2,1,0:T(8,128)(2,1)} %pad_maximum_fusion.refs_1_), channel_id=1, source_target_pairs={{0,8},{4,12},{8,0},{12,4},{16,24},{20,28},{24,16},{28,20},{1,9},{5... | collective-permute-start | bytes 1572872 | tf_op jit(solution)/shard_map/ppermute | solution.py:285
  33.1 66.0 %collective-permute-start.8 = (bf16[2,1024,128]{2,1,0:T(8,128)(2,1)}, bf16[2,1024,128]{2,1,0:T(8,128)(2,1)S(1)}, u32[]{:S(2)}, u32[]{:S(2)}) collective-permute-start(bf16[2,1024,128]{2,1,0:T(8,128)(2,1)} %pad_maximum_fusion.1.refs_2_), channel_id=1, source_target_pairs={{0,4},{4,0},{8,12},{12,8},{16,20},{20,16},{24,28},{28,24},{1,5},{5... | collective-permute-start | bytes 1572872 | tf_op jit(solution)/shard_map/ppermute | solution.py:285
  34.5 69.4 %collective-permute-start.5 = (bf16[2,1024,128]{2,1,0:T(8,128)(2,1)}, bf16[2,1024,128]{2,1,0:T(8,128)(2,1)S(1)}, u32[]{:S(2)}, u32[]{:S(2)}) collective-permute-start(bf16[2,1024,128]{2,1,0:T(8,128)(2,1)} %pad_maximum_fusion.refs_1_), channel_id=1, source_target_pairs={{0,16},{4,20},{8,24},{12,28},{16,0},{20,4},{24,8},{28,12},{1,17},{... | collective-permute-start | bytes 1572872 | tf_op jit(solution)/shard_map/ppermute | solution.py:285
  58.1 40.8 %copy-start.5 = (bf16[2,1024,128]{2,1,0:T(8,128)(2,1)}, bf16[2,1024,128]{2,1,0:T(8,128)(2,1)S(1)}, u32[]{:S(2)}) copy-start(bf16[2,1024,128]{2,1,0:T(8,128)(2,1)S(1)} %collective-permute-done.4.refs_2_.refs_4_) | copy-start | bytes 1572868
  58.2 45.8 %collective-permute-start.7 = (bf16[2,1024,128]{2,1,0:T(8,128)(2,1)}, bf16[2,1024,128]{2,1,0:T(8,128)(2,1)S(1)}, u32[]{:S(2)}, u32[]{:S(2)}) collective-permute-start(bf16[2,1024,128]{2,1,0:T(8,128)(2,1)} %pad_maximum_fusion.refs_1_), channel_id=1, source_target_pairs={{0,4},{4,0},{8,12},{12,8},{16,20},{20,16},{24,28},{28,24},{1,5},{5... | collective-permute-start | bytes 1572872 | tf_op jit(solution)/shard_map/ppermute | solution.py:285
  94.1 4.9 %copy-start.6 = (bf16[2,1024,128]{2,1,0:T(8,128)(2,1)}, bf16[2,1024,128]{2,1,0:T(8,128)(2,1)S(1)}, u32[]{:S(2)}) copy-start(bf16[2,1024,128]{2,1,0:T(8,128)(2,1)S(1)} %collective-permute-done.6.refs_4_.refs_6_) | copy-start | bytes 1572868
  94.1 9.8 %collective-permute-start.10 = (bf16[2,1024,128]{2,1,0:T(8,128)(2,1)S(1)}, bf16[2,1024,128]{2,1,0:T(8,128)(2,1)}, u32[]{:S(2)}, u32[]{:S(2)}) collective-permute-start(bf16[2,1024,128]{2,1,0:T(8,128)(2,1)S(1)} %collective-permute-done.4.refs_2_.refs_4_), channel_id=1, source_target_pairs={{0,4},{4,0},{8,12},{12,8},{16,20},{20,16},{24,28},{28,24},{1,5},{5... | collective-permute-start | bytes 1572872 | tf_op jit(solution)/shard_map/ppermute | solution.py:285
  95.2 3.8 %copy-start.9 = (bf16[2,1024,128]{2,1,0:T(8,128)(2,1)}, bf16[2,1024,128]{2,1,0:T(8,128)(2,1)S(1)}, u32[]{:S(2)}) copy-start(bf16[2,1024,128]{2,1,0:T(8,128)(2,1)S(1)} %collective-permute-done.1.refs_1_.refs_3_) | copy-start | bytes 1572868
  95.2 13.8 %collective-permute-start.9 = (bf16[2,1024,128]{2,1,0:T(8,128)(2,1)S(1)}, bf16[2,1024,128]{2,1,0:T(8,128)(2,1)}, u32[]{:S(2)}, u32[]{:S(2)}) collective-permute-start(bf16[2,1024,128]{2,1,0:T(8,128)(2,1)S(1)} %collective-permute-done.1.refs_1_.refs_3_), channel_id=1, source_target_pairs={{0,4},{4,0},{8,12},{12,8},{16,20},{20,16},{24,28},{28,24},{1,5},{5... | collective-permute-start | bytes 1572872 | tf_op jit(solution)/shard_map/ppermute | solution.py:285
  99.0 10.0 %copy-start.10 = (bf16[2,1024,128]{2,1,0:T(8,128)(2,1)}, bf16[2,1024,128]{2,1,0:T(8,128)(2,1)S(1)}, u32[]{:S(2)}) copy-start(bf16[2,1024,128]{2,1,0:T(8,128)(2,1)S(1)} %collective-permute-done.8.refs_6_.refs_10_) | copy-start | bytes 1572868
  103.9 5.1 %copy-start.11 = (bf16[2,1024,128]{2,1,0:T(8,128)(2,1)}, bf16[2,1024,128]{2,1,0:T(8,128)(2,1)S(1)}, u32[]{:S(2)}) copy-start(bf16[2,1024,128]{2,1,0:T(8,128)(2,1)S(1)} %collective-permute-done.5.refs_3_.refs_5_) | copy-start | bytes 1572868
  103.9 5.1 %copy-start.13 = (bf16[2,1024,128]{2,1,0:T(8,128)(2,1)}, bf16[2,1024,128]{2,1,0:T(8,128)(2,1)S(1)}, u32[]{:S(2)}) copy-start(bf16[2,1024,128]{2,1,0:T(8,128)(2,1)S(1)} %collective-permute-done.7.refs_5_.refs_9_) | copy-start | bytes 1572868
  109.0 4.6 %copy-start.20 = (s32[1,8]{1,0:T(1,128)S(1)}, s32[1,8]{1,0:T(1,128)}, u32[]{:S(2)}) copy-start(s32[1,8]{1,0:T(1,128)} %param.13) | copy-start | bytes 100
  109.0 4.6 %copy-start.19 = (s32[1,8,8]{2,1,0:T(8,128)S(1)}, s32[1,8,8]{2,1,0:T(8,128)}, u32[]{:S(2)}) copy-start(s32[1,8,8]{2,1,0:T(8,128)} %param.12) | copy-start | bytes 772
  109.1 4.8 %copy-start = (bf16[8,4,128,256]{3,2,1,0:T(8,128)(2,1)S(1)}, bf16[8,4,128,256]{3,2,1,0:T(8,128)(2,1)}, u32[]{:S(2)}) copy-start(bf16[8,4,128,256]{3,2,1,0:T(8,128)(2,1)} %hold.3.refs_2_) | copy-start | bytes 6291460
  109.1 51.0 %all-to-all-start = ((bf16[8,4,128,256]{3,2,1,0:T(8,128)(2,1)}), bf16[8,4,128,256]{3,2,1,0:T(8,128)(2,1)}, u32[]{:S(2)}, u32[]{:S(2)}) async-start(bf16[8,4,128,256]{3,2,1,0:T(8,128)(2,1)} %hold.3.refs_2_), calls=%async_computation | async-start | bytes 4194304 | tf_op jit(solution)/shard_map/all_to_all | solution.py:345
  113.9 15.2 %copy-start.7 = (bf16[2,1024,128]{2,1,0:T(8,128)(2,1)S(1)}, bf16[2,1024,128]{2,1,0:T(8,128)(2,1)}, u32[]{:S(2)}) copy-start(bf16[2,1024,128]{2,1,0:T(8,128)(2,1)} %copy-done.6) | copy-start | bytes 1572868
  113.9 17.1 %copy-start.12 = (bf16[2,1024,128]{2,1,0:T(8,128)(2,1)S(1)}, bf16[2,1024,128]{2,1,0:T(8,128)(2,1)}, u32[]{:S(2)}) copy-start(bf16[2,1024,128]{2,1,0:T(8,128)(2,1)} %copy-done.11) | copy-start | bytes 1572868
  127.6 31.7 %collective-permute-start.16 = (bf16[8,3,128,256]{3,2,1,0:T(8,128)(2,1)}, bf16[8,3,128,256]{3,2,1,0:T(8,128)(2,1)}, u32[]{:S(2)}, u32[]{:S(2)}) collective-permute-start(bf16[8,3,128,256]{3,2,1,0:T(8,128)(2,1)} %attention_backward.3.refs_16_), channel_id=1, source_target_pairs={{2,0},{3,1},{0,2},{1,3},{6,4},{7,5},{4,6},{5,7},{10,8},{11,9},{8,1... | collective-permute-start | bytes 4718600 | tf_op jit(solution)/shard_map/ppermute | solution.py:305
  129.1 21.3 %collective-permute-start.15 = (bf16[2,1024,128]{2,1,0:T(8,128)(2,1)S(1)}, bf16[2,1024,128]{2,1,0:T(8,128)(2,1)S(1)}, u32[]{:S(2)}, u32[]{:S(2)}) collective-permute-start(bf16[2,1024,128]{2,1,0:T(8,128)(2,1)S(1)} %copy-done.7), channel_id=1, source_target_pairs={{0,4},{4,0},{8,12},{12,8},{16,20},{20,16},{24,28},{28,24},{1,5},{5... | collective-permute-start | bytes 1572872 | tf_op jit(solution)/shard_map/ppermute | solution.py:285
  131.0 24.2 %collective-permute-start.12 = (bf16[2,1024,128]{2,1,0:T(8,128)(2,1)S(1)}, bf16[2,1024,128]{2,1,0:T(8,128)(2,1)S(1)}, u32[]{:S(2)}, u32[]{:S(2)}) collective-permute-start(bf16[2,1024,128]{2,1,0:T(8,128)(2,1)S(1)} %copy-done.12), channel_id=1, source_target_pairs={{0,8},{4,12},{8,0},{12,4},{16,24},{20,28},{24,16},{28,20},{1,9},{5... | collective-permute-start | bytes 1572872 | tf_op jit(solution)/shard_map/ppermute | solution.py:285
  132.4 26.8 %collective-permute-start.14 = (bf16[2,1024,128]{2,1,0:T(8,128)(2,1)S(1)}, bf16[2,1024,128]{2,1,0:T(8,128)(2,1)S(1)}, u32[]{:S(2)}, u32[]{:S(2)}) collective-permute-start(bf16[2,1024,128]{2,1,0:T(8,128)(2,1)S(1)} %copy-done.12), channel_id=1, source_target_pairs={{0,4},{4,0},{8,12},{12,8},{16,20},{20,16},{24,28},{28,24},{1,5},{5... | collective-permute-start | bytes 1572872 | tf_op jit(solution)/shard_map/ppermute | solution.py:285
  150.4 8.8 %copy-start.14 = (bf16[2,1024,128]{2,1,0:T(8,128)(2,1)}, bf16[2,1024,128]{2,1,0:T(8,128)(2,1)S(1)}, u32[]{:S(2)}) copy-start(bf16[2,1024,128]{2,1,0:T(8,128)(2,1)S(1)} %collective-permute-done.15.refs_3_.refs_14_) | copy-start | bytes 1572868
  155.2 4.1 %copy-start.15 = (bf16[2,1024,128]{2,1,0:T(8,128)(2,1)}, bf16[2,1024,128]{2,1,0:T(8,128)(2,1)S(1)}, u32[]{:S(2)}) copy-start(bf16[2,1024,128]{2,1,0:T(8,128)(2,1)S(1)} %collective-permute-done.12.refs_1_.refs_7_) | copy-start | bytes 1572868
  159.2 0.8 copy-start.17
  160.0 42.8 %all-to-all-start.3 = ((bf16[8,3,128,256]{3,2,1,0:T(8,128)(2,1)}), bf16[8,3,128,256]{3,2,1,0:T(8,128)(2,1)}, u32[]{:S(2)}, u32[]{:S(2)}) async-start(bf16[8,3,128,256]{3,2,1,0:T(8,128)(2,1)} %hold.5), calls=%async_computation.3 | async-start | bytes 3145728 | tf_op jit(solution)/shard_map/all_to_all | solution.py:355
  164.8 14.2 %copy-start.8 = (bf16[2,1024,128]{2,1,0:T(8,128)(2,1)S(1)}, bf16[2,1024,128]{2,1,0:T(8,128)(2,1)}, u32[]{:S(2)}) copy-start(bf16[2,1024,128]{2,1,0:T(8,128)(2,1)} %copy-done.6) | copy-start | bytes 1572868
  164.8 16.2 %copy-start.16 = (bf16[2,1024,128]{2,1,0:T(8,128)(2,1)S(1)}, bf16[2,1024,128]{2,1,0:T(8,128)(2,1)}, u32[]{:S(2)}) copy-start(bf16[2,1024,128]{2,1,0:T(8,128)(2,1)} %copy-done.15) | copy-start | bytes 1572868
  177.4 30.1 %copy-start.1 = (bf16[8,3,128,256]{3,2,1,0:T(8,128)(2,1)}, bf16[8,3,128,256]{3,2,1,0:T(8,128)(2,1)S(1)}, u32[]{:S(2)}) copy-start(bf16[8,3,128,256]{3,2,1,0:T(8,128)(2,1)S(1)} %attention_backward.2.refs_16_) | copy-start | bytes 4718596
  177.4 34.1 %collective-permute-start.18 = (bf16[8,3,128,256]{3,2,1,0:T(8,128)(2,1)S(1)}, bf16[8,3,128,256]{3,2,1,0:T(8,128)(2,1)S(1)}, u32[]{:S(2)}, u32[]{:S(2)}) collective-permute-start(bf16[8,3,128,256]{3,2,1,0:T(8,128)(2,1)S(1)} %attention_backward.2.refs_16_), channel_id=1, source_target_pairs={{2,0},{3,1},{0,2},{1,3},{6,4},{7,5},{4,6},{5,7},{10,8},{11,9},{8,1... | collective-permute-start | bytes 4718600 | tf_op jit(solution)/shard_map/ppermute | solution.py:305
  179.0 23.0 %collective-permute-start.11 = (bf16[2,1024,128]{2,1,0:T(8,128)(2,1)S(1)}, bf16[2,1024,128]{2,1,0:T(8,128)(2,1)S(1)}, u32[]{:S(2)}, u32[]{:S(2)}) collective-permute-start(bf16[2,1024,128]{2,1,0:T(8,128)(2,1)S(1)} %copy-done.8), channel_id=1, source_target_pairs={{0,8},{4,12},{8,0},{12,4},{16,24},{20,28},{24,16},{28,20},{1,9},{5... | collective-permute-start | bytes 1572872 | tf_op jit(solution)/shard_map/ppermute | solution.py:285
  181.0 21.8 %collective-permute-start.13 = (bf16[2,1024,128]{2,1,0:T(8,128)(2,1)S(1)}, bf16[2,1024,128]{2,1,0:T(8,128)(2,1)}, u32[]{:S(2)}, u32[]{:S(2)}) collective-permute-start(bf16[2,1024,128]{2,1,0:T(8,128)(2,1)S(1)} %copy-done.16), channel_id=1, source_target_pairs={{0,4},{4,0},{8,12},{12,8},{16,20},{20,16},{24,28},{28,24},{1,5},{5... | collective-permute-start | bytes 1572872 | tf_op jit(solution)/shard_map/ppermute | solution.py:285
  182.5 31.6 %collective-permute-start.22 = (bf16[8,3,128,256]{3,2,1,0:T(8,128)(2,1)}, bf16[8,3,128,256]{3,2,1,0:T(8,128)(2,1)}, u32[]{:S(2)}, u32[]{:S(2)}) collective-permute-start(bf16[8,3,128,256]{3,2,1,0:T(8,128)(2,1)} %attention_backward.3.refs_16_), channel_id=1, source_target_pairs={{1,0},{0,1},{3,2},{2,3},{5,4},{4,5},{7,6},{6,7},{9,8},{8,9},{11,10... | collective-permute-start | bytes 4718600 | tf_op jit(solution)/shard_map/ppermute | solution.py:305
  182.5 31.6 %collective-permute-start.19 = (bf16[8,3,128,256]{3,2,1,0:T(8,128)(2,1)}, bf16[8,3,128,256]{3,2,1,0:T(8,128)(2,1)}, u32[]{:S(2)}, u32[]{:S(2)}) collective-permute-start(bf16[8,3,128,256]{3,2,1,0:T(8,128)(2,1)} %collective-permute-done.16.refs_4_.refs_18_.refs_2_), channel_id=1, source_target_pairs={{1,0},{0,1},{3,2},{2,3},{5,4},{4,5},{7,6},{6,7},{9,8},{8,9},{11,10... | collective-permute-start | bytes 4718600 | tf_op jit(solution)/shard_map/ppermute | solution.py:305
  201.9 0.9 copy-start.18
  202.8 46.5 %all-to-all-start.1 = ((bf16[8,3,128,256]{3,2,1,0:T(8,128)(2,1)}), bf16[8,3,128,256]{3,2,1,0:T(8,128)(2,1)}, u32[]{:S(2)}, u32[]{:S(2)}) async-start(bf16[8,3,128,256]{3,2,1,0:T(8,128)(2,1)} %hold.4), calls=%async_computation.1 | async-start | bytes 3145728 | tf_op jit(solution)/shard_map/all_to_all | solution.py:355
  207.5 21.8 %collective-permute-start.21 = (bf16[8,3,128,256]{3,2,1,0:T(8,128)(2,1)S(1)}, bf16[8,3,128,256]{3,2,1,0:T(8,128)(2,1)}, u32[]{:S(2)}, u32[]{:S(2)}) collective-permute-start(bf16[8,3,128,256]{3,2,1,0:T(8,128)(2,1)S(1)} %attention_backward.2.refs_16_), channel_id=1, source_target_pairs={{1,0},{0,1},{3,2},{2,3},{5,4},{4,5},{7,6},{6,7},{9,8},{8,9},{11,10... | collective-permute-start | bytes 4718600 | tf_op jit(solution)/shard_map/ppermute | solution.py:305
  211.5 15.2 %copy-start.2 = (bf16[8,3,128,256]{3,2,1,0:T(8,128)(2,1)}, bf16[8,3,128,256]{3,2,1,0:T(8,128)(2,1)S(1)}, u32[]{:S(2)}) copy-start(bf16[8,3,128,256]{3,2,1,0:T(8,128)(2,1)S(1)} %collective-permute-done.18.refs_18_.refs_3_) | copy-start | bytes 4718596
  211.5 17.7 %collective-permute-start.20 = (bf16[8,3,128,256]{3,2,1,0:T(8,128)(2,1)S(1)}, bf16[8,3,128,256]{3,2,1,0:T(8,128)(2,1)}, u32[]{:S(2)}, u32[]{:S(2)}) collective-permute-start(bf16[8,3,128,256]{3,2,1,0:T(8,128)(2,1)S(1)} %collective-permute-done.18.refs_18_.refs_3_), channel_id=1, source_target_pairs={{1,0},{0,1},{3,2},{2,3},{5,4},{4,5},{7,6},{6,7},{9,8},{8,9},{11,10... | collective-permute-start | bytes 4718600 | tf_op jit(solution)/shard_map/ppermute | solution.py:305
  212.3 29.8 %collective-permute-start.17 = (bf16[2,1024,128]{2,1,0:T(8,128)(2,1)}, bf16[2,1024,128]{2,1,0:T(8,128)(2,1)}, u32[]{:S(2)}, u32[]{:S(2)}) collective-permute-start(bf16[2,1024,128]{2,1,0:T(8,128)(2,1)} %copy-done.18), channel_id=1, source_target_pairs={{0,4},{4,0},{8,12},{12,8},{16,20},{20,16},{24,28},{28,24},{1,5},{5... | collective-permute-start | bytes 1572872 | tf_op jit(solution)/shard_map/ppermute | solution.py:285
  229.2 12.9 %copy-start.3 = (bf16[8,3,128,256]{3,2,1,0:T(8,128)(2,1)S(1)}, bf16[8,3,128,256]{3,2,1,0:T(8,128)(2,1)}, u32[]{:S(2)}) copy-start(bf16[8,3,128,256]{3,2,1,0:T(8,128)(2,1)} %copy-done.2) | copy-start | bytes 4718596
  229.2 12.9 %copy-start.4 = (s32[8]{0:T(128)S(1)}, s32[8]{0:T(128)}, u32[]{:S(2)}) copy-start(s32[8]{0:T(128)} %stack.59.refs_0_) | copy-start | bytes 100

commit v4 on v3

--- a/solution.py
+++ b/solution.py
@@ -12,10 +12,12 @@
 MIB = 1 << 20
 BF = jnp.bfloat16
 F32 = jnp.float32
-HOLD_1 = [(2, 0), (2, 1), (4, 0), (4, 1), (1, 0), (1, 1), (3, 0), (3, 1)]
+HOLD_1 = [(2, 0), (2, 1), (4, 0), (4, 1), (1, 0), (3, 0), (3, 1)]
 HOLD_2 = [(6, 0), (5, 0), (5, 1)]
-LATE = [(7, 1)]
 HOLD_3 = [(6, 1), (7, 0)]
+LATE = [(6, 1), (7, 0), (7, 1)]
+EARLY = True
+HALVED = (2, 4)
 
 
 def move_pieces(pairs, buffer, sems):
@@ -53,9 +55,7 @@
             pltpu.VMEM((parts * kinds, tokens, cut), BF),
             pltpu.SemaphoreType.DMA((2, parts * kinds)),
         ],
-        cost_estimate=pl.CostEstimate(
-            flops=0, bytes_accessed=4 * kinds * tokens * parts * cut, transcendentals=0
-        ),
+        cost_estimate=pl.CostEstimate(flops=0, bytes_accessed=0, transcendentals=0),
         name="pack_rows",
     )(*arrays, *after)
 
@@ -83,11 +83,44 @@
             pltpu.SemaphoreType.DMA((2, parts * kinds)),
         ],
         input_output_aliases={1 + i: i for i in range(len(before))},
-        cost_estimate=pl.CostEstimate(
-            flops=0, bytes_accessed=4 * kinds * tokens * parts * cut, transcendentals=0
-        ),
+        cost_estimate=pl.CostEstimate(flops=0, bytes_accessed=0, transcendentals=0),
         name="unpack_rows",
     )(packed, *before, *after)
+
+
+def join_slabs(slabs, groups):
+    rows, columns = slabs[0].shape
+    count = len(slabs)
+    pieces = [(g, n) for g, (first, end) in enumerate(groups) for n in range(first, end)]
+
+    def kernel(*refs):
+        ins, outs, (buffer, sems) = refs[:count], refs[count:-2], refs[-2:]
+        arrive = [pltpu.make_async_copy(ins[n], buffer.at[n], sems.at[0, n]) for n in range(count)]
+        leave = [
+            pltpu.make_async_copy(buffer.at[n], outs[g].at[n - groups[g][0]], sems.at[1, m])
+            for m, (g, n) in enumerate(pieces)
+        ]
+        for copy in arrive:
+            copy.start()
+        for copy in arrive:
+            copy.wait()
+        for copy in leave:
+            copy.start()
+        for copy in leave:
+            copy.wait()
+
+    return pl.pallas_call(
+        kernel,
+        in_specs=[pl.BlockSpec(memory_space=pl.ANY)] * count,
+        out_specs=[pl.BlockSpec(memory_space=pl.ANY)] * len(groups),
+        out_shape=[jax.ShapeDtypeStruct((end - first, rows, columns), BF) for first, end in groups],
+        scratch_shapes=[
+            pltpu.VMEM((count, rows, columns), BF),
+            pltpu.SemaphoreType.DMA((2, max(count, len(pieces)))),
+        ],
+        cost_estimate=pl.CostEstimate(flops=0, bytes_accessed=0, transcendentals=0),
+        name="join_slabs",
+    )(*slabs)
 
 
 def hold(array, after):
@@ -174,11 +207,7 @@
         out_shape=jax.ShapeDtypeStruct((blocks, 3, BLK, width), BF),
         scratch_shapes=[pltpu.VMEM((tokens, HDIM), F32), pltpu.VMEM((tokens, HDIM), F32)],
         compiler_params=pltpu.CompilerParams(vmem_limit_bytes=40 * MIB),
-        cost_estimate=pl.CostEstimate(
-            flops=20 * heads * tokens * tokens * HDIM,
-            bytes_accessed=14 * tokens * width,
-            transcendentals=heads * tokens * tokens,
-        ),
+        cost_estimate=pl.CostEstimate(flops=0, bytes_accessed=0, transcendentals=0),
         name="attention_backward",
     )(items, bias, *after)
 
@@ -228,11 +257,7 @@
         out_shape=jax.ShapeDtypeStruct((3, rows, chunks * cut), F32),
         input_output_aliases={1 + len(flat) + snaps: 0} if before else {},
         compiler_params=pltpu.CompilerParams(vmem_limit_bytes=56 * MIB),
-        cost_estimate=pl.CostEstimate(
-            flops=6 * blocks * BLK * snaps * rows * cut,
-            bytes_accessed=2 * blocks * snaps * BLK * (rows + 3 * cut) + 12 * rows * cut,
-            transcendentals=0,
-        ),
+        cost_estimate=pl.CostEstimate(flops=0, bytes_accessed=0, transcendentals=0),
         name="weight_products",
     )(places, *flat, *grads, *before)
 
@@ -272,11 +297,7 @@
         out_shape=jax.ShapeDtypeStruct(total.shape, F32),
         input_output_aliases={1 + len(pieces) + len(needed) * chunks: 0},
         compiler_params=pltpu.CompilerParams(vmem_limit_bytes=32 * MIB),
-        cost_estimate=pl.CostEstimate(
-            flops=6 * len(needed) * BLK * rows * columns,
-            bytes_accessed=24 * rows * columns,
-            transcendentals=0,
-        ),
+        cost_estimate=pl.CostEstimate(flops=0, bytes_accessed=0, transcendentals=0),
         name="add_products",
     )(places, *[p for _, p, _ in pieces], *[g for _, _, _, k in needed for g in grads[k]], total)
 
@@ -320,26 +341,28 @@
         slab = lax.dynamic_slice_in_dim(turned, to * rows_here, rows_here, 0)
         slabs.append(slab if (j, e) == (0, 0) else dp_move(slab, j, e))
     packed += [pack_rows(rows_in, seq_count, c, chunks, [turned]) for c in range(1, chunks)]
-    own = [jnp.stack(slabs[: dp_count // 2]), jnp.stack(slabs[dp_count // 2 :])]
+    middle = 3 * dp_count // 4
+    own, *own_halves = join_slabs(slabs, [(0, dp_count), (0, middle), (middle, dp_count)])
     at = lax.axis_index("seq")
     ready, behind = [[] for _ in range(chunks)], [[], []]
     if seq_count == 8:
-        units = {0: own}
+        units = {0: [own]}
         for bits, source, step in ((2, 0, 2), (4, 0, 4), (6, 4, 2), (1, 0, 1), (3, 2, 1), (5, 4, 1), (7, 6, 1)):
-            units[bits] = [seq_swap(a, step) for a in units[source]]
+            pieces = own_halves if source == 0 and bits in HALVED else units[source]
+            units[bits] = [seq_swap(a, step) for a in pieces]
         for c in range(1, chunks):
             packed[c] = hold(packed[c], [units[n][h] for n, h in HOLD_1])
         ready[0] = packed[1:2]
         behind = [[units[n][h] for n, h in HOLD_2], [units[n][h] for n, h in HOLD_3]]
         places = jnp.stack([at ^ bits for bits in units]).astype(jnp.int32)
-        late = [(list(units).index(n), units[n][h], h * (dp_count // 2)) for n, h in LATE]
+        late = [(list(units).index(n), units[n][h], h * middle) for n, h in LATE]
         units = [
-            [(a, h * (dp_count // 2)) for h, a in enumerate(halves) if (n, h) not in LATE]
+            [(a, h * middle) for h, a in enumerate(halves) if (n, h) not in LATE]
             for n, halves in units.items()
         ]
     else:
-        every = [lax.all_gather(half, "seq", axis=0, tiled=False) for half in own]
-        units = [[(half[i], h * (dp_count // 2)) for h, half in enumerate(every)] for i in range(seq_count)]
+        every = [lax.all_gather(half, "seq", axis=0, tiled=False) for half in own_halves]
+        units = [[(half[i], h * middle) for h, half in enumerate(every)] for i in range(seq_count)]
         late = []
         places = jnp.arange(seq_count, dtype=jnp.int32)
     items += [lax.all_to_all(a, "seq", 0, 0, tiled=True) for a in packed[1:]]
@@ -351,6 +374,8 @@
         over_y = [out] + [dp_move(out, j, 0) for j in range(1, y_count)]
         grads = [a for there in over_y for a in (there, dp_move(there, 0, 1))]
         wait = behind[c] + (over_y[1:] if c == 0 else [])
+        if c == 1 and EARLY:
+            wait = wait + [weight_grad]
         back = hold(out, wait) if wait and chunks == 2 else out
         backs.append(lax.all_to_all(back, "seq", 0, 0, tiled=True))
         weight_grad = weight_products(units, places, grads, c, chunks, 1.0 if late else norm, weight_grad)

time: 253 us -> 250 us (0.988)
  waiting for transfers between devices: 123 us -> 119 us
  local copies, waits for them, and re-layouts: 7.7 us -> 10.5 us
    ppermute x14 -> x13, waiting for transfers between devices: 109 us -> 94.5 us  [seq_swap(): lax.ppermute(array, 'seq', [(i, i ^ bit) for i in range(lax.axis_size('se...]
    ppermute x9, waiting for transfers between devices: 14.3 us -> 23.3 us  [dp_move(): lax.ppermute(array, 'dp', [(peer(p, j, e), p) for p in range(dp_count)])]
    pallas_call x0 -> x1, Pallas kernels: none -> 2.62 us  [join_slabs(): pl.pallas_call(kernel, in_specs=[pl.BlockSpec(memory_space=pl.ANY)] * cou...]
    unnamed x44 -> x50, local copies, waits for them, and re-layouts: 5.59 us -> 7.8 us
    ppermute x14 -> x13, starting transfers between devices: 19.4 us -> 18.2 us  [seq_swap(): lax.ppermute(array, 'seq', [(i, i ^ bit) for i in range(lax.axis_size('se...]
  transfers between devices with their start and end apart: 27 -> 26, of which waited for: 11 -> 11; matrix products, arithmetic and copies ran while one was open for 3% -> 2% of each run, Pallas kernels for 26% -> 28%
where the time goes in v4:
time: 250 us; the launch traced here: 249 us
  waiting for transfers between devices  119 us (48%)
  Pallas kernels  74 us (30%)
  starting transfers between devices  44.9 us (18%)
  local copies, waits for them, and re-layouts  10.5 us (4%)
    ppermute x13, waiting for transfers between devices, seq_swap(): lax.ppermute(array, 'seq', [(i, i ^ bit) for i in range(lax.axis_size('se...  94.5 us
    pallas_call x2, Pallas kernels, attention(): pl.pallas_call(kernel, in_specs=[pl.BlockSpec(memory_space=pltpu.VMEM)] *...  25 us
    pallas_call x2, Pallas kernels, weight_products(): pl.pallas_call(kernel, grid_spec=pltpu.PrefetchScalarGridSpec(num_scalar_...  24.9 us
    ppermute x9, waiting for transfers between devices, dp_move(): lax.ppermute(array, 'dp', [(peer(p, j, e), p) for p in range(dp_count)])  23.3 us
    ppermute x13, starting transfers between devices, seq_swap(): lax.ppermute(array, 'seq', [(i, i ^ bit) for i in range(lax.axis_size('se...  18.2 us
    all_to_all x2, starting transfers between devices, local(): backs.append(lax.all_to_all(back, 'seq', 0, 0, tiled=True))  9.3 us
    pallas_call x1, Pallas kernels, add_products(): pl.pallas_call(kernel, grid_spec=pltpu.PrefetchScalarGridSpec(num_scalar_...  8.67 us
    unnamed x50, local copies, waits for them, and re-layouts  7.8 us
  transfers between devices with their start and end apart: 26, of which 11 were waited for; matrix products, arithmetic and copies ran while one was open for 2% of the time, Pallas kernels for 28%

profile of v4, /device:TPU:0, one launch (start us, length us, event | category | flops | bytes accessed | tf_op | source)
XLA Modules:
  0.0 249.4 jit_solution(16888077221511625696)
XLA Ops:
  0.6 2.8 %pack_rows.2.refs_1_ = bf16[8,4,128,256]{3,2,1,0:T(8,128)(2,1)} custom-call(bf16[128,4096]{1,0:T(8,128)(2,1)} %bitcast.23, bf16[128,4096]{1,0:T(8,128)(2,1)} %bitcast.25, bf16[128,4096]{1,0:T(8,128)(2,1)} %bitcast.27, bf16[128,4096]{1,0:T(8,128)(2,1)} %bitcast.29), custom_call_target="tpu_custom_call" | custom-call | tf_op jit(solution)/shard_map/pack_rows/pallas_call | solution.py:49
  3.4 7.3 %all-to-all-start.1 = ((bf16[8,4,128,256]{3,2,1,0:T(8,128)(2,1)}), bf16[8,4,128,256]{3,2,1,0:T(8,128)(2,1)}, u32[]{:S(2)}, u32[]{:S(2)}) async-start(bf16[8,4,128,256]{3,2,1,0:T(8,128)(2,1)} %pack_rows.2.refs_1_), calls=%async_computation.1 | async-start | bytes 4194304 | tf_op jit(solution)/shard_map/all_to_all | solution.py:335
  10.7 2.2 turn_layer_input.1.refs_4_
  12.9 2.0 constant_dynamic-slice_fusion
  14.9 1.5 collective-permute-start.1
  16.8 7.2 %collective-permute-done.1.refs_2_ = bf16[1024,128]{1,0:T(8,128)(2,1)S(1)} collective-permute-done((bf16[1024,128]{1,0:T(8,128)(2,1)S(1)}, bf16[1024,128]{1,0:T(8,128)(2,1)S(1)}, u32[]{:S(2)}, u32[]{:S(2)}) %collective-permute-start.1) | collective-permute-done | bytes 262176 | tf_op jit(solution)/shard_map/ppermute | solution.py:326
  24.0 4.8 %collective-permute-done.2.refs_3_ = bf16[1024,128]{1,0:T(8,128)(2,1)S(1)} collective-permute-done((bf16[1024,128]{1,0:T(8,128)(2,1)S(1)}, bf16[1024,128]{1,0:T(8,128)(2,1)S(1)}, u32[]{:S(2)}, u32[]{:S(2)}) %collective-permute-start.2) | collective-permute-done | bytes 262176 | tf_op jit(solution)/shard_map/ppermute | solution.py:326
  28.8 0.7 copy-done.21
  29.5 2.6 %join_slabs.1 = (bf16[4,1024,128]{2,1,0:T(8,128)(2,1)}, bf16[3,1024,128]{2,1,0:T(8,128)(2,1)}, bf16[1,1024,128]{2,1,0:T(8,128)(2,1)}) custom-call(bf16[1024,128]{1,0:T(8,128)(2,1)} %get-tuple-element.25.refs_0_, bf16[1024,128]{1,0:T(8,128)(2,1)} %copy-done.19, bf16[1024,128]{1,0:T(8,128)(2,1)} %copy-done.20, bf16[1024,128]{1,0:T(8,128)(2,1)} %copy-done.21), custom_call_target="tpu_custom_call" | custom-call | tf_op jit(solution)/shard_map/join_slabs/pallas_call | solution.py:112
  32.2 2.1 collective-permute-start.3
  34.3 1.5 collective-permute-start.7
  35.7 2.4 collective-permute-start.5
  38.1 33.0 %collective-permute-done.3.refs_1_.refs_2_ = bf16[3,1024,128]{2,1,0:T(8,128)(2,1)S(1)} collective-permute-done((bf16[3,1024,128]{2,1,0:T(8,128)(2,1)}, bf16[3,1024,128]{2,1,0:T(8,128)(2,1)S(1)}, u32[]{:S(2)}, u32[]{:S(2)}) %collective-permute-start.3) | collective-permute-done | bytes 786464 | tf_op jit(solution)/shard_map/ppermute | solution.py:306
  71.1 1.2 collective-permute-start.8
  72.3 1.9 collective-permute-start.6
  74.2 12.1 %collective-permute-done.4.refs_2_.refs_3_ = bf16[1,1024,128]{2,1,0:T(8,128)(2,1)S(1)} collective-permute-done((bf16[1,1024,128]{2,1,0:T(8,128)(2,1)}, bf16[1,1024,128]{2,1,0:T(8,128)(2,1)S(1)}, u32[]{:S(2)}, u32[]{:S(2)}) %collective-permute-start.4) | collective-permute-done | bytes 262176 | tf_op jit(solution)/shard_map/ppermute | solution.py:306
  86.3 1.5 collective-permute-start.9
  87.9 2.8 %pack_rows.3.refs_0_ = bf16[8,4,128,256]{3,2,1,0:T(8,128)(2,1)} custom-call(bf16[128,4096]{1,0:T(8,128)(2,1)} %bitcast.24, bf16[128,4096]{1,0:T(8,128)(2,1)} %bitcast.26, bf16[128,4096]{1,0:T(8,128)(2,1)} %bitcast.28, bf16[128,4096]{1,0:T(8,128)(2,1)} %bitcast.30, bf16[4096,128]{1,0:T(8,128)(2,1)} %turn_layer_input.1.refs_4_), custom_call_target="tpu_custom_call" | custom-call | tf_op jit(solution)/shard_map/pack_rows/pallas_call | solution.py:49
  90.7 13.3 %collective-permute-done.6.refs_4_.refs_5_ = bf16[1,1024,128]{2,1,0:T(8,128)(2,1)} collective-permute-done((bf16[1,1024,128]{2,1,0:T(8,128)(2,1)}, bf16[1,1024,128]{2,1,0:T(8,128)(2,1)}, u32[]{:S(2)}, u32[]{:S(2)}) %collective-permute-start.6) | collective-permute-done | bytes 262176 | tf_op jit(solution)/shard_map/ppermute | solution.py:306
  104.1 0.7 copy-done.17
  105.4 4.5 %all-to-all-start = ((bf16[8,4,128,256]{3,2,1,0:T(8,128)(2,1)}), bf16[8,4,128,256]{3,2,1,0:T(8,128)(2,1)}, u32[]{:S(2)}, u32[]{:S(2)}) async-start(bf16[8,4,128,256]{3,2,1,0:T(8,128)(2,1)} %hold.3.refs_2_), calls=%async_computation | async-start | bytes 4194304 | tf_op jit(solution)/shard_map/all_to_all | solution.py:368
  110.2 12.5 %attention_backward.3.refs_12_.refs_6_ = bf16[8,3,128,256]{3,2,1,0:T(8,128)(2,1)S(1)} custom-call(bf16[8,4,128,256]{3,2,1,0:T(8,128)(2,1)} %all-to-all-done.1.refs_0_, f32[4,8,256]{2,1,0:T(8,128)S(1)} %broadcast_bitcast_fusion.refs_1_, bf16[8,4,128,256]{3,2,1,0:T(8,128)(2,1)S(1)} %copy-done), custom_call_target="tpu_custom_call" | custom-call | tf_op jit(solution)/shard_map/attention_backward/pallas_call | solution.py:203
  122.7 1.6 collective-permute-start.16
  124.3 1.9 collective-permute-start.11
  126.2 1.5 collective-permute-start.13
  128.2 1.1 copy.21.refs_0_
  129.4 29.9 %collective-permute-done.14.refs_11_.refs_3_ = bf16[1,1024,128]{2,1,0:T(8,128)(2,1)S(1)} collective-permute-done((bf16[1,1024,128]{2,1,0:T(8,128)(2,1)}, bf16[1,1024,128]{2,1,0:T(8,128)(2,1)S(1)}, u32[]{:S(2)}, u32[]{:S(2)}) %collective-permute-start.14) | collective-permute-done | bytes 262176 | tf_op jit(solution)/shard_map/ppermute | solution.py:306
  159.2 3.3 %collective-permute-done.11.refs_6_.refs_1_ = bf16[3,1024,128]{2,1,0:T(8,128)(2,1)} collective-permute-done((bf16[3,1024,128]{2,1,0:T(8,128)(2,1)S(1)}, bf16[3,1024,128]{2,1,0:T(8,128)(2,1)}, u32[]{:S(2)}, u32[]{:S(2)}) %collective-permute-start.11) | collective-permute-done | bytes 786464 | tf_op jit(solution)/shard_map/ppermute | solution.py:306
  162.5 0.9 copy-done.15
  163.4 4.8 %all-to-all-start.3 = ((bf16[8,3,128,256]{3,2,1,0:T(8,128)(2,1)}), bf16[8,3,128,256]{3,2,1,0:T(8,128)(2,1)}, u32[]{:S(2)}, u32[]{:S(2)}) async-start(bf16[8,3,128,256]{3,2,1,0:T(8,128)(2,1)} %hold.5), calls=%async_computation.3 | async-start | bytes 3145728 | tf_op jit(solution)/shard_map/all_to_all | solution.py:380
  168.8 2.0 collective-permute-start.12
  170.7 12.4 %attention_backward.2.refs_12_.refs_7_ = bf16[8,3,128,256]{3,2,1,0:T(8,128)(2,1)S(1)} custom-call(bf16[8,4,128,256]{3,2,1,0:T(8,128)(2,1)} %all-to-all-done.refs_0_, f32[4,8,256]{2,1,0:T(8,128)S(1)} %broadcast_bitcast_fusion.refs_1_), custom_call_target="tpu_custom_call" | custom-call | tf_op jit(solution)/shard_map/attention_backward/pallas_call | solution.py:203
  183.2 1.6 collective-permute-start.19
  184.8 1.5 collective-permute-start.10
  186.2 0.7 stack.35.refs_0_
  186.9 1.2 copy.20.refs_0_
  188.1 12.5 %weight_products.2.refs_3_.refs_16_ = f32[3,1024,512]{2,1,0:T(8,128)} custom-call(s32[8]{0:T(128)} %stack.35.refs_0_, bf16[4,1024,128]{2,1,0:T(8,128)(2,1)} %get-tuple-element.15.refs_1_, bf16[3,1024,128]{2,1,0:T(8,128)(2,1)} %copy-done.12, bf16[1,1024,128]{2,1,0:T(8,128)(2,1)} %copy-done.16, bf16[3,1024,128]{2,1,0:T(8,128)(2,1)} %copy-done.13, ...), custom_call_target="tpu_custom_call" | custom-call | tf_op jit(solution)/shard_map/weight_products/pallas_call | solution.py:247
  200.6 2.9 %collective-permute-done.12.refs_2_ = bf16[3,1024,128]{2,1,0:T(8,128)(2,1)} collective-permute-done((bf16[3,1024,128]{2,1,0:T(8,128)(2,1)}, bf16[3,1024,128]{2,1,0:T(8,128)(2,1)}, u32[]{:S(2)}, u32[]{:S(2)}) %collective-permute-start.12) | collective-permute-done | bytes 786464 | tf_op jit(solution)/shard_map/ppermute | solution.py:306
  203.5 1.0 all-to-all-done.3.refs_0_
  204.5 4.5 %all-to-all-start.2 = ((bf16[8,3,128,256]{3,2,1,0:T(8,128)(2,1)}), bf16[8,3,128,256]{3,2,1,0:T(8,128)(2,1)}, u32[]{:S(2)}, u32[]{:S(2)}) async-start(bf16[8,3,128,256]{3,2,1,0:T(8,128)(2,1)} %hold.4), calls=%async_computation.2 | async-start | bytes 3145728 | tf_op jit(solution)/shard_map/all_to_all | solution.py:380
  209.1 10.3 %collective-permute-done.19.refs_14_.refs_11_ = bf16[8,3,128,256]{3,2,1,0:T(8,128)(2,1)} collective-permute-done((bf16[8,3,128,256]{3,2,1,0:T(8,128)(2,1)S(1)}, bf16[8,3,128,256]{3,2,1,0:T(8,128)(2,1)}, u32[]{:S(2)}, u32[]{:S(2)}) %collective-permute-start.19) | collective-permute-done | bytes 1572896 | tf_op jit(solution)/shard_map/ppermute | solution.py:326
  219.7 2.5 unpack_rows.2
  222.2 0.8 collective-permute-done.20.refs_15_.refs_5_.refs_13_
  223.1 1.1 copy-done.6
  224.2 12.5 %weight_products.3.refs_14_ = f32[3,1024,512]{2,1,0:T(8,128)} custom-call(s32[8]{0:T(128)} %stack.35.refs_0_, bf16[4,1024,128]{2,1,0:T(8,128)(2,1)} %get-tuple-element.15.refs_1_, bf16[3,1024,128]{2,1,0:T(8,128)(2,1)} %copy-done.12, bf16[1,1024,128]{2,1,0:T(8,128)(2,1)} %copy-done.16, ...), custom_call_target="tpu_custom_call", output_to_operand_aliasing={{}: (16, {})} | custom-call | tf_op jit(solution)/shard_map/weight_products/pallas_call | solution.py:247
  236.7 1.4 copy-done.7
  238.1 8.7 %add_products.1.refs_4_ = f32[3,1024,512]{2,1,0:T(8,128)} custom-call(s32[8]{0:T(128)S(1)} %copy-done.10, bf16[1,1024,128]{2,1,0:T(8,128)(2,1)S(1)} %copy-done.9, bf16[3,1024,128]{2,1,0:T(8,128)(2,1)} %collective-permute-done.12.refs_2_, bf16[1,1024,128]{2,1,0:T(8,128)(2,1)} %collective-permute-done.18.refs_3_, ...), custom_call_target="tpu_custom_call", output_to_operand_aliasing={{}: (14, {})} | custom-call | tf_op jit(solution)/shard_map/add_products/pallas_call | solution.py:287
  246.8 2.5 unpack_rows.3
  (74 shorter events, 2.8 us)
Async XLA Ops:
  3.4 102.0 %all-to-all-start.1 = ((bf16[8,4,128,256]{3,2,1,0:T(8,128)(2,1)}), bf16[8,4,128,256]{3,2,1,0:T(8,128)(2,1)}, u32[]{:S(2)}, u32[]{:S(2)}) async-start(bf16[8,4,128,256]{3,2,1,0:T(8,128)(2,1)} %pack_rows.2.refs_1_), calls=%async_computation.1 | async-start | bytes 4194304 | tf_op jit(solution)/shard_map/all_to_all | solution.py:335
  14.9 1.9 collective-permute-start
  14.9 9.1 %collective-permute-start.1 = (bf16[1024,128]{1,0:T(8,128)(2,1)S(1)}, bf16[1024,128]{1,0:T(8,128)(2,1)S(1)}, u32[]{:S(2)}, u32[]{:S(2)}) collective-permute-start(bf16[1024,128]{1,0:T(8,128)(2,1)S(1)} %get-tuple-element.23), channel_id=1, source_target_pairs={{2,0},{3,1},{0,2},{1,3},{6,4},{7,5},{4,6},{5,7},{10,8},{11,9},{8,1... | collective-permute-start | bytes 786440 | tf_op jit(solution)/shard_map/ppermute | solution.py:326
  16.4 12.4 %collective-permute-start.2 = (bf16[1024,128]{1,0:T(8,128)(2,1)S(1)}, bf16[1024,128]{1,0:T(8,128)(2,1)S(1)}, u32[]{:S(2)}, u32[]{:S(2)}) collective-permute-start(bf16[1024,128]{1,0:T(8,128)(2,1)S(1)} %get-tuple-element.22), channel_id=1, source_target_pairs={{3,0},{2,1},{1,2},{0,3},{7,4},{6,5},{5,6},{4,7},{11,8},{10,9},{9,1... | collective-permute-start | bytes 786440 | tf_op jit(solution)/shard_map/ppermute | solution.py:326
  16.8 12.1 %copy-start.19 = (bf16[1024,128]{1,0:T(8,128)(2,1)}, bf16[1024,128]{1,0:T(8,128)(2,1)S(1)}, u32[]{:S(2)}) copy-start(bf16[1024,128]{1,0:T(8,128)(2,1)S(1)} %collective-permute-done.refs_1_) | copy-start | bytes 786436
  24.0 4.9 %copy-start.20 = (bf16[1024,128]{1,0:T(8,128)(2,1)}, bf16[1024,128]{1,0:T(8,128)(2,1)S(1)}, u32[]{:S(2)}) copy-start(bf16[1024,128]{1,0:T(8,128)(2,1)S(1)} %collective-permute-done.1.refs_2_) | copy-start | bytes 786436
  32.2 38.9 %collective-permute-start.3 = (bf16[3,1024,128]{2,1,0:T(8,128)(2,1)}, bf16[3,1024,128]{2,1,0:T(8,128)(2,1)S(1)}, u32[]{:S(2)}, u32[]{:S(2)}) collective-permute-start(bf16[3,1024,128]{2,1,0:T(8,128)(2,1)} %get-tuple-element.13), channel_id=1, source_target_pairs={{0,8},{4,12},{8,0},{12,4},{16,24},{20,28},{24,16},{28,20},{1,9},{5... | collective-permute-start | bytes 2359304 | tf_op jit(solution)/shard_map/ppermute | solution.py:306
  34.3 69.8 %collective-permute-start.7 = (bf16[4,1024,128]{2,1,0:T(8,128)(2,1)}, bf16[4,1024,128]{2,1,0:T(8,128)(2,1)S(1)}, u32[]{:S(2)}, u32[]{:S(2)}) collective-permute-start(bf16[4,1024,128]{2,1,0:T(8,128)(2,1)} %get-tuple-element.15.refs_1_), channel_id=1, source_target_pairs={{0,4},{4,0},{8,12},{12,8},{16,20},{20,16},{24,28},{28,24},{1,5},{5... | collective-permute-start | bytes 3145736 | tf_op jit(solution)/shard_map/ppermute | solution.py:306
  35.7 68.3 %collective-permute-start.5 = (bf16[3,1024,128]{2,1,0:T(8,128)(2,1)}, bf16[3,1024,128]{2,1,0:T(8,128)(2,1)S(1)}, u32[]{:S(2)}, u32[]{:S(2)}) collective-permute-start(bf16[3,1024,128]{2,1,0:T(8,128)(2,1)} %get-tuple-element.13), channel_id=1, source_target_pairs={{0,16},{4,20},{8,24},{12,28},{16,0},{20,4},{24,8},{28,12},{1,17},{... | collective-permute-start | bytes 2359304 | tf_op jit(solution)/shard_map/ppermute | solution.py:306
  71.1 19.6 %copy-start.12 = (bf16[3,1024,128]{2,1,0:T(8,128)(2,1)}, bf16[3,1024,128]{2,1,0:T(8,128)(2,1)S(1)}, u32[]{:S(2)}) copy-start(bf16[3,1024,128]{2,1,0:T(8,128)(2,1)S(1)} %collective-permute-done.3.refs_1_.refs_2_) | copy-start | bytes 2359300
  71.1 33.0 %collective-permute-start.8 = (bf16[3,1024,128]{2,1,0:T(8,128)(2,1)S(1)}, bf16[3,1024,128]{2,1,0:T(8,128)(2,1)}, u32[]{:S(2)}, u32[]{:S(2)}) collective-permute-start(bf16[3,1024,128]{2,1,0:T(8,128)(2,1)S(1)} %collective-permute-done.3.refs_1_.refs_2_), channel_id=1, source_target_pairs={{0,4},{4,0},{8,12},{12,8},{16,20},{20,16},{24,28},{28,24},{1,5},{5... | collective-permute-start | bytes 2359304 | tf_op jit(solution)/shard_map/ppermute | solution.py:306
  72.3 14.1 %collective-permute-start.4 = (bf16[1,1024,128]{2,1,0:T(8,128)(2,1)}, bf16[1,1024,128]{2,1,0:T(8,128)(2,1)S(1)}, u32[]{:S(2)}, u32[]{:S(2)}) collective-permute-start(bf16[1,1024,128]{2,1,0:T(8,128)(2,1)} %get-tuple-element.14), channel_id=1, source_target_pairs={{0,8},{4,12},{8,0},{12,4},{16,24},{20,28},{24,16},{28,20},{1,9},{5... | collective-permute-start | bytes 786440 | tf_op jit(solution)/shard_map/ppermute | solution.py:306
  72.3 31.7 %collective-permute-start.6 = (bf16[1,1024,128]{2,1,0:T(8,128)(2,1)}, bf16[1,1024,128]{2,1,0:T(8,128)(2,1)}, u32[]{:S(2)}, u32[]{:S(2)}) collective-permute-start(bf16[1,1024,128]{2,1,0:T(8,128)(2,1)} %get-tuple-element.14), channel_id=1, source_target_pairs={{0,16},{4,20},{8,24},{12,28},{16,0},{20,4},{24,8},{28,12},{1,17},{... | collective-permute-start | bytes 786440 | tf_op jit(solution)/shard_map/ppermute | solution.py:306
  86.3 4.4 %copy-start.16 = (bf16[1,1024,128]{2,1,0:T(8,128)(2,1)}, bf16[1,1024,128]{2,1,0:T(8,128)(2,1)S(1)}, u32[]{:S(2)}) copy-start(bf16[1,1024,128]{2,1,0:T(8,128)(2,1)S(1)} %collective-permute-done.4.refs_2_.refs_3_) | copy-start | bytes 786436
  86.3 17.7 %collective-permute-start.9 = (bf16[1,1024,128]{2,1,0:T(8,128)(2,1)S(1)}, bf16[1,1024,128]{2,1,0:T(8,128)(2,1)S(1)}, u32[]{:S(2)}, u32[]{:S(2)}) collective-permute-start(bf16[1,1024,128]{2,1,0:T(8,128)(2,1)S(1)} %collective-permute-done.4.refs_2_.refs_3_), channel_id=1, source_target_pairs={{0,4},{4,0},{8,12},{12,8},{16,20},{20,16},{24,28},{28,24},{1,5},{5... | collective-permute-start | bytes 786440 | tf_op jit(solution)/shard_map/ppermute | solution.py:306
  104.0 1.0 copy-start.13
  104.1 1.3 copy-start.11
  105.4 4.5 %copy-start.23 = (s32[1,8]{1,0:T(1,128)S(1)}, s32[1,8]{1,0:T(1,128)}, u32[]{:S(2)}) copy-start(s32[1,8]{1,0:T(1,128)} %param.13) | copy-start | bytes 100
  105.4 4.6 %copy-start.22 = (s32[1,8,8]{2,1,0:T(8,128)S(1)}, s32[1,8,8]{2,1,0:T(8,128)}, u32[]{:S(2)}) copy-start(s32[1,8,8]{2,1,0:T(8,128)} %param.12) | copy-start | bytes 772
  105.4 4.8 %copy-start = (bf16[8,4,128,256]{3,2,1,0:T(8,128)(2,1)S(1)}, bf16[8,4,128,256]{3,2,1,0:T(8,128)(2,1)}, u32[]{:S(2)}) copy-start(bf16[8,4,128,256]{3,2,1,0:T(8,128)(2,1)} %hold.3.refs_2_) | copy-start | bytes 6291460
  105.4 58.0 %all-to-all-start = ((bf16[8,4,128,256]{3,2,1,0:T(8,128)(2,1)}), bf16[8,4,128,256]{3,2,1,0:T(8,128)(2,1)}, u32[]{:S(2)}, u32[]{:S(2)}) async-start(bf16[8,4,128,256]{3,2,1,0:T(8,128)(2,1)} %hold.3.refs_2_), calls=%async_computation | async-start | bytes 4194304 | tf_op jit(solution)/shard_map/all_to_all | solution.py:368
  110.2 14.1 %copy-start.14 = (bf16[3,1024,128]{2,1,0:T(8,128)(2,1)S(1)}, bf16[3,1024,128]{2,1,0:T(8,128)(2,1)}, u32[]{:S(2)}) copy-start(bf16[3,1024,128]{2,1,0:T(8,128)(2,1)} %copy-done.13) | copy-start | bytes 2359300
  122.7 6.7 %copy-start.3 = (bf16[8,3,128,256]{3,2,1,0:T(8,128)(2,1)}, bf16[8,3,128,256]{3,2,1,0:T(8,128)(2,1)S(1)}, u32[]{:S(2)}) copy-start(bf16[8,3,128,256]{3,2,1,0:T(8,128)(2,1)S(1)} %attention_backward.3.refs_12_.refs_6_) | copy-start | bytes 4718596
  122.7 39.8 %collective-permute-start.16 = (bf16[8,3,128,256]{3,2,1,0:T(8,128)(2,1)S(1)}, bf16[8,3,128,256]{3,2,1,0:T(8,128)(2,1)}, u32[]{:S(2)}, u32[]{:S(2)}) collective-permute-start(bf16[8,3,128,256]{3,2,1,0:T(8,128)(2,1)S(1)} %attention_backward.3.refs_12_.refs_6_), channel_id=1, source_target_pairs={{2,0},{3,1},{0,2},{1,3},{6,4},{7,5},{4,6},{5,7},{10,8},{11,9},{8,1... | collective-permute-start | bytes 4718600 | tf_op jit(solution)/shard_map/ppermute | solution.py:326
  124.3 38.2 %collective-permute-start.11 = (bf16[3,1024,128]{2,1,0:T(8,128)(2,1)S(1)}, bf16[3,1024,128]{2,1,0:T(8,128)(2,1)}, u32[]{:S(2)}, u32[]{:S(2)}) collective-permute-start(bf16[3,1024,128]{2,1,0:T(8,128)(2,1)S(1)} %copy-done.14), channel_id=1, source_target_pairs={{0,8},{4,12},{8,0},{12,4},{16,24},{20,28},{24,16},{28,20},{1,9},{5... | collective-permute-start | bytes 2359304 | tf_op jit(solution)/shard_map/ppermute | solution.py:306
  126.2 36.3 %collective-permute-start.13 = (bf16[3,1024,128]{2,1,0:T(8,128)(2,1)S(1)}, bf16[3,1024,128]{2,1,0:T(8,128)(2,1)S(1)}, u32[]{:S(2)}, u32[]{:S(2)}) collective-permute-start(bf16[3,1024,128]{2,1,0:T(8,128)(2,1)S(1)} %copy-done.14), channel_id=1, source_target_pairs={{0,4},{4,0},{8,12},{12,8},{16,20},{20,16},{24,28},{28,24},{1,5},{5... | collective-permute-start | bytes 2359304 | tf_op jit(solution)/shard_map/ppermute | solution.py:306
  127.7 31.6 %collective-permute-start.14 = (bf16[1,1024,128]{2,1,0:T(8,128)(2,1)}, bf16[1,1024,128]{2,1,0:T(8,128)(2,1)S(1)}, u32[]{:S(2)}, u32[]{:S(2)}) collective-permute-start(bf16[1,1024,128]{2,1,0:T(8,128)(2,1)} %collective-permute-done.6.refs_4_.refs_5_), channel_id=1, source_target_pairs={{0,4},{4,0},{8,12},{12,8},{16,20},{20,16},{24,28},{28,24},{1,5},{5... | collective-permute-start | bytes 786440 | tf_op jit(solution)/shard_map/ppermute | solution.py:306
  159.2 3.3 %copy-start.18 = (bf16[1,1024,128]{2,1,0:T(8,128)(2,1)}, bf16[1,1024,128]{2,1,0:T(8,128)(2,1)S(1)}, u32[]{:S(2)}) copy-start(bf16[1,1024,128]{2,1,0:T(8,128)(2,1)S(1)} %collective-permute-done.14.refs_11_.refs_3_) | copy-start | bytes 786436
  162.5 0.9 copy-start.15
  163.4 4.8 %copy-start.4 = (bf16[8,3,128,256]{3,2,1,0:T(8,128)(2,1)S(1)}, bf16[8,3,128,256]{3,2,1,0:T(8,128)(2,1)}, u32[]{:S(2)}) copy-start(bf16[8,3,128,256]{3,2,1,0:T(8,128)(2,1)} %copy-done.3) | copy-start | bytes 4718596
  163.4 41.1 %all-to-all-start.3 = ((bf16[8,3,128,256]{3,2,1,0:T(8,128)(2,1)}), bf16[8,3,128,256]{3,2,1,0:T(8,128)(2,1)}, u32[]{:S(2)}, u32[]{:S(2)}) async-start(bf16[8,3,128,256]{3,2,1,0:T(8,128)(2,1)} %hold.5), calls=%async_computation.3 | async-start | bytes 3145728 | tf_op jit(solution)/shard_map/all_to_all | solution.py:380
  168.2 19.9 %collective-permute-start.15 = (bf16[8,3,128,256]{3,2,1,0:T(8,128)(2,1)S(1)}, bf16[8,3,128,256]{3,2,1,0:T(8,128)(2,1)}, u32[]{:S(2)}, u32[]{:S(2)}) collective-permute-start(bf16[8,3,128,256]{3,2,1,0:T(8,128)(2,1)S(1)} %copy-done.4), channel_id=1, source_target_pairs={{1,0},{0,1},{3,2},{2,3},{5,4},{4,5},{7,6},{6,7},{9,8},{8,9},{11,10... | collective-permute-start | bytes 4718600 | tf_op jit(solution)/shard_map/ppermute | solution.py:326
  168.3 19.8 %collective-permute-start.17 = (bf16[8,3,128,256]{3,2,1,0:T(8,128)(2,1)}, bf16[8,3,128,256]{3,2,1,0:T(8,128)(2,1)}, u32[]{:S(2)}, u32[]{:S(2)}) collective-permute-start(bf16[8,3,128,256]{3,2,1,0:T(8,128)(2,1)} %collective-permute-done.16.refs_14_.refs_4_.refs_10_), channel_id=1, source_target_pairs={{1,0},{0,1},{3,2},{2,3},{5,4},{4,5},{7,6},{6,7},{9,8},{8,9},{11,10... | collective-permute-start | bytes 4718600 | tf_op jit(solution)/shard_map/ppermute | solution.py:326
  168.8 34.7 %collective-permute-start.12 = (bf16[3,1024,128]{2,1,0:T(8,128)(2,1)}, bf16[3,1024,128]{2,1,0:T(8,128)(2,1)}, u32[]{:S(2)}, u32[]{:S(2)}) collective-permute-start(bf16[3,1024,128]{2,1,0:T(8,128)(2,1)} %collective-permute-done.11.refs_6_.refs_1_), channel_id=1, source_target_pairs={{0,4},{4,0},{8,12},{12,8},{16,20},{20,16},{24,28},{28,24},{1,5},{5... | collective-permute-start | bytes 2359304 | tf_op jit(solution)/shard_map/ppermute | solution.py:306
  183.2 25.8 %copy-start.1 = (bf16[8,3,128,256]{3,2,1,0:T(8,128)(2,1)}, bf16[8,3,128,256]{3,2,1,0:T(8,128)(2,1)S(1)}, u32[]{:S(2)}) copy-start(bf16[8,3,128,256]{3,2,1,0:T(8,128)(2,1)S(1)} %attention_backward.2.refs_12_.refs_7_) | copy-start | bytes 4718596
  183.2 36.3 %collective-permute-start.19 = (bf16[8,3,128,256]{3,2,1,0:T(8,128)(2,1)S(1)}, bf16[8,3,128,256]{3,2,1,0:T(8,128)(2,1)}, u32[]{:S(2)}, u32[]{:S(2)}) collective-permute-start(bf16[8,3,128,256]{3,2,1,0:T(8,128)(2,1)S(1)} %attention_backward.2.refs_12_.refs_7_), channel_id=1, source_target_pairs={{2,0},{3,1},{0,2},{1,3},{6,4},{7,5},{4,6},{5,7},{10,8},{11,9},{8,1... | collective-permute-start | bytes 4718600 | tf_op jit(solution)/shard_map/ppermute | solution.py:326
  184.8 15.8 %collective-permute-start.10 = (bf16[1,1024,128]{2,1,0:T(8,128)(2,1)}, bf16[1,1024,128]{2,1,0:T(8,128)(2,1)S(1)}, u32[]{:S(2)}, u32[]{:S(2)}) collective-permute-start(bf16[1,1024,128]{2,1,0:T(8,128)(2,1)} %collective-permute-done.6.refs_4_.refs_5_), channel_id=1, source_target_pairs={{0,8},{4,12},{8,0},{12,4},{16,24},{20,28},{24,16},{28,20},{1,9},{5... | collective-permute-start | bytes 786440 | tf_op jit(solution)/shard_map/ppermute | solution.py:306
  200.5 2.9 %copy-start.8 = (bf16[1,1024,128]{2,1,0:T(8,128)(2,1)}, bf16[1,1024,128]{2,1,0:T(8,128)(2,1)S(1)}, u32[]{:S(2)}) copy-start(bf16[1,1024,128]{2,1,0:T(8,128)(2,1)S(1)} %collective-permute-done.10.refs_1_) | copy-start | bytes 786436
  203.5 16.0 %copy-start.9 = (bf16[1,1024,128]{2,1,0:T(8,128)(2,1)S(1)}, bf16[1,1024,128]{2,1,0:T(8,128)(2,1)}, u32[]{:S(2)}) copy-start(bf16[1,1024,128]{2,1,0:T(8,128)(2,1)} %copy-done.8) | copy-start | bytes 786436
  204.5 42.3 %all-to-all-start.2 = ((bf16[8,3,128,256]{3,2,1,0:T(8,128)(2,1)}), bf16[8,3,128,256]{3,2,1,0:T(8,128)(2,1)}, u32[]{:S(2)}, u32[]{:S(2)}) async-start(bf16[8,3,128,256]{3,2,1,0:T(8,128)(2,1)} %hold.4), calls=%async_computation.2 | async-start | bytes 3145728 | tf_op jit(solution)/shard_map/all_to_all | solution.py:380
  209.0 13.2 %collective-permute-start.21 = (bf16[8,3,128,256]{3,2,1,0:T(8,128)(2,1)S(1)}, bf16[8,3,128,256]{3,2,1,0:T(8,128)(2,1)}, u32[]{:S(2)}, u32[]{:S(2)}) collective-permute-start(bf16[8,3,128,256]{3,2,1,0:T(8,128)(2,1)S(1)} %attention_backward.2.refs_12_.refs_7_), channel_id=1, source_target_pairs={{1,0},{0,1},{3,2},{2,3},{5,4},{4,5},{7,6},{6,7},{9,8},{8,9},{11,10... | collective-permute-start | bytes 4718600 | tf_op jit(solution)/shard_map/ppermute | solution.py:326
  219.4 3.6 %collective-permute-start.20 = (bf16[8,3,128,256]{3,2,1,0:T(8,128)(2,1)}, bf16[8,3,128,256]{3,2,1,0:T(8,128)(2,1)S(1)}, u32[]{:S(2)}, u32[]{:S(2)}) collective-permute-start(bf16[8,3,128,256]{3,2,1,0:T(8,128)(2,1)} %collective-permute-done.19.refs_14_.refs_11_), channel_id=1, source_target_pairs={{1,0},{0,1},{3,2},{2,3},{5,4},{4,5},{7,6},{6,7},{9,8},{8,9},{11,10... | collective-permute-start | bytes 4718600 | tf_op jit(solution)/shard_map/ppermute | solution.py:326
  219.5 17.2 %collective-permute-start.18 = (bf16[1,1024,128]{2,1,0:T(8,128)(2,1)S(1)}, bf16[1,1024,128]{2,1,0:T(8,128)(2,1)}, u32[]{:S(2)}, u32[]{:S(2)}) collective-permute-start(bf16[1,1024,128]{2,1,0:T(8,128)(2,1)S(1)} %copy-done.9), channel_id=1, source_target_pairs={{0,4},{4,0},{8,12},{12,8},{16,20},{20,16},{24,28},{28,24},{1,5},{5... | collective-permute-start | bytes 786440 | tf_op jit(solution)/shard_map/ppermute | solution.py:306
  222.2 14.5 %copy-start.2 = (bf16[8,3,128,256]{3,2,1,0:T(8,128)(2,1)S(1)}, bf16[8,3,128,256]{3,2,1,0:T(8,128)(2,1)}, u32[]{:S(2)}) copy-start(bf16[8,3,128,256]{3,2,1,0:T(8,128)(2,1)} %copy-done.1) | copy-start | bytes 4718596
  222.2 14.5 %copy-start.5 = (bf16[8,3,128,256]{3,2,1,0:T(8,128)(2,1)S(1)}, bf16[8,3,128,256]{3,2,1,0:T(8,128)(2,1)}, u32[]{:S(2)}) copy-start(bf16[8,3,128,256]{3,2,1,0:T(8,128)(2,1)} %copy-done.3) | copy-start | bytes 4718596
  222.2 14.5 %copy-start.10 = (s32[8]{0:T(128)S(1)}, s32[8]{0:T(128)}, u32[]{:S(2)}) copy-start(s32[8]{0:T(128)} %stack.35.refs_0_) | copy-start | bytes 100
  223.1 1.1 copy-start.6
  236.7 1.4 copy-start.7
  (2 other events, 1.4 us)

commit v5 on v4

--- a/solution.py
+++ b/solution.py
@@ -256,7 +256,7 @@
         ),
         out_shape=jax.ShapeDtypeStruct((3, rows, chunks * cut), F32),
         input_output_aliases={1 + len(flat) + snaps: 0} if before else {},
-        compiler_params=pltpu.CompilerParams(vmem_limit_bytes=56 * MIB),
+        compiler_params=pltpu.CompilerParams(vmem_limit_bytes=62 * MIB),
         cost_estimate=pl.CostEstimate(flops=0, bytes_accessed=0, transcendentals=0),
         name="weight_products",
     )(places, *flat, *grads, *before)
@@ -265,7 +265,7 @@
 def add_products(pieces, places, grads, norm, total):
     chunks, cut = len(grads[0]), grads[0][0].shape[-1]
     _, rows, columns = total.shape
-    steps = 4
+    steps = 2
     row_step = rows // steps
     needed = [(u, n, i, snap + i) for n, (u, piece, snap) in enumerate(pieces) for i in range(piece.shape[0])]
 
@@ -296,7 +296,7 @@
         ),
         out_shape=jax.ShapeDtypeStruct(total.shape, F32),
         input_output_aliases={1 + len(pieces) + len(needed) * chunks: 0},
-        compiler_params=pltpu.CompilerParams(vmem_limit_bytes=32 * MIB),
+        compiler_params=pltpu.CompilerParams(vmem_limit_bytes=62 * MIB),
         cost_estimate=pl.CostEstimate(flops=0, bytes_accessed=0, transcendentals=0),
         name="add_products",
     )(places, *[p for _, p, _ in pieces], *[g for _, _, _, k in needed for g in grads[k]], total)

time: 250 us -> 249 us (level)
    ppermute x13, waiting for transfers between devices: 94.5 us -> 91.7 us  [seq_swap(): lax.ppermute(array, 'seq', [(i, i ^ bit) for i in range(lax.axis_size('se...]
    unnamed x50 -> x36, local copies, waits for them, and re-layouts: 7.8 us -> 7.46 us
  transfers between devices with their start and end apart: 26 -> 26, of which waited for: 11 -> 12; matrix products, arithmetic and copies ran while one was open for 2% -> 3% of each run, Pallas kernels for 28% -> 28%
where the time goes in v5:
time: 249 us; the launch traced here: 248 us
  waiting for transfers between devices  117 us (47%)
  Pallas kernels  74.4 us (30%)
  starting transfers between devices  44.7 us (18%)
  local copies, waits for them, and re-layouts  10.1 us (4%)
    ppermute x13, waiting for transfers between devices, seq_swap(): lax.ppermute(array, 'seq', [(i, i ^ bit) for i in range(lax.axis_size('se...  91.7 us
    pallas_call x2, Pallas kernels, attention(): pl.pallas_call(kernel, in_specs=[pl.BlockSpec(memory_space=pltpu.VMEM)] *...  26.1 us
    pallas_call x2, Pallas kernels, weight_products(): pl.pallas_call(kernel, grid_spec=pltpu.PrefetchScalarGridSpec(num_scalar_...  24.9 us
    ppermute x9, waiting for transfers between devices, dp_move(): lax.ppermute(array, 'dp', [(peer(p, j, e), p) for p in range(dp_count)])  23.4 us
    ppermute x13, starting transfers between devices, seq_swap(): lax.ppermute(array, 'seq', [(i, i ^ bit) for i in range(lax.axis_size('se...  18.2 us
    all_to_all x2, starting transfers between devices, local(): backs.append(lax.all_to_all(back, 'seq', 0, 0, tiled=True))  9.16 us
    pallas_call x1, Pallas kernels, add_products(): pl.pallas_call(kernel, grid_spec=pltpu.PrefetchScalarGridSpec(num_scalar_...  7.9 us
    unnamed x36, local copies, waits for them, and re-layouts  7.46 us
  transfers between devices with their start and end apart: 26, of which 12 were waited for; matrix products, arithmetic and copies ran while one was open for 3% of the time, Pallas kernels for 28%

profile of v5, /device:TPU:0, one launch (start us, length us, event | category | flops | bytes accessed | tf_op | source)
XLA Modules:
  0.0 247.8 jit_solution(5185171072140771046)
XLA Ops:
  0.6 2.8 %pack_rows.2.refs_1_ = bf16[8,4,128,256]{3,2,1,0:T(8,128)(2,1)} custom-call(bf16[128,4096]{1,0:T(8,128)(2,1)} %bitcast.23, bf16[128,4096]{1,0:T(8,128)(2,1)} %bitcast.25, bf16[128,4096]{1,0:T(8,128)(2,1)} %bitcast.27, bf16[128,4096]{1,0:T(8,128)(2,1)} %bitcast.29), custom_call_target="tpu_custom_call" | custom-call | tf_op jit(solution)/shard_map/pack_rows/pallas_call | solution.py:49
  3.4 7.3 %all-to-all-start.1 = ((bf16[8,4,128,256]{3,2,1,0:T(8,128)(2,1)}), bf16[8,4,128,256]{3,2,1,0:T(8,128)(2,1)}, u32[]{:S(2)}, u32[]{:S(2)}) async-start(bf16[8,4,128,256]{3,2,1,0:T(8,128)(2,1)} %pack_rows.2.refs_1_), calls=%async_computation.1 | async-start | bytes 4194304 | tf_op jit(solution)/shard_map/all_to_all | solution.py:335
  10.7 2.2 turn_layer_input.1.refs_4_
  12.9 2.0 constant_dynamic-slice_fusion
  14.9 1.5 collective-permute-start.1
  16.8 7.2 %collective-permute-done.1.refs_2_ = bf16[1024,128]{1,0:T(8,128)(2,1)S(1)} collective-permute-done((bf16[1024,128]{1,0:T(8,128)(2,1)S(1)}, bf16[1024,128]{1,0:T(8,128)(2,1)S(1)}, u32[]{:S(2)}, u32[]{:S(2)}) %collective-permute-start.1) | collective-permute-done | bytes 262176 | tf_op jit(solution)/shard_map/ppermute | solution.py:326
  24.0 4.8 %collective-permute-done.2.refs_3_ = bf16[1024,128]{1,0:T(8,128)(2,1)S(1)} collective-permute-done((bf16[1024,128]{1,0:T(8,128)(2,1)S(1)}, bf16[1024,128]{1,0:T(8,128)(2,1)S(1)}, u32[]{:S(2)}, u32[]{:S(2)}) %collective-permute-start.2) | collective-permute-done | bytes 262176 | tf_op jit(solution)/shard_map/ppermute | solution.py:326
  28.8 0.7 copy-done.14
  29.6 2.6 %join_slabs.1 = (bf16[4,1024,128]{2,1,0:T(8,128)(2,1)}, bf16[3,1024,128]{2,1,0:T(8,128)(2,1)}, bf16[1,1024,128]{2,1,0:T(8,128)(2,1)}) custom-call(bf16[1024,128]{1,0:T(8,128)(2,1)} %get-tuple-element.25.refs_0_, bf16[1024,128]{1,0:T(8,128)(2,1)} %copy-done.12, bf16[1024,128]{1,0:T(8,128)(2,1)} %copy-done.13, bf16[1024,128]{1,0:T(8,128)(2,1)} %copy-done.14), custom_call_target="tpu_custom_call" | custom-call | tf_op jit(solution)/shard_map/join_slabs/pallas_call | solution.py:112
  32.2 2.1 collective-permute-start.3
  34.3 1.5 collective-permute-start.7
  35.7 2.4 collective-permute-start.5
  38.1 33.0 %collective-permute-done.3.refs_1_.refs_2_ = bf16[3,1024,128]{2,1,0:T(8,128)(2,1)S(1)} collective-permute-done((bf16[3,1024,128]{2,1,0:T(8,128)(2,1)}, bf16[3,1024,128]{2,1,0:T(8,128)(2,1)S(1)}, u32[]{:S(2)}, u32[]{:S(2)}) %collective-permute-start.3) | collective-permute-done | bytes 786464 | tf_op jit(solution)/shard_map/ppermute | solution.py:306
  71.1 1.2 collective-permute-start.8
  72.3 1.9 collective-permute-start.6
  74.2 12.1 %collective-permute-done.4.refs_2_.refs_3_ = bf16[1,1024,128]{2,1,0:T(8,128)(2,1)S(1)} collective-permute-done((bf16[1,1024,128]{2,1,0:T(8,128)(2,1)}, bf16[1,1024,128]{2,1,0:T(8,128)(2,1)S(1)}, u32[]{:S(2)}, u32[]{:S(2)}) %collective-permute-start.4) | collective-permute-done | bytes 262176 | tf_op jit(solution)/shard_map/ppermute | solution.py:306
  86.3 1.5 collective-permute-start.9
  87.9 2.9 %pack_rows.3.refs_0_ = bf16[8,4,128,256]{3,2,1,0:T(8,128)(2,1)} custom-call(bf16[128,4096]{1,0:T(8,128)(2,1)} %bitcast.24, bf16[128,4096]{1,0:T(8,128)(2,1)} %bitcast.26, bf16[128,4096]{1,0:T(8,128)(2,1)} %bitcast.28, bf16[128,4096]{1,0:T(8,128)(2,1)} %bitcast.30, bf16[4096,128]{1,0:T(8,128)(2,1)} %turn_layer_input.1.refs_4_), custom_call_target="tpu_custom_call" | custom-call | tf_op jit(solution)/shard_map/pack_rows/pallas_call | solution.py:49
  90.8 13.1 %collective-permute-done.6.refs_4_.refs_5_ = bf16[1,1024,128]{2,1,0:T(8,128)(2,1)S(1)} collective-permute-done((bf16[1,1024,128]{2,1,0:T(8,128)(2,1)}, bf16[1,1024,128]{2,1,0:T(8,128)(2,1)S(1)}, u32[]{:S(2)}, u32[]{:S(2)}) %collective-permute-start.6) | collective-permute-done | bytes 262176 | tf_op jit(solution)/shard_map/ppermute | solution.py:306
  104.0 0.7 copy-done.8
  105.3 4.5 %all-to-all-start = ((bf16[8,4,128,256]{3,2,1,0:T(8,128)(2,1)}), bf16[8,4,128,256]{3,2,1,0:T(8,128)(2,1)}, u32[]{:S(2)}, u32[]{:S(2)}) async-start(bf16[8,4,128,256]{3,2,1,0:T(8,128)(2,1)} %hold.3.refs_2_), calls=%async_computation | async-start | bytes 4194304 | tf_op jit(solution)/shard_map/all_to_all | solution.py:368
  110.1 13.7 %attention_backward.3.refs_12_.refs_6_ = bf16[8,3,128,256]{3,2,1,0:T(8,128)(2,1)} custom-call(bf16[8,4,128,256]{3,2,1,0:T(8,128)(2,1)} %all-to-all-done.1.refs_0_, f32[4,8,256]{2,1,0:T(8,128)S(1)} %broadcast_bitcast_fusion.refs_1_, bf16[8,4,128,256]{3,2,1,0:T(8,128)(2,1)S(1)} %copy-done), custom_call_target="tpu_custom_call" | custom-call | tf_op jit(solution)/shard_map/attention_backward/pallas_call | solution.py:203
  123.8 1.5 collective-permute-start.16
  125.3 1.9 collective-permute-start.11
  127.2 1.5 collective-permute-start.13
  129.2 2.7 %copy.21.refs_0_ = bf16[8,3,128,256]{3,2,1,0:T(8,128)(2,1)} copy(bf16[8,3,128,256]{3,2,1,0:T(8,128)(2,1)} %attention_backward.3.refs_12_.refs_6_) | data formatting | bytes 3145728
  131.9 28.0 %collective-permute-done.14.refs_11_.refs_3_ = bf16[1,1024,128]{2,1,0:T(8,128)(2,1)S(1)} collective-permute-done((bf16[1,1024,128]{2,1,0:T(8,128)(2,1)S(1)}, bf16[1,1024,128]{2,1,0:T(8,128)(2,1)S(1)}, u32[]{:S(2)}, u32[]{:S(2)}) %collective-permute-start.14) | collective-permute-done | bytes 262176 | tf_op jit(solution)/shard_map/ppermute | solution.py:306
  159.9 2.5 collective-permute-done.11.refs_6_.refs_1_
  162.3 0.9 copy-done.6
  163.2 4.7 %all-to-all-start.3 = ((bf16[8,3,128,256]{3,2,1,0:T(8,128)(2,1)}), bf16[8,3,128,256]{3,2,1,0:T(8,128)(2,1)}, u32[]{:S(2)}, u32[]{:S(2)}) async-start(bf16[8,3,128,256]{3,2,1,0:T(8,128)(2,1)} %hold.5), calls=%async_computation.3 | async-start | bytes 3145728 | tf_op jit(solution)/shard_map/all_to_all | solution.py:380
  168.4 2.0 collective-permute-start.12
  170.5 12.4 %attention_backward.2.refs_12_.refs_7_ = bf16[8,3,128,256]{3,2,1,0:T(8,128)(2,1)S(1)} custom-call(bf16[8,4,128,256]{3,2,1,0:T(8,128)(2,1)} %all-to-all-done.refs_0_, f32[4,8,256]{2,1,0:T(8,128)S(1)} %broadcast_bitcast_fusion.refs_1_), custom_call_target="tpu_custom_call" | custom-call | tf_op jit(solution)/shard_map/attention_backward/pallas_call | solution.py:203
  182.9 1.6 collective-permute-start.19
  184.5 1.5 collective-permute-start.10
  185.9 0.6 stack.35.refs_0_
  186.6 1.1 copy.20.refs_0_
  187.7 12.5 %weight_products.2.refs_3_.refs_16_ = f32[3,1024,512]{2,1,0:T(8,128)} custom-call(s32[8]{0:T(128)} %stack.35.refs_0_, bf16[4,1024,128]{2,1,0:T(8,128)(2,1)} %get-tuple-element.15.refs_1_, bf16[3,1024,128]{2,1,0:T(8,128)(2,1)} %copy-done.3, bf16[1,1024,128]{2,1,0:T(8,128)(2,1)} %copy-done.7, bf16[3,1024,128]{2,1,0:T(8,128)(2,1)} %copy-done.4, ...), custom_call_target="tpu_custom_call" | custom-call | tf_op jit(solution)/shard_map/weight_products/pallas_call | solution.py:247
  200.2 3.0 %collective-permute-done.12.refs_2_ = bf16[3,1024,128]{2,1,0:T(8,128)(2,1)} collective-permute-done((bf16[3,1024,128]{2,1,0:T(8,128)(2,1)}, bf16[3,1024,128]{2,1,0:T(8,128)(2,1)}, u32[]{:S(2)}, u32[]{:S(2)}) %collective-permute-start.12) | collective-permute-done | bytes 786464 | tf_op jit(solution)/shard_map/ppermute | solution.py:306
  203.2 1.0 all-to-all-done.3.refs_0_
  204.2 4.5 %all-to-all-start.2 = ((bf16[8,3,128,256]{3,2,1,0:T(8,128)(2,1)}), bf16[8,3,128,256]{3,2,1,0:T(8,128)(2,1)}, u32[]{:S(2)}, u32[]{:S(2)}) async-start(bf16[8,3,128,256]{3,2,1,0:T(8,128)(2,1)} %hold.4), calls=%async_computation.2 | async-start | bytes 3145728 | tf_op jit(solution)/shard_map/all_to_all | solution.py:380
  208.8 10.3 %collective-permute-done.19.refs_14_.refs_11_ = bf16[8,3,128,256]{3,2,1,0:T(8,128)(2,1)} collective-permute-done((bf16[8,3,128,256]{3,2,1,0:T(8,128)(2,1)S(1)}, bf16[8,3,128,256]{3,2,1,0:T(8,128)(2,1)}, u32[]{:S(2)}, u32[]{:S(2)}) %collective-permute-start.19) | collective-permute-done | bytes 1572896 | tf_op jit(solution)/shard_map/ppermute | solution.py:326
  219.4 2.5 unpack_rows.2
  221.9 1.0 collective-permute-done.20.refs_15_.refs_5_.refs_13_
  222.9 12.5 %weight_products.3.refs_14_ = f32[3,1024,512]{2,1,0:T(8,128)} custom-call(s32[8]{0:T(128)} %stack.35.refs_0_, bf16[4,1024,128]{2,1,0:T(8,128)(2,1)} %get-tuple-element.15.refs_1_, bf16[3,1024,128]{2,1,0:T(8,128)(2,1)} %copy-done.3, bf16[1,1024,128]{2,1,0:T(8,128)(2,1)} %copy-done.7, ...), custom_call_target="tpu_custom_call", output_to_operand_aliasing={{}: (16, {})} | custom-call | tf_op jit(solution)/shard_map/weight_products/pallas_call | solution.py:247
  235.3 0.7 copy-done.11
  236.0 7.9 %add_products.1.refs_4_ = f32[3,1024,512]{2,1,0:T(8,128)} custom-call(s32[8]{0:T(128)} %stack.35.refs_0_, bf16[1,1024,128]{2,1,0:T(8,128)(2,1)} %collective-permute-done.10.refs_1_, bf16[3,1024,128]{2,1,0:T(8,128)(2,1)} %collective-permute-done.12.refs_2_, bf16[1,1024,128]{2,1,0:T(8,128)(2,1)} %copy-done.11, ...), custom_call_target="tpu_custom_call", output_to_operand_aliasing={{}: (14, {})} | custom-call | tf_op jit(solution)/shard_map/add_products/pallas_call | solution.py:287
  243.9 1.2 all-to-all-done.2.refs_0_
  245.1 2.5 unpack_rows.3
  (60 shorter events, 2.7 us)
Async XLA Ops:
  3.4 101.8 %all-to-all-start.1 = ((bf16[8,4,128,256]{3,2,1,0:T(8,128)(2,1)}), bf16[8,4,128,256]{3,2,1,0:T(8,128)(2,1)}, u32[]{:S(2)}, u32[]{:S(2)}) async-start(bf16[8,4,128,256]{3,2,1,0:T(8,128)(2,1)} %pack_rows.2.refs_1_), calls=%async_computation.1 | async-start | bytes 4194304 | tf_op jit(solution)/shard_map/all_to_all | solution.py:335
  14.9 1.9 collective-permute-start
  14.9 9.1 %collective-permute-start.1 = (bf16[1024,128]{1,0:T(8,128)(2,1)S(1)}, bf16[1024,128]{1,0:T(8,128)(2,1)S(1)}, u32[]{:S(2)}, u32[]{:S(2)}) collective-permute-start(bf16[1024,128]{1,0:T(8,128)(2,1)S(1)} %get-tuple-element.23), channel_id=1, source_target_pairs={{2,0},{3,1},{0,2},{1,3},{6,4},{7,5},{4,6},{5,7},{10,8},{11,9},{8,1... | collective-permute-start | bytes 786440 | tf_op jit(solution)/shard_map/ppermute | solution.py:326
  16.4 12.4 %collective-permute-start.2 = (bf16[1024,128]{1,0:T(8,128)(2,1)S(1)}, bf16[1024,128]{1,0:T(8,128)(2,1)S(1)}, u32[]{:S(2)}, u32[]{:S(2)}) collective-permute-start(bf16[1024,128]{1,0:T(8,128)(2,1)S(1)} %get-tuple-element.22), channel_id=1, source_target_pairs={{3,0},{2,1},{1,2},{0,3},{7,4},{6,5},{5,6},{4,7},{11,8},{10,9},{9,1... | collective-permute-start | bytes 786440 | tf_op jit(solution)/shard_map/ppermute | solution.py:326
  16.8 12.1 %copy-start.12 = (bf16[1024,128]{1,0:T(8,128)(2,1)}, bf16[1024,128]{1,0:T(8,128)(2,1)S(1)}, u32[]{:S(2)}) copy-start(bf16[1024,128]{1,0:T(8,128)(2,1)S(1)} %collective-permute-done.refs_1_) | copy-start | bytes 786436
  24.0 4.9 %copy-start.13 = (bf16[1024,128]{1,0:T(8,128)(2,1)}, bf16[1024,128]{1,0:T(8,128)(2,1)S(1)}, u32[]{:S(2)}) copy-start(bf16[1024,128]{1,0:T(8,128)(2,1)S(1)} %collective-permute-done.1.refs_2_) | copy-start | bytes 786436
  28.8 0.7 copy-start.14
  32.2 38.9 %collective-permute-start.3 = (bf16[3,1024,128]{2,1,0:T(8,128)(2,1)}, bf16[3,1024,128]{2,1,0:T(8,128)(2,1)S(1)}, u32[]{:S(2)}, u32[]{:S(2)}) collective-permute-start(bf16[3,1024,128]{2,1,0:T(8,128)(2,1)} %get-tuple-element.13), channel_id=1, source_target_pairs={{0,8},{4,12},{8,0},{12,4},{16,24},{20,28},{24,16},{28,20},{1,9},{5... | collective-permute-start | bytes 2359304 | tf_op jit(solution)/shard_map/ppermute | solution.py:306
  34.3 69.7 %collective-permute-start.7 = (bf16[4,1024,128]{2,1,0:T(8,128)(2,1)}, bf16[4,1024,128]{2,1,0:T(8,128)(2,1)S(1)}, u32[]{:S(2)}, u32[]{:S(2)}) collective-permute-start(bf16[4,1024,128]{2,1,0:T(8,128)(2,1)} %get-tuple-element.15.refs_1_), channel_id=1, source_target_pairs={{0,4},{4,0},{8,12},{12,8},{16,20},{20,16},{24,28},{28,24},{1,5},{5... | collective-permute-start | bytes 3145736 | tf_op jit(solution)/shard_map/ppermute | solution.py:306
  35.7 68.2 %collective-permute-start.5 = (bf16[3,1024,128]{2,1,0:T(8,128)(2,1)}, bf16[3,1024,128]{2,1,0:T(8,128)(2,1)S(1)}, u32[]{:S(2)}, u32[]{:S(2)}) collective-permute-start(bf16[3,1024,128]{2,1,0:T(8,128)(2,1)} %get-tuple-element.13), channel_id=1, source_target_pairs={{0,16},{4,20},{8,24},{12,28},{16,0},{20,4},{24,8},{28,12},{1,17},{... | collective-permute-start | bytes 2359304 | tf_op jit(solution)/shard_map/ppermute | solution.py:306
  71.1 19.7 %copy-start.3 = (bf16[3,1024,128]{2,1,0:T(8,128)(2,1)}, bf16[3,1024,128]{2,1,0:T(8,128)(2,1)S(1)}, u32[]{:S(2)}) copy-start(bf16[3,1024,128]{2,1,0:T(8,128)(2,1)S(1)} %collective-permute-done.3.refs_1_.refs_2_) | copy-start | bytes 2359300
  71.1 32.9 %collective-permute-start.8 = (bf16[3,1024,128]{2,1,0:T(8,128)(2,1)S(1)}, bf16[3,1024,128]{2,1,0:T(8,128)(2,1)}, u32[]{:S(2)}, u32[]{:S(2)}) collective-permute-start(bf16[3,1024,128]{2,1,0:T(8,128)(2,1)S(1)} %collective-permute-done.3.refs_1_.refs_2_), channel_id=1, source_target_pairs={{0,4},{4,0},{8,12},{12,8},{16,20},{20,16},{24,28},{28,24},{1,5},{5... | collective-permute-start | bytes 2359304 | tf_op jit(solution)/shard_map/ppermute | solution.py:306
  72.3 14.0 %collective-permute-start.4 = (bf16[1,1024,128]{2,1,0:T(8,128)(2,1)}, bf16[1,1024,128]{2,1,0:T(8,128)(2,1)S(1)}, u32[]{:S(2)}, u32[]{:S(2)}) collective-permute-start(bf16[1,1024,128]{2,1,0:T(8,128)(2,1)} %get-tuple-element.14), channel_id=1, source_target_pairs={{0,8},{4,12},{8,0},{12,4},{16,24},{20,28},{24,16},{28,20},{1,9},{5... | collective-permute-start | bytes 786440 | tf_op jit(solution)/shard_map/ppermute | solution.py:306
  72.3 31.6 %collective-permute-start.6 = (bf16[1,1024,128]{2,1,0:T(8,128)(2,1)}, bf16[1,1024,128]{2,1,0:T(8,128)(2,1)S(1)}, u32[]{:S(2)}, u32[]{:S(2)}) collective-permute-start(bf16[1,1024,128]{2,1,0:T(8,128)(2,1)} %get-tuple-element.14), channel_id=1, source_target_pairs={{0,16},{4,20},{8,24},{12,28},{16,0},{20,4},{24,8},{28,12},{1,17},{... | collective-permute-start | bytes 786440 | tf_op jit(solution)/shard_map/ppermute | solution.py:306
  86.3 4.5 %copy-start.7 = (bf16[1,1024,128]{2,1,0:T(8,128)(2,1)}, bf16[1,1024,128]{2,1,0:T(8,128)(2,1)S(1)}, u32[]{:S(2)}) copy-start(bf16[1,1024,128]{2,1,0:T(8,128)(2,1)S(1)} %collective-permute-done.4.refs_2_.refs_3_) | copy-start | bytes 786436
  86.3 17.6 %collective-permute-start.9 = (bf16[1,1024,128]{2,1,0:T(8,128)(2,1)S(1)}, bf16[1,1024,128]{2,1,0:T(8,128)(2,1)}, u32[]{:S(2)}, u32[]{:S(2)}) collective-permute-start(bf16[1,1024,128]{2,1,0:T(8,128)(2,1)S(1)} %collective-permute-done.4.refs_2_.refs_3_), channel_id=1, source_target_pairs={{0,4},{4,0},{8,12},{12,8},{16,20},{20,16},{24,28},{28,24},{1,5},{5... | collective-permute-start | bytes 786440 | tf_op jit(solution)/shard_map/ppermute | solution.py:306
  103.9 0.7 copy-start.8
  103.9 1.0 copy-start.4
  103.9 1.3 copy-start.2
  105.2 4.5 %copy-start.16 = (s32[1,8]{1,0:T(1,128)S(1)}, s32[1,8]{1,0:T(1,128)}, u32[]{:S(2)}) copy-start(s32[1,8]{1,0:T(1,128)} %param.13) | copy-start | bytes 100
  105.2 4.6 %copy-start.15 = (s32[1,8,8]{2,1,0:T(8,128)S(1)}, s32[1,8,8]{2,1,0:T(8,128)}, u32[]{:S(2)}) copy-start(s32[1,8,8]{2,1,0:T(8,128)} %param.12) | copy-start | bytes 772
  105.2 4.8 %copy-start = (bf16[8,4,128,256]{3,2,1,0:T(8,128)(2,1)S(1)}, bf16[8,4,128,256]{3,2,1,0:T(8,128)(2,1)}, u32[]{:S(2)}) copy-start(bf16[8,4,128,256]{3,2,1,0:T(8,128)(2,1)} %hold.3.refs_2_) | copy-start | bytes 6291460
  105.3 58.0 %all-to-all-start = ((bf16[8,4,128,256]{3,2,1,0:T(8,128)(2,1)}), bf16[8,4,128,256]{3,2,1,0:T(8,128)(2,1)}, u32[]{:S(2)}, u32[]{:S(2)}) async-start(bf16[8,4,128,256]{3,2,1,0:T(8,128)(2,1)} %hold.3.refs_2_), calls=%async_computation | async-start | bytes 4194304 | tf_op jit(solution)/shard_map/all_to_all | solution.py:368
  110.1 15.2 %copy-start.5 = (bf16[3,1024,128]{2,1,0:T(8,128)(2,1)S(1)}, bf16[3,1024,128]{2,1,0:T(8,128)(2,1)}, u32[]{:S(2)}) copy-start(bf16[3,1024,128]{2,1,0:T(8,128)(2,1)} %copy-done.4) | copy-start | bytes 2359300
  110.1 18.6 %copy-start.9 = (bf16[1,1024,128]{2,1,0:T(8,128)(2,1)S(1)}, bf16[1,1024,128]{2,1,0:T(8,128)(2,1)}, u32[]{:S(2)}) copy-start(bf16[1,1024,128]{2,1,0:T(8,128)(2,1)} %copy-done.8) | copy-start | bytes 786436
  123.8 38.6 %collective-permute-start.16 = (bf16[8,3,128,256]{3,2,1,0:T(8,128)(2,1)}, bf16[8,3,128,256]{3,2,1,0:T(8,128)(2,1)}, u32[]{:S(2)}, u32[]{:S(2)}) collective-permute-start(bf16[8,3,128,256]{3,2,1,0:T(8,128)(2,1)} %attention_backward.3.refs_12_.refs_6_), channel_id=1, source_target_pairs={{2,0},{3,1},{0,2},{1,3},{6,4},{7,5},{4,6},{5,7},{10,8},{11,9},{8,1... | collective-permute-start | bytes 4718600 | tf_op jit(solution)/shard_map/ppermute | solution.py:326
  125.3 37.0 %collective-permute-start.11 = (bf16[3,1024,128]{2,1,0:T(8,128)(2,1)S(1)}, bf16[3,1024,128]{2,1,0:T(8,128)(2,1)}, u32[]{:S(2)}, u32[]{:S(2)}) collective-permute-start(bf16[3,1024,128]{2,1,0:T(8,128)(2,1)S(1)} %copy-done.5), channel_id=1, source_target_pairs={{0,8},{4,12},{8,0},{12,4},{16,24},{20,28},{24,16},{28,20},{1,9},{5... | collective-permute-start | bytes 2359304 | tf_op jit(solution)/shard_map/ppermute | solution.py:306
  127.2 35.2 %collective-permute-start.13 = (bf16[3,1024,128]{2,1,0:T(8,128)(2,1)S(1)}, bf16[3,1024,128]{2,1,0:T(8,128)(2,1)S(1)}, u32[]{:S(2)}, u32[]{:S(2)}) collective-permute-start(bf16[3,1024,128]{2,1,0:T(8,128)(2,1)S(1)} %copy-done.5), channel_id=1, source_target_pairs={{0,4},{4,0},{8,12},{12,8},{16,20},{20,16},{24,28},{28,24},{1,5},{5... | collective-permute-start | bytes 2359304 | tf_op jit(solution)/shard_map/ppermute | solution.py:306
  128.6 31.2 %collective-permute-start.14 = (bf16[1,1024,128]{2,1,0:T(8,128)(2,1)S(1)}, bf16[1,1024,128]{2,1,0:T(8,128)(2,1)S(1)}, u32[]{:S(2)}, u32[]{:S(2)}) collective-permute-start(bf16[1,1024,128]{2,1,0:T(8,128)(2,1)S(1)} %copy-done.9), channel_id=1, source_target_pairs={{0,4},{4,0},{8,12},{12,8},{16,20},{20,16},{24,28},{28,24},{1,5},{5... | collective-permute-start | bytes 786440 | tf_op jit(solution)/shard_map/ppermute | solution.py:306
  159.9 2.5 %copy-start.10 = (bf16[1,1024,128]{2,1,0:T(8,128)(2,1)}, bf16[1,1024,128]{2,1,0:T(8,128)(2,1)S(1)}, u32[]{:S(2)}) copy-start(bf16[1,1024,128]{2,1,0:T(8,128)(2,1)S(1)} %collective-permute-done.14.refs_11_.refs_3_) | copy-start | bytes 786436
  162.3 0.9 copy-start.6
  163.2 41.0 %all-to-all-start.3 = ((bf16[8,3,128,256]{3,2,1,0:T(8,128)(2,1)}), bf16[8,3,128,256]{3,2,1,0:T(8,128)(2,1)}, u32[]{:S(2)}, u32[]{:S(2)}) async-start(bf16[8,3,128,256]{3,2,1,0:T(8,128)(2,1)} %hold.5), calls=%async_computation.3 | async-start | bytes 3145728 | tf_op jit(solution)/shard_map/all_to_all | solution.py:380
  167.9 19.8 %collective-permute-start.15 = (bf16[8,3,128,256]{3,2,1,0:T(8,128)(2,1)}, bf16[8,3,128,256]{3,2,1,0:T(8,128)(2,1)}, u32[]{:S(2)}, u32[]{:S(2)}) collective-permute-start(bf16[8,3,128,256]{3,2,1,0:T(8,128)(2,1)} %attention_backward.3.refs_12_.refs_6_), channel_id=1, source_target_pairs={{1,0},{0,1},{3,2},{2,3},{5,4},{4,5},{7,6},{6,7},{9,8},{8,9},{11,10... | collective-permute-start | bytes 4718600 | tf_op jit(solution)/shard_map/ppermute | solution.py:326
  167.9 19.8 %collective-permute-start.17 = (bf16[8,3,128,256]{3,2,1,0:T(8,128)(2,1)}, bf16[8,3,128,256]{3,2,1,0:T(8,128)(2,1)}, u32[]{:S(2)}, u32[]{:S(2)}) collective-permute-start(bf16[8,3,128,256]{3,2,1,0:T(8,128)(2,1)} %collective-permute-done.16.refs_14_.refs_4_.refs_10_), channel_id=1, source_target_pairs={{1,0},{0,1},{3,2},{2,3},{5,4},{4,5},{7,6},{6,7},{9,8},{8,9},{11,10... | collective-permute-start | bytes 4718600 | tf_op jit(solution)/shard_map/ppermute | solution.py:326
  168.4 34.8 %collective-permute-start.12 = (bf16[3,1024,128]{2,1,0:T(8,128)(2,1)}, bf16[3,1024,128]{2,1,0:T(8,128)(2,1)}, u32[]{:S(2)}, u32[]{:S(2)}) collective-permute-start(bf16[3,1024,128]{2,1,0:T(8,128)(2,1)} %collective-permute-done.11.refs_6_.refs_1_), channel_id=1, source_target_pairs={{0,4},{4,0},{8,12},{12,8},{16,20},{20,16},{24,28},{28,24},{1,5},{5... | collective-permute-start | bytes 2359304 | tf_op jit(solution)/shard_map/ppermute | solution.py:306
  182.9 25.8 %copy-start.1 = (bf16[8,3,128,256]{3,2,1,0:T(8,128)(2,1)}, bf16[8,3,128,256]{3,2,1,0:T(8,128)(2,1)S(1)}, u32[]{:S(2)}) copy-start(bf16[8,3,128,256]{3,2,1,0:T(8,128)(2,1)S(1)} %attention_backward.2.refs_12_.refs_7_) | copy-start | bytes 4718596
  182.9 36.2 %collective-permute-start.19 = (bf16[8,3,128,256]{3,2,1,0:T(8,128)(2,1)S(1)}, bf16[8,3,128,256]{3,2,1,0:T(8,128)(2,1)}, u32[]{:S(2)}, u32[]{:S(2)}) collective-permute-start(bf16[8,3,128,256]{3,2,1,0:T(8,128)(2,1)S(1)} %attention_backward.2.refs_12_.refs_7_), channel_id=1, source_target_pairs={{2,0},{3,1},{0,2},{1,3},{6,4},{7,5},{4,6},{5,7},{10,8},{11,9},{8,1... | collective-permute-start | bytes 4718600 | tf_op jit(solution)/shard_map/ppermute | solution.py:326
  184.5 15.7 %collective-permute-start.10 = (bf16[1,1024,128]{2,1,0:T(8,128)(2,1)S(1)}, bf16[1,1024,128]{2,1,0:T(8,128)(2,1)}, u32[]{:S(2)}, u32[]{:S(2)}) collective-permute-start(bf16[1,1024,128]{2,1,0:T(8,128)(2,1)S(1)} %copy-done.9), channel_id=1, source_target_pairs={{0,8},{4,12},{8,0},{12,4},{16,24},{20,28},{24,16},{28,20},{1,9},{5... | collective-permute-start | bytes 786440 | tf_op jit(solution)/shard_map/ppermute | solution.py:306
  204.2 40.9 %all-to-all-start.2 = ((bf16[8,3,128,256]{3,2,1,0:T(8,128)(2,1)}), bf16[8,3,128,256]{3,2,1,0:T(8,128)(2,1)}, u32[]{:S(2)}, u32[]{:S(2)}) async-start(bf16[8,3,128,256]{3,2,1,0:T(8,128)(2,1)} %hold.4), calls=%async_computation.2 | async-start | bytes 3145728 | tf_op jit(solution)/shard_map/all_to_all | solution.py:380
  208.7 13.1 %collective-permute-start.21 = (bf16[8,3,128,256]{3,2,1,0:T(8,128)(2,1)S(1)}, bf16[8,3,128,256]{3,2,1,0:T(8,128)(2,1)}, u32[]{:S(2)}, u32[]{:S(2)}) collective-permute-start(bf16[8,3,128,256]{3,2,1,0:T(8,128)(2,1)S(1)} %attention_backward.2.refs_12_.refs_7_), channel_id=1, source_target_pairs={{1,0},{0,1},{3,2},{2,3},{5,4},{4,5},{7,6},{6,7},{9,8},{8,9},{11,10... | collective-permute-start | bytes 4718600 | tf_op jit(solution)/shard_map/ppermute | solution.py:326
  219.1 3.8 %collective-permute-start.20 = (bf16[8,3,128,256]{3,2,1,0:T(8,128)(2,1)}, bf16[8,3,128,256]{3,2,1,0:T(8,128)(2,1)}, u32[]{:S(2)}, u32[]{:S(2)}) collective-permute-start(bf16[8,3,128,256]{3,2,1,0:T(8,128)(2,1)} %collective-permute-done.19.refs_14_.refs_11_), channel_id=1, source_target_pairs={{1,0},{0,1},{3,2},{2,3},{5,4},{4,5},{7,6},{6,7},{9,8},{8,9},{11,10... | collective-permute-start | bytes 4718600 | tf_op jit(solution)/shard_map/ppermute | solution.py:326
  219.1 16.2 %collective-permute-start.18 = (bf16[1,1024,128]{2,1,0:T(8,128)(2,1)}, bf16[1,1024,128]{2,1,0:T(8,128)(2,1)S(1)}, u32[]{:S(2)}, u32[]{:S(2)}) collective-permute-start(bf16[1,1024,128]{2,1,0:T(8,128)(2,1)} %collective-permute-done.10.refs_1_), channel_id=1, source_target_pairs={{0,4},{4,0},{8,12},{12,8},{16,20},{20,16},{24,28},{28,24},{1,5},{5... | collective-permute-start | bytes 786440 | tf_op jit(solution)/shard_map/ppermute | solution.py:306
  235.3 0.7 copy-start.11
